TPU v7x, 32 devices: a whole 2x2x4 slice. The times are simulated.
32 devices in a mesh: scene: 2 (over y), tok: 4 (over z), col: 2 (over x), rep: 2 (over core).
Axes of the slice: x: 2, y: 2, z: 4, core: 2. Of those that a mesh axis runs over, the one named last changes fastest.
Arguments:
- tokens: float32 [8192, 512], P(('scene', 'tok'), ('col', 'rep')), parts along dimension 0
- w_qkv: float32 [2, 3, 512, 512], P(None, None, None, ('col', 'rep'))
- w_out: float32 [2, 512, 512], P(None, ('col', 'rep')), may hold values from -0.25 to 0.25
- w_up: float32 [2, 512, 2048], P(None, None, ('col', 'rep')), may hold values from -0.25 to 0.25
- w_down: float32 [2, 2048, 512], P(None, ('col', 'rep')), may hold values from -0.125 to 0.125
- attn_gain: float32 [2, 512], replicated, may hold values from 0.1 to 1.9
- mlp_gain: float32 [2, 512], replicated, may hold values from 0.1 to 1.9
- dest_device: int32 [128], P(('scene', 'tok')), parts along dimension 0, may hold values from 0 to 3, as said below
- dest_slot: int32 [128], P(('scene', 'tok')), parts along dimension 0, may hold values from 0 to 15, as said below
- pillar: int32 [8192], P(('scene', 'tok')), parts along dimension 0, may hold values from -1 to 2047, as said below
- depth_weight: float32 [2, 3, 3, 512], replicated, may hold values from -2 to 2
- point_weight: float32 [2, 512, 1024], replicated, may hold values from -0.25 to 0.25
- raster_gain: float32 [2, 512], replicated, may hold values from 0.1 to 1.9
Outputs:
- raster: float32 [128, 32, 512], P(('scene', 'tok', 'rep'), 'col'), parts along dimension 0
There are 2 independent parts, one for each index of `scene`. A program takes and returns all parts, laid end to end along the dimension named above; an argument that names none is the same for every part. Nothing has to cross between parts.
Inputs may be any that keep to these rules, and one draw needn't show every extreme that they name: `dest_device`: together with dest_slot the blocks fill every index of tok's 16 slots exactly once. At most 5 blocks of one index of tok go to one index, and every index sends exactly 5 blocks to some index. `dest_slot`: the slot of the block among the 16 of its destination. The token at Hilbert position t has a cell in raster rows i * 16 to (i + 1) * 16 - 1 with i = t // 1024, or -1 if it has no pillar; several tokens may share a cell.
All inputs are finite; a program needn't handle non-finite values.
Results may differ from a plain program's by a relative error of at most 0.00012.
Values sent between devices are 32-bit elements; how exact they have to be, the bound alone decides.
No kernel may reach another device: no remote copies, remote signals or barrier semaphores. Data moves between devices by JAX's collectives and lax.ppermute only.
A program may use at most 128 MiB of HBM per device.

v0:
```python
import jax
import jax.numpy as jnp
from jax import lax
from jax.sharding import PartitionSpec as P

PATCH = 1024
TR = 16
TC = 16
HD = 16


MATMUL_PRECISION = lax.Precision.HIGHEST
EPSILON = 1e-05


def padded(block, sides, width):
    for axis, dim in sides:
        count = lax.axis_size(axis)
        forward = [(i, i + 1) for i in range(count - 1)]
        backward = [(target, source) for source, target in forward]
        low = lax.ppermute(
            lax.slice_in_dim(block, block.shape[dim] - width, None, axis=dim), axis, forward
        )
        high = lax.ppermute(lax.slice_in_dim(block, 0, width, axis=dim), axis, backward)
        block = jnp.concatenate([low, block, high], axis=dim)
    return block


def layer_norm(values, gain_row):
    average = jnp.mean(values, axis=-1, keepdims=True)
    centered = values - average
    variance = jnp.mean(centered * centered, axis=-1, keepdims=True)
    return centered * lax.rsqrt(variance + EPSILON) * gain_row


def patch_attention(query_projection, key_proj, value_proj):
    scores = jnp.einsum(
        "qhd,khd->hqk", query_projection, key_proj, precision=MATMUL_PRECISION
    ) * HD ** (-0.5)
    scores = scores - jnp.max(scores, axis=-1, keepdims=True)
    weights = jnp.exp(scores)
    weights = weights / jnp.sum(weights, axis=-1, keepdims=True)
    return jnp.einsum("hqk,khd->qhd", weights, value_proj, precision=MATMUL_PRECISION)


def matmul(left, right):
    return jnp.dot(left, right, precision=MATMUL_PRECISION, preferred_element_type=jnp.float32)


def widen(slice_cols):
    return lax.all_gather(slice_cols, ("col", "rep"), axis=1, tiled=True)


def block_layer(stream, layer_index, w_qkv, w_out, w_up, w_down, attn_gain, mlp_gain):
    row_count = stream.shape[0]
    local_cols = w_qkv.shape[-1]
    heads_here = local_cols // HD
    normed = layer_norm(stream, attn_gain[layer_index])
    shaped = tuple(
        (
            matmul(normed, w_qkv[layer_index, j]).reshape(row_count // PATCH, PATCH, heads_here, HD)
            for j in range(3)
        )
    )

    def attend_patch(operands):
        return patch_attention(operands[0], operands[1], operands[2]).reshape(PATCH, local_cols)

    attended = lax.map(attend_patch, shaped).reshape(row_count, local_cols)
    partial_out = matmul(attended, w_out[layer_index])
    stream = stream + lax.psum(partial_out, ("col", "rep"))
    normed = layer_norm(stream, mlp_gain[layer_index])
    hidden = jax.nn.gelu(matmul(normed, w_up[layer_index]), approximate=False)
    partial_mlp = matmul(hidden, w_down[layer_index])
    summed_share = lax.psum_scatter(partial_mlp, ("col", "rep"), scatter_dimension=1, tiled=True)
    feature_width = summed_share.shape[1]
    own_cols = lax.dynamic_slice_in_dim(
        stream, lax.axis_index(("col", "rep")) * feature_width, feature_width, 1
    )
    return own_cols + summed_share


def send_blocks(block_list, dest_device, dest_slot):
    block_count, rows_per_block, feature_width = block_list.shape
    peers = lax.axis_size("tok")
    capacity = max(2, (block_count + peers - 4) // (peers - 1))
    order_index = jnp.arange(block_count, dtype=jnp.int32)
    earlier = (dest_device[:, None] == dest_device[None, :]) & (
        order_index[None, :] < order_index[:, None]
    )
    prior_count = jnp.sum(earlier.astype(jnp.int32), axis=1)
    slot_key = dest_device * capacity + prior_count
    select_entries = (
        jnp.arange(peers * capacity, dtype=jnp.int32)[:, None] == slot_key[None, :]
    ).astype(jnp.float32)
    outgoing = jnp.einsum(
        "jb,brf->jrf", select_entries, block_list, precision=MATMUL_PRECISION
    ).reshape(peers, capacity, rows_per_block, feature_width)
    slot_codes = matmul(select_entries, (dest_slot + 1).astype(jnp.float32)).reshape(
        peers, capacity
    )
    incoming, arrived = (
        lax.all_to_all(outgoing, "tok", split_axis=0, concat_axis=0, tiled=True),
        lax.all_to_all(slot_codes, "tok", split_axis=0, concat_axis=0, tiled=True),
    )
    wanted = (order_index + 1).astype(jnp.float32)
    placing = (wanted[:, None] == arrived.reshape(-1)[None, :]).astype(jnp.float32)
    flat_incoming = incoming.reshape(peers * capacity, rows_per_block, feature_width)
    return jnp.einsum("sj,jrf->srf", placing, flat_incoming, precision=MATMUL_PRECISION)


def raster_cells(extended, depth_weight, point_weight, gain_row):
    row_count = extended.shape[0] - 2
    col_count = extended.shape[1] - 2
    count_of_channels = extended.shape[2]
    normed = (
        extended
        * lax.rsqrt(jnp.mean(extended * extended, axis=-1, keepdims=True) + EPSILON)
        * gain_row
    )
    mixed_cells = jnp.zeros((row_count, col_count, count_of_channels), jnp.float32)
    for row_tap in range(3):
        for col_tap in range(3):
            mixed_cells = (
                mixed_cells
                + normed[row_tap : row_tap + row_count, col_tap : col_tap + col_count]
                * depth_weight[row_tap, col_tap]
            )
    combined = matmul(mixed_cells.reshape(row_count * col_count, count_of_channels), point_weight)
    combined = combined.reshape(row_count, col_count, 2 * count_of_channels)
    centre = extended[1:-1, 1:-1]
    return centre + combined[..., :count_of_channels] * jax.nn.sigmoid(
        combined[..., count_of_channels:]
    )


def on_device(
    tokens,
    w_qkv,
    w_out,
    w_up,
    w_down,
    attn_gain,
    mlp_gain,
    dest_device,
    dest_slot,
    pillar,
    depth_weight,
    point_weight,
    raster_gain,
):
    stream = widen(tokens)
    first_out = block_layer(stream, 0, w_qkv, w_out, w_up, w_down, attn_gain, mlp_gain)
    feature_width = first_out.shape[1]
    block_count = dest_device.shape[0]
    block_list = first_out.reshape(block_count, first_out.shape[0] // block_count, feature_width)
    reordered_tokens = send_blocks(block_list, dest_device, dest_slot)
    stream = widen(reordered_tokens.reshape(-1, feature_width))
    stream = widen(block_layer(stream, 1, w_qkv, w_out, w_up, w_down, attn_gain, mlp_gain))
    rep_rows = TR // lax.axis_size("rep")
    row_start = lax.axis_index(("tok", "rep")) * rep_rows
    col_start = lax.axis_index("col") * TC
    full_width = TC * lax.axis_size("col")
    cell_rows = row_start + jnp.arange(rep_rows, dtype=jnp.int32)[:, None]
    cell_ids = (
        cell_rows * full_width + col_start + jnp.arange(TC, dtype=jnp.int32)[None, :]
    ).reshape(-1)
    onehot = (pillar[:, None] == cell_ids[None, :]).astype(jnp.float32)
    raster = jnp.einsum("tc,td->cd", onehot, stream, precision=MATMUL_PRECISION).reshape(
        rep_rows, TC, -1
    )
    for layer_index in range(2):
        extended = padded(raster, ((("tok", "rep"), 0), ("col", 1)), 1)
        raster = raster_cells(
            extended, depth_weight[layer_index], point_weight[layer_index], raster_gain[layer_index]
        )
    return raster


def solution(mesh):
    placed = (
        P(("scene", "tok"), ("col", "rep")),
        P(None, None, None, ("col", "rep")),
        P(None, ("col", "rep"), None),
        P(None, None, ("col", "rep")),
        P(None, ("col", "rep"), None),
        P(),
        P(),
        P(("scene", "tok")),
        P(("scene", "tok")),
        P(("scene", "tok")),
        P(),
        P(),
        P(),
    )
    return jax.shard_map(
        on_device,
        mesh=mesh,
        in_specs=placed,
        out_specs=P(("scene", "tok", "rep"), "col", None),
        check_vma=False,
    )
```

profile of v0, /device:TPU:1, one launch (start us, length us, event | category | flops | bytes accessed | tf_op | source)
XLA Modules:
  0.0 511.2 jit_solution(3229951573968464027)
XLA Ops:
  9.9 24.4 %all-gather.4.cloned.1.call-done = f32[1024,512]{1,0:T(8,128)} async-done(((f32[1024,128]{1,0:T(8,128)}), f32[1024,512]{1,0:T(8,128)}) %all-gather.4.cloned.1.call-update) | async-done | bytes 2097168 | tf_op jit(solution)/shard_map/all_gather | solution.py:51
  34.3 2.0 reduce_sum.120
  36.9 2.5 fusion.30
  39.5 2.5 fusion.32
  42.1 28.0 %multiply_reduce_fusion.1 = (f32[8,1024]{1,0:T(8,128)S(1)}, f32[8,1024,1024]{1,2,0:T(8,128)S(1)}) fusion(f32[1024,8,16]{0,2,1:T(8,128)S(1)} %fusion.32, f32[1024,8,16]{0,2,1:T(8,128)S(1)} %fusion.30), kind=kOutput, calls=%fused_computation.7 | convolution fusion | flops 1627381760 | bytes 34635776 | tf_op jit(solution)/shard_map/while/body/eval_jaxpr/qhd,khd->hqk/dot_general | solution.py:37
  70.1 5.9 %fusion.4 = f32[8,1024]{1,0:T(8,128)S(1)} fusion(f32[8,1024,1024]{1,2,0:T(8,128)S(1)} %get-tuple-element.80, f32[8,1024]{1,0:T(8,128)S(1)} %get-tuple-element.79), kind=kLoop, calls=%fused_computation.8 | loop fusion | flops 25157632 | bytes 33619968 | tf_op jit(solution)/shard_map/while/body/eval_jaxpr/reduce_sum | solution.py:42
  76.0 5.2 %copy-done = f32[8,1024,1024]{1,2,0:T(8,128)} copy-done((f32[8,1024,1024]{1,2,0:T(8,128)}, f32[8,1024,1024]{1,2,0:T(8,128)S(1)}, u32[]{:S(2)}) %copy-start) | copy-done | bytes 33554456
  81.1 3.4 fusion.34
  84.5 25.6 %fusion.2 = f32[8,16,1024]{2,1,0:T(8,128)S(1)} fusion(f32[1024,8,16]{0,2,1:T(8,128)} %fusion.34, f32[8,1024,1024]{1,2,0:T(8,128)} %copy-done, f32[8,1024]{1,0:T(8,128)S(1)} %fusion.4, f32[8,1024]{1,0:T(8,128)S(1)} %get-tuple-element.79), kind=kOutput, calls=%fused_computation.4 | convolution fusion | flops 1635778560 | bytes 34668544 | tf_op jit(solution)/shard_map/while/body/eval_jaxpr/hqk,khd->qhd/dot_general | solution.py:43
  110.1 4.1 fusion.299
  114.3 51.0 %all-reduce.3.cloned.1.call-done = f32[1024,512]{1,0:T(8,128)} async-done(((f32[1024,512]{1,0:T(8,128)}), f32[1024,512]{1,0:T(8,128)}) %all-reduce.3.cloned.1.call-update) | async-done | bytes 2097168 | tf_op jit(solution)/shard_map/psum | solution.py:71
  165.3 1.9 fusion.399
  167.6 1.9 copy-done.6
  169.5 3.7 fusion.143
  173.2 9.5 %fusion.14 = f32[1024,512]{1,0:T(8,128)} fusion(f32[1024,512]{1,0:T(8,128)S(1)} %fusion.143, f32[2,512,512]{2,1,0:T(8,128)S(1)} %copy-done.15), kind=kOutput, calls=%fused_computation.20 | convolution fusion | flops 3254779904 | bytes 5242880 | tf_op jit(solution)/shard_map/dot_general | solution.py:47
  184.4 4.3 all-to-all-start
  188.7 25.8 %reduce-scatter.3.cloned.1.call-done = f32[1024,128]{1,0:T(8,128)} async-done(((f32[1024,512]{1,0:T(8,128)}), f32[1024,128]{1,0:T(8,128)}) %reduce-scatter.3.cloned.1.call-update) | async-done | bytes 524304 | tf_op jit(solution)/shard_map/reduce_scatter | solution.py:75
  217.6 4.3 all-to-all-start.1
  223.2 15.5 %all-to-all-done.1 = f32[4,5,64,128]{3,2,1,0:T(8,128)S(1)} async-done(((f32[4,5,64,128]{3,2,1,0:T(8,128)}), f32[4,5,64,128]{3,2,1,0:T(8,128)S(1)}, u32[]{:S(2)}, u32[]{:S(2)}) %all-to-all-start.1) | async-done | bytes 655392 | tf_op jit(solution)/shard_map/all_to_all | solution.py:103
  240.9 21.9 %all-gather.6.cloned.1.call-done = f32[1024,512]{1,0:T(8,128)} async-done(((f32[1024,128]{1,0:T(8,128)}), f32[1024,512]{1,0:T(8,128)}) %all-gather.6.cloned.1.call-update) | async-done | bytes 2097168 | tf_op jit(solution)/shard_map/all_gather | solution.py:51
  262.8 2.0 reduce_sum.125
  265.5 2.5 fusion.24
  268.0 2.5 fusion.26
  270.6 27.9 %multiply_reduce_fusion = (f32[8,1024]{1,0:T(8,128)S(1)}, f32[8,1024,1024]{1,2,0:T(8,128)S(1)}) fusion(f32[1024,8,16]{0,2,1:T(8,128)S(1)} %fusion.26, f32[1024,8,16]{0,2,1:T(8,128)S(1)} %fusion.24), kind=kOutput, calls=%fused_computation.6 | convolution fusion | flops 1627381760 | bytes 34635776 | tf_op jit(solution)/shard_map/while/body/eval_jaxpr/qhd,khd->hqk/dot_general | solution.py:37
  298.5 5.9 %fusion.5 = f32[8,1024]{1,0:T(8,128)S(1)} fusion(f32[8,1024,1024]{1,2,0:T(8,128)S(1)} %get-tuple-element.82, f32[8,1024]{1,0:T(8,128)S(1)} %get-tuple-element.81), kind=kLoop, calls=%fused_computation.9 | loop fusion | flops 25157632 | bytes 33619968 | tf_op jit(solution)/shard_map/while/body/eval_jaxpr/reduce_sum | solution.py:42
  304.4 5.2 %copy-done.1 = f32[8,1024,1024]{1,2,0:T(8,128)} copy-done((f32[8,1024,1024]{1,2,0:T(8,128)}, f32[8,1024,1024]{1,2,0:T(8,128)S(1)}, u32[]{:S(2)}) %copy-start.1) | copy-done | bytes 33554456
  309.6 2.5 fusion.28
  312.1 25.0 %fusion = f32[8,16,1024]{2,1,0:T(8,128)S(1)} fusion(f32[1024,8,16]{0,2,1:T(8,128)S(1)} %fusion.28, f32[8,1024,1024]{1,2,0:T(8,128)} %copy-done.1, f32[8,1024]{1,0:T(8,128)S(1)} %fusion.5, f32[8,1024]{1,0:T(8,128)S(1)} %get-tuple-element.81), kind=kOutput, calls=%fused_computation.2 | convolution fusion | flops 1635778560 | bytes 34668544 | tf_op jit(solution)/shard_map/while/body/eval_jaxpr/hqk,khd->qhd/dot_general | solution.py:43
  337.2 4.1 fusion.297
  341.3 51.0 %all-reduce.5.cloned.1.call-done = f32[1024,512]{1,0:T(8,128)} async-done(((f32[1024,512]{1,0:T(8,128)}), f32[1024,512]{1,0:T(8,128)}) %all-reduce.5.cloned.1.call-update) | async-done | bytes 2097168 | tf_op jit(solution)/shard_map/psum | solution.py:71
  392.3 1.9 fusion.398
  394.7 1.9 copy-done.7
  396.6 3.7 fusion.89
  400.2 9.5 %fusion.18 = f32[1024,512]{1,0:T(8,128)} fusion(f32[1024,512]{1,0:T(8,128)S(1)} %fusion.89, f32[2,512,512]{2,1,0:T(8,128)S(1)} %copy-done.16), kind=kOutput, calls=%fused_computation.23 | convolution fusion | flops 3254779904 | bytes 5242880 | tf_op jit(solution)/shard_map/dot_general | solution.py:47
  409.8 31.7 %reduce-scatter.5.cloned.1.call-done = f32[1024,128]{1,0:T(8,128)} async-done(((f32[1024,512]{1,0:T(8,128)}), f32[1024,128]{1,0:T(8,128)}) %reduce-scatter.5.cloned.1.call-update) | async-done | bytes 524304 | tf_op jit(solution)/shard_map/reduce_scatter | solution.py:75
  441.5 2.1 dynamic-slice_add_fusion
  443.8 23.2 %all-gather.8.cloned.1.call-done = f32[1024,512]{1,0:T(8,128)} async-done(((f32[1024,128]{1,0:T(8,128)}), f32[1024,512]{1,0:T(8,128)}) %all-gather.8.cloned.1.call-update) | async-done | bytes 2097168 | tf_op jit(solution)/shard_map/all_gather | solution.py:51
  467.0 2.8 fusion.253
  469.8 3.3 collective-permute-start
  473.1 1.9 collective-permute-start.1
  475.1 3.3 collective-permute-done.1
  478.4 2.2 collective-permute-start.2
  481.9 3.2 collective-permute-done.3
  485.4 1.5 fusion.22
  487.0 3.3 collective-permute-start.4
  490.3 1.9 collective-permute-start.5
  492.3 3.3 collective-permute-done.5
  498.3 3.2 collective-permute-done.7
  (112 shorter events, 21.3 us)
Async XLA Ops:
  6.5 27.7 %all-gather.4.cloned.1.call-start = ((), (), s32[]{:S(2)}) async-start(), calls=%async_computation.4 | async-start | bytes 2621440 | tf_op jit(solution)/shard_map/all_gather | solution.py:51
  7.3 2.6 copy-start.10
  7.3 158.0 %all-reduce.3.cloned.1.call-start = ((), (), s32[]{:S(2)}) async-start(), calls=%async_computation.5 | async-start | bytes 4194304 | tf_op jit(solution)/shard_map/psum | solution.py:71
  34.3 2.2 copy-start.2
  36.5 3.0 copy-start.8
  70.1 11.1 %copy-start = (f32[8,1024,1024]{1,2,0:T(8,128)}, f32[8,1024,1024]{1,2,0:T(8,128)S(1)}, u32[]{:S(2)}) copy-start(f32[8,1024,1024]{1,2,0:T(8,128)S(1)} %get-tuple-element.80) | copy-start | bytes 100663296
  110.1 4.2 copy-start.11
  114.2 100.2 %reduce-scatter.3.cloned.1.call-start = ((), (), s32[]{:S(2)}) async-start(), calls=%async_computation.6 | async-start | bytes 2621440 | tf_op jit(solution)/shard_map/reduce_scatter | solution.py:75
  167.2 6.0 %copy-start.4 = (f32[1024,512]{1,0:T(8,128)}, f32[1024,512]{1,0:T(8,128)S(1)}, u32[]{:S(2)}) copy-start(f32[1024,512]{1,0:T(8,128)S(1)} %get-tuple-element.31) | copy-start | bytes 6291460
  167.2 2.4 copy-start.6
  169.5 3.7 copy-start.15
  182.7 0.7 copy-start.17
  182.7 0.8 copy-start.18
  184.4 33.2 %all-to-all-start = ((f32[4,1,5]{2,1,0:T(1,128)}), f32[4,1,5]{2,1,0:T(1,128)S(1)}, u32[]{:S(2)}, u32[]{:S(2)}) async-start(f32[4,1,5]{2,1,0:T(1,128)} %bitcast.2), calls=%async_computation | async-start | bytes 4096 | tf_op jit(solution)/shard_map/all_to_all | solution.py:104
  217.6 21.1 %all-to-all-start.1 = ((f32[4,5,64,128]{3,2,1,0:T(8,128)}), f32[4,5,64,128]{3,2,1,0:T(8,128)S(1)}, u32[]{:S(2)}, u32[]{:S(2)}) async-start(f32[4,5,64,128]{3,2,1,0:T(8,128)} %copy.48), calls=%async_computation.2 | async-start | bytes 1310720 | tf_op jit(solution)/shard_map/all_to_all | solution.py:103
  221.9 40.9 %all-gather.6.cloned.1.call-start = ((), (), s32[]{:S(2)}) async-start(), calls=%async_computation.7 | async-start | bytes 2621440 | tf_op jit(solution)/shard_map/all_gather | solution.py:51
  240.5 151.8 %all-reduce.5.cloned.1.call-start = ((), (), s32[]{:S(2)}) async-start(), calls=%async_computation.8 | async-start | bytes 4194304 | tf_op jit(solution)/shard_map/psum | solution.py:71
  262.8 2.2 copy-start.3
  298.5 11.1 %copy-start.1 = (f32[8,1024,1024]{1,2,0:T(8,128)}, f32[8,1024,1024]{1,2,0:T(8,128)S(1)}, u32[]{:S(2)}) copy-start(f32[8,1024,1024]{1,2,0:T(8,128)S(1)} %get-tuple-element.82) | copy-start | bytes 100663296
  341.3 100.2 %reduce-scatter.5.cloned.1.call-start = ((), (), s32[]{:S(2)}) async-start(), calls=%async_computation.9 | async-start | bytes 2621440 | tf_op jit(solution)/shard_map/reduce_scatter | solution.py:75
  394.2 6.0 %copy-start.5 = (f32[1024,512]{1,0:T(8,128)}, f32[1024,512]{1,0:T(8,128)S(1)}, u32[]{:S(2)}) copy-start(f32[1024,512]{1,0:T(8,128)S(1)} %get-tuple-element.24) | copy-start | bytes 6291460
  394.2 2.4 copy-start.7
  396.6 3.7 copy-start.16
  409.8 34.0 %copy-start.9 = (f32[2,3,3,512]{3,0,2,1:T(2,128)S(1)}, f32[2,3,3,512]{3,0,2,1:T(2,128)}, u32[]{:S(2)}) copy-start(f32[2,3,3,512]{3,0,2,1:T(2,128)} %param.23) | copy-start | bytes 110596
  409.8 57.3 %copy-start.13 = (s32[1024]{0:T(1024)S(1)}, s32[1024]{0:T(1024)}, u32[]{:S(2)}) copy-start(s32[1024]{0:T(1024)} %param.22) | copy-start | bytes 12292
  409.8 57.2 %all-gather.8.cloned.1.call-start = ((), (), s32[]{:S(2)}) async-start(), calls=%async_computation.10 | async-start | bytes 2621440 | tf_op jit(solution)/shard_map/all_gather | solution.py:51
  443.5 38.3 %copy-start.12 = (f32[2,512]{1,0:T(2,128)S(1)}, f32[2,512]{1,0:T(2,128)}, u32[]{:S(2)}) copy-start(f32[2,512]{1,0:T(2,128)} %param.25) | copy-start | bytes 12292
  467.0 18.4 %copy-start.14 = (f32[2,512,1024]{2,1,0:T(8,128)S(1)}, f32[2,512,1024]{2,1,0:T(8,128)}, u32[]{:S(2)}) copy-start(f32[2,512,1024]{2,1,0:T(8,128)} %param.24) | copy-start | bytes 12582916
  469.8 5.2 %collective-permute-start = (f32[1,16,512]{2,1,0:T(8,128)S(1)}, f32[1,16,512]{2,1,0:T(8,128)S(1)}, u32[]{:S(2)}, u32[]{:S(2)}) collective-permute-start(f32[1,16,512]{2,1,0:T(8,128)S(1)} %get-tuple-element.51), channel_id=1, source_target_pairs={{0,1},{1,4},{4,5},{5,8},{8,9},{9,12},{12,13},{2,3},{3,6},{6,7},{7,... | collective-permute-start | bytes 98312 | tf_op jit(solution)/shard_map/ppermute | solution.py:21
  473.1 5.2 %collective-permute-start.1 = (f32[1,16,512]{2,1,0:T(8,128)S(1)}, f32[1,16,512]{2,1,0:T(8,128)S(1)}, u32[]{:S(2)}, u32[]{:S(2)}) collective-permute-start(f32[1,16,512]{2,1,0:T(8,128)S(1)} %get-tuple-element.52), channel_id=1, source_target_pairs={{1,0},{4,1},{5,4},{8,5},{9,8},{12,9},{13,12},{3,2},{6,3},{7,6},{10... | collective-permute-start | bytes 98312 | tf_op jit(solution)/shard_map/ppermute | solution.py:24
  478.4 3.5 collective-permute-start.2
  480.6 4.5 collective-permute-start.3
  487.0 5.3 %collective-permute-start.4 = (f32[1,16,512]{2,1,0:T(8,128)S(1)}, f32[1,16,512]{2,1,0:T(8,128)S(1)}, u32[]{:S(2)}, u32[]{:S(2)}) collective-permute-start(f32[1,16,512]{2,1,0:T(8,128)S(1)} %get-tuple-element.49), channel_id=1, source_target_pairs={{0,1},{1,4},{4,5},{5,8},{8,9},{9,12},{12,13},{2,3},{3,6},{6,7},{7,... | collective-permute-start | bytes 98312 | tf_op jit(solution)/shard_map/ppermute | solution.py:21
  490.3 5.2 %collective-permute-start.5 = (f32[1,16,512]{2,1,0:T(8,128)S(1)}, f32[1,16,512]{2,1,0:T(8,128)S(1)}, u32[]{:S(2)}, u32[]{:S(2)}) collective-permute-start(f32[1,16,512]{2,1,0:T(8,128)S(1)} %get-tuple-element.50), channel_id=1, source_target_pairs={{1,0},{4,1},{5,4},{8,5},{9,8},{12,9},{13,12},{3,2},{6,3},{7,6},{10... | collective-permute-start | bytes 98312 | tf_op jit(solution)/shard_map/ppermute | solution.py:24
  495.6 2.7 collective-permute-start.6
  497.0 4.5 collective-permute-start.7
Sparse Core Ops, SparseCore 0:
  8.9 25.3 all-gather.3
  114.4 50.8 all-reduce.2
  182.9 31.5 reduce-scatter.2
  240.6 22.1 all-gather.5
  341.4 50.8 all-reduce.4
  409.9 31.5 reduce-scatter.4
  443.7 23.2 all-gather.7
where the time goes:
time: 516 us; the launch traced here: 511 us
  waiting for transfers between devices  258 us (50%)
  matrix products  165 us (32%)
  other arithmetic  27 us (5%)
  starting transfers between devices  25.4 us (5%)
  local copies, waits for them, and re-layouts  21.6 us (4%)
  between operations  14.3 us (3%)
    psum x2, waiting for transfers between devices, block_layer(): stream = stream + lax.psum(partial_out, ('col', 'rep'))  102 us
    all_gather x3, waiting for transfers between devices, widen(): return lax.all_gather(slice_cols, ('col', 'rep'), axis=1, tiled=True)  69.5 us
    reduce_scatter x2, waiting for transfers between devices, block_layer(): lax.psum_scatter(partial_mlp, ('col', 'rep'), scatter_dimension=1, tiled=...  57.4 us
    dot_general x2, matrix products, patch_attention(): jnp.einsum('qhd,khd->hqk', query_projection, key_proj, precision=MATMUL_P...  56 us
    dot_general x15, matrix products, matmul(): jnp.dot(left, right, precision=MATMUL_PRECISION, preferred_element_type=j...  53.7 us
    dot_general x2, matrix products, patch_attention(): jnp.einsum('hqk,khd->qhd', weights, value_proj, precision=MATMUL_PRECISION)  50.6 us
    unnamed x45, local copies, waits for them, and re-layouts  16.8 us
    all_to_all x1, waiting for transfers between devices, send_blocks(): lax.all_to_all(outgoing, 'tok', split_axis=0, concat_axis=0, tiled=True)  15.5 us
  transfers between devices with their start and end apart: 17, of which 12 were waited for; matrix products, arithmetic and copies ran while one was open for 2% of the time, Pallas kernels for 0%

commit v1 on v0

v1 whole, which is shorter than its diff:
```python
import functools

import jax
import jax.numpy as jnp
from jax import lax
from jax.experimental import pallas as pl
from jax.experimental.pallas import tpu as pltpu
from jax.sharding import PartitionSpec as P

PATCH = 1024
TR = 16
TC = 16
HD = 16
EPSILON = 1e-05
LOG2E = 1.4426950408889634
BF = jnp.bfloat16
F32 = jnp.float32
VMEM_LIMIT = 56 * 2**20
BORDER = 2


def vmem():
    return pl.BlockSpec(memory_space=pltpu.VMEM)


def smem():
    return pl.BlockSpec(memory_space=pltpu.SMEM)


def params():
    return pltpu.CompilerParams(vmem_limit_bytes=VMEM_LIMIT)


def split2(x):
    high = x.astype(BF)
    return high, (x - high.astype(F32)).astype(BF)


def split3(x):
    first = x.astype(BF)
    rest = x - first.astype(F32)
    second = rest.astype(BF)
    return first, second, (rest - second.astype(F32)).astype(BF)


def dot3(left, right, dims=(((1,), (0,)), ((), ()))):
    lh, ll = left
    rh, rl = right
    dot = functools.partial(lax.dot_general, dimension_numbers=dims, preferred_element_type=F32)
    return dot(lh, rh) + dot(lh, rl) + dot(ll, rh)


def layer_norm(values, gain_row):
    average = jnp.mean(values, axis=-1, keepdims=True)
    centered = values - average
    variance = jnp.mean(centered * centered, axis=-1, keepdims=True)
    return centered * lax.rsqrt(variance + EPSILON) * gain_row


def shift_by(k, count):
    return [(i, (i + k) % count) for i in range(count)]


def gather_slabs(piece):
    cols = lax.axis_size("col")
    reps = lax.axis_size("rep")
    far = [lax.ppermute(piece, "col", shift_by(k, cols)) for k in range(1, cols)]
    return [(p, lax.ppermute(p, "rep", shift_by(1, reps))) for p in [piece] + far]


def attention_kernel(cols, heads_per_step, place, *refs):
    slabs = refs[: 2 * cols]
    gain, wq0, wq1, wo0, wo1, keep_ref = refs[2 * cols : 2 * cols + 6]
    send_refs = refs[2 * cols + 6 : 2 * cols + 6 + cols - 1]
    x_all, q_t, k_t, v_t, attended = refs[2 * cols + 6 + cols - 1 :]
    col, rep = place[0], place[1]
    rows, width = x_all.shape
    slab = width // cols
    half = q_t.shape[1]
    step = pl.program_id(0)

    @pl.when(step == 0)
    def _():
        for k in range(cols):
            near, other = slabs[2 * k][...], slabs[2 * k + 1][...]
            low = jnp.where(rep == 0, near, other)
            high = jnp.where(rep == 0, other, near)
            at = pl.multiple_of(lax.rem(col + cols - k, cols) * slab, 128)
            x_all[:, pl.ds(at, slab)] = jnp.concatenate([low, high], axis=1)
        weights = [
            split2(jnp.concatenate([wq0[0, j], wq1[0, j]], axis=1)) for j in range(3)
        ]
        chunk = 256
        for start in range(0, rows, chunk):
            normed = split2(layer_norm(x_all[start : start + chunk, :], gain[...]))
            k_t[:, start : start + chunk] = dot3(normed, weights[1]).T
            v_t[:, start : start + chunk] = dot3(normed, weights[2]).T
        for start in range(0, half, chunk):
            at = pl.multiple_of(rep * half + start, chunk)
            normed = split2(layer_norm(x_all[pl.ds(at, chunk), :], gain[...]))
            q_t[:, start : start + chunk] = dot3(normed, weights[0]).T * (LOG2E * HD**-0.5)

    chunk = min(256, half)
    base = step * heads_per_step * HD

    def head_rows(h):
        return pl.ds(pl.multiple_of(base + h * HD, HD), HD)

    keys, values = [], []
    for h in range(heads_per_step):
        k1, k2, k3 = split3(k_t[head_rows(h), :])
        keys.append(jnp.concatenate([k1, k2, k1, k3, k2, k1], axis=0))
        v1, v2 = split2(v_t[head_rows(h), :])
        ones = jnp.ones_like(v1)
        values.append((jnp.concatenate([v1, v2, ones], axis=0), jnp.concatenate([v1, ones], axis=0)))

    def scores(h, at):
        q1, q2, q3 = split3(q_t[head_rows(h), at : at + chunk])
        queries = jnp.concatenate([q1, q1, q2, q1, q2, q3], axis=0)
        return lax.dot_general(
            keys[h], queries, (((0,), (0,)), ((), ())), preferred_element_type=F32
        )

    items = [(h, at) for h in range(heads_per_step) for at in range(0, half, chunk)]
    current = scores(*items[0])
    for i, (h, at) in enumerate(items):
        following = scores(*items[i + 1]) if i + 1 < len(items) else None
        weights = jnp.exp2(current - jnp.max(current, axis=0, keepdims=True))
        high, low = split2(weights)
        first = jnp.dot(values[h][0], high, preferred_element_type=F32)
        second = jnp.dot(values[h][1], low, preferred_element_type=F32)
        total = first[:HD] + first[HD : 2 * HD] + second[:HD]
        norm = first[2 * HD : 2 * HD + 1] + second[HD : HD + 1]
        attended[head_rows(h), at : at + chunk] = total / norm
        current = following

    @pl.when(step == pl.num_programs(0) - 1)
    def _():
        w_out = split2(jnp.concatenate([wo0[0], wo1[0]], axis=0))
        part = half // cols
        for k in range(cols):
            quarter = lax.rem(col + k, cols)
            at = pl.multiple_of(quarter * part, 128)
            mine = split2(attended[:, pl.ds(at, part)].T)
            result = dot3(mine, w_out)
            if k == 0:
                keep_ref[...] = result + x_all[pl.ds(rep * half + at, part), :]
            else:
                send_refs[k - 1][...] = result


def attention(place, slabs, gain, w_qkv, w_out, layer_index):
    cols = len(slabs)
    reps = lax.axis_size("rep")
    rows = slabs[0][0].shape[0]
    width = w_out[0].shape[-1]
    chip_width = 2 * w_qkv[0].shape[-1]
    half = rows // reps
    part = half // cols
    heads = chip_width // HD
    heads_per_step = 4
    local = w_qkv[0].shape[-1]
    fixed = lambda *block: pl.BlockSpec(
        (1,) + block, lambda h: (layer_index,) + (0,) * len(block)
    )
    out_block = pl.BlockSpec((part, width), lambda h: (0, 0))
    return pl.pallas_call(
        functools.partial(attention_kernel, cols, heads_per_step),
        grid=(heads // heads_per_step,),
        in_specs=[smem()]
        + [vmem()] * (2 * cols)
        + [vmem()]
        + [fixed(3, width, local)] * 2
        + [fixed(local, width)] * 2,
        out_specs=[out_block] * cols,
        out_shape=[jax.ShapeDtypeStruct((part, width), F32)] * cols,
        scratch_shapes=[
            pltpu.VMEM((rows, width), F32),
            pltpu.VMEM((chip_width, half), F32),
            pltpu.VMEM((chip_width, rows), F32),
            pltpu.VMEM((chip_width, rows), F32),
            pltpu.VMEM((chip_width, half), F32),
        ],
        compiler_params=params(),
        cost_estimate=pl.CostEstimate(
            flops=6 * 10**9, bytes_accessed=6 * 10**6, transcendentals=heads * rows * half
        ),
        name="attention",
    )(
        place,
        *[p for pair in slabs for p in pair],
        gain[layer_index][None],
        *w_qkv,
        *w_out,
    )


def mlp_rows(values, gain_row, up, down):
    normed = split2(layer_norm(values, gain_row))
    result = None
    for w_up, w_down in zip(up, down):
        hidden = dot3(normed, w_up)
        hidden = split2(hidden * (0.5 + 0.5 * lax.erf(hidden * 0.5**0.5)))
        term = dot3(hidden, w_down)
        result = term if result is None else result + term
    return result


def mlp_kernel(cols, place, *refs):
    pieces = refs[:cols]
    gain, wu0, wu1, wd0, wd1, keep_ref = refs[cols : cols + 6]
    send_refs = refs[cols + 6 : cols + 6 + cols - 1]
    partial, residual = refs[cols + 6 + cols - 1 :]
    col = place[0]
    part, width = pieces[0].shape
    slab = width // cols
    up = [split2(w[0]) for w in (wu0, wu1)]
    down = [split2(w[0]) for w in (wd0, wd1)]
    for k in range(cols):
        at = pl.multiple_of(lax.rem(col + cols - k, cols) * part, 128)
        values = pieces[k][...]
        partial[pl.ds(at, part), :] = mlp_rows(values, gain[...], up, down)
        residual[pl.ds(at, part), :] = values
    for k in range(cols):
        at = pl.multiple_of(lax.rem(col + k, cols) * slab, 128)
        if k == 0:
            keep_ref[...] = partial[:, pl.ds(at, slab)] + residual[:, pl.ds(at, slab)]
        else:
            send_refs[k - 1][...] = partial[:, pl.ds(at, slab)]


def mlp(place, pieces, gain, w_up, w_down, layer_index):
    cols = len(pieces)
    part, width = pieces[0].shape
    local = w_up[0].shape[-1]
    rows = part * cols
    slab = width // cols
    fixed = lambda *block: pl.BlockSpec(
        (1,) + block, lambda i: (layer_index,) + (0,) * len(block)
    )
    out_block = pl.BlockSpec((rows, slab), lambda i: (0, 0))
    return pl.pallas_call(
        functools.partial(mlp_kernel, cols),
        grid=(1,),
        in_specs=[smem()]
        + [vmem()] * (cols + 1)
        + [fixed(width, local)] * 2
        + [fixed(local, width)] * 2,
        out_specs=[out_block] * cols,
        out_shape=[jax.ShapeDtypeStruct((rows, slab), F32)] * cols,
        scratch_shapes=[pltpu.VMEM((rows, width), F32)] * 2,
        compiler_params=params(),
        cost_estimate=pl.CostEstimate(
            flops=4 * rows * width * 2 * local * 3, bytes_accessed=6 * 10**6, transcendentals=0
        ),
        name="mlp",
    )(place, *pieces, gain[layer_index][None], *w_up, *w_down)


def pooled_mlp_kernel(cols, place, *refs):
    pieces = refs[:cols]
    pillar, cells, gain, wu0, wu1, wd0, wd1 = refs[cols : cols + 7]
    own_refs = refs[cols + 7 : 2 * cols + 7]
    other_refs = refs[2 * cols + 7 :]
    col, rep = place[0], place[1]
    part = pieces[0].shape[0]
    up = [split2(w[0]) for w in (wu0, wu1)]
    down = [split2(w[0]) for w in (wd0, wd1)]
    totals = [None] * (2 * cols)
    for k in range(cols):
        source = lax.rem(col + cols - k, cols)
        at = pl.multiple_of(rep * part * cols + source * part, 128)
        tokens_cells = pillar[:, pl.ds(at, part)]
        values = pieces[k][...]
        result = mlp_rows(values, gain[...], up, down)
        if k == 0:
            result = result + values
        high, low = split2(result)
        for i in range(2 * cols):
            chosen = jnp.where(cells[i] == tokens_cells, 1.0, 0.0).astype(BF)
            term = jnp.dot(chosen, high, preferred_element_type=F32) + jnp.dot(
                chosen, low, preferred_element_type=F32
            )
            totals[i] = term if totals[i] is None else totals[i] + term
    for k in range(cols):
        own_refs[k][...] = totals[2 * k]
        other_refs[k][...] = totals[2 * k + 1]


def pooled_mlp(place, pieces, pillar, cells, gain, w_up, w_down, layer_index):
    cols = len(pieces)
    part, width = pieces[0].shape
    local = w_up[0].shape[-1]
    rows = part * cols
    count = cells.shape[1]
    fixed = lambda *block: pl.BlockSpec(
        (1,) + block, lambda i: (layer_index,) + (0,) * len(block)
    )
    out_block = pl.BlockSpec((count, width), lambda i: (0, 0))
    outs = pl.pallas_call(
        functools.partial(pooled_mlp_kernel, cols),
        grid=(1,),
        in_specs=[smem()]
        + [vmem()] * (cols + 3)
        + [fixed(width, local)] * 2
        + [fixed(local, width)] * 2,
        out_specs=[out_block] * (2 * cols),
        out_shape=[jax.ShapeDtypeStruct((count, width), F32)] * (2 * cols),
        compiler_params=params(),
        cost_estimate=pl.CostEstimate(
            flops=4 * rows * width * 2 * local * 3, bytes_accessed=6 * 10**6, transcendentals=0
        ),
        name="mlp_pool",
    )(place, *pieces, pillar, cells, gain[layer_index][None], *w_up, *w_down)
    return outs[:cols], outs[cols:]


def pick_blocks_kernel(outs, counts, index, *refs):
    sources = refs[: len(counts)]
    targets = refs[len(counts) : len(counts) + outs]
    blocks = refs[-1]
    start = 0
    for ref, count in zip(sources, counts):
        blocks[start : start + count] = ref[...]
        start += count
    each = targets[0].shape[0]
    for o in range(outs):
        for j in range(each):
            targets[o][j] = blocks[index[o * each + j]]


def pick_blocks(sources, index, outs, each):
    counts = [s.shape[0] for s in sources]
    shape = sources[0].shape[1:]
    return pl.pallas_call(
        functools.partial(pick_blocks_kernel, outs, counts),
        in_specs=[smem()] + [vmem()] * len(sources),
        out_specs=[vmem()] * outs,
        out_shape=[jax.ShapeDtypeStruct((each,) + shape, F32)] * outs,
        scratch_shapes=[pltpu.VMEM((sum(counts),) + shape, F32)],
        compiler_params=params(),
        name="pick_blocks",
    )(index, *sources)


def routes(dest_device, dest_slot):
    count = dest_device.shape[0]
    peers = lax.axis_size("tok")
    capacity = max(2, (count + peers - 4) // (peers - 1))
    order = jnp.arange(count, dtype=jnp.int32)
    earlier = (dest_device[:, None] == dest_device[None, :]) & (order[None, :] < order[:, None])
    rank = jnp.sum(earlier.astype(jnp.int32), axis=1)
    shifts = jnp.arange(peers, dtype=jnp.int32)
    targets = (lax.axis_index("tok") + shifts) % peers
    places = jnp.arange(capacity, dtype=jnp.int32)
    chosen = (
        (targets[:, None, None] == dest_device[None, None, :])
        & (places[None, :, None] == rank[None, None, :])
    ).astype(jnp.int32)
    blocks = jnp.sum(chosen * order, axis=-1)
    slots = jnp.sum(chosen * (dest_slot + 1), axis=-1)
    arrived = jnp.stack(
        [slots[0]]
        + [lax.ppermute(slots[k], "tok", shift_by(k, peers)) for k in range(1, peers)]
    ).reshape(-1)
    matches = (arrived[None, :] == order[:, None] + 1).astype(jnp.int32)
    sources = jnp.sum(matches * jnp.arange(peers * capacity, dtype=jnp.int32), axis=1)
    return blocks, sources


def raster_kernel(reps, place, tile, halo, depth, point, gain, out_ref, cells, normed):
    tok, col, rep, height, full_width = (place[i] for i in (2, 0, 1, 3, 4))
    tile_rows = out_ref.shape[0]
    tile_cols = out_ref.shape[1]
    width = out_ref.shape[2]
    wide = tile_cols + 2 * BORDER
    kept = tile_rows + BORDER
    padded = cells.shape[1]
    cells[...] = jnp.zeros_like(cells)
    normed[...] = jnp.zeros_like(normed)
    first = BORDER * (1 - rep)
    for i in range(kept):
        cells[first + i, 0:wide, :] = tile[i * wide : (i + 1) * wide, :]
    other = (tile_rows + BORDER) * rep
    for i in range(BORDER):
        cells[other + i, 0:wide, :] = halo[i * wide : (i + 1) * wide, :]
    lead = 8
    row_zero = tok * (tile_rows * reps) + rep * tile_rows - BORDER
    col_zero = col * tile_cols - BORDER
    for layer in range(2):
        rim = layer + 1
        grid_rows = tile_rows + 2 * BORDER - 2 * rim
        low_col, span = (0, padded) if layer == 0 else (BORDER, tile_cols)
        values = cells[...]
        mean = jnp.mean(values * values, axis=-1, keepdims=True)
        normed[:, lead : lead + padded, :] = values * lax.rsqrt(mean + EPSILON) * gain[layer : layer + 1]
        mixed = None
        for a in range(3):
            for b in range(3):
                start = lead + low_col + b - 1
                term = (
                    normed[rim - 1 + a : rim - 1 + a + grid_rows, start : start + span, :]
                    * depth[layer, a, b][None, None, :]
                )
                mixed = term if mixed is None else mixed + term
        left = split2(mixed.reshape(grid_rows * span, width))
        value = dot3(left, split2(point[layer, :, :width]))
        gate = dot3(left, split2(point[layer, :, width:]))
        change = (value * jax.nn.sigmoid(gate)).reshape(grid_rows, span, width)
        centre = cells[rim : rim + grid_rows, low_col : low_col + span, :]
        if layer == 0:
            row = row_zero + rim + lax.broadcasted_iota(jnp.int32, (grid_rows, span, 1), 0)
            column = col_zero + lax.broadcasted_iota(jnp.int32, (grid_rows, span, 1), 1)
            inside = (row >= 0) & (row < height) & (column >= 0) & (column < full_width)
            cells[rim : rim + grid_rows, :, :] = jnp.where(inside, centre + change, 0.0)
        else:
            out_ref[...] = centre + change


def raster_layers(place, tile, halo, depth_weight, point_weight, raster_gain, tile_rows):
    reps = lax.axis_size("rep")
    width = tile.shape[-1]
    padded = -(-(TC + 2 * BORDER) // 8) * 8
    return pl.pallas_call(
        functools.partial(raster_kernel, reps),
        in_specs=[smem()] + [vmem()] * 5,
        out_specs=vmem(),
        out_shape=jax.ShapeDtypeStruct((tile_rows, TC, width), F32),
        scratch_shapes=[
            pltpu.VMEM((tile_rows + 2 * BORDER, padded, width), F32),
            pltpu.VMEM((tile_rows + 2 * BORDER, padded + 16, width), F32),
        ],
        compiler_params=params(),
        name="raster",
    )(place, tile, halo, depth_weight, point_weight, raster_gain)


def tile_cells(tile_rows):
    cols = lax.axis_size("col")
    tok, col, rep = (lax.axis_index(a) for a in ("tok", "col", "rep"))
    full_width = TC * cols
    wide = TC + 2 * BORDER
    flat = jnp.arange((tile_rows + BORDER) * wide, dtype=jnp.int32)
    row, column = flat // wide, flat % wide
    tables = []
    for k in range(cols):
        for r in (rep, 1 - rep):
            x = ((col + k) % cols) * TC - BORDER + column
            y = tok * TR + r * (tile_rows - BORDER) + row
            tables.append(jnp.where((x >= 0) & (x < full_width), y * full_width + x, -2))
    return jnp.stack(tables)[:, :, None]


def on_device(
    tokens,
    w_qkv,
    w_out,
    w_up,
    w_down,
    attn_gain,
    mlp_gain,
    dest_device,
    dest_slot,
    pillar,
    depth_weight,
    point_weight,
    raster_gain,
):
    cols, reps, toks = (lax.axis_size(a) for a in ("col", "rep", "tok"))
    tok, col, rep = (lax.axis_index(a) for a in ("tok", "col", "rep"))
    swap = shift_by(1, reps)
    place = jnp.stack([col, rep, tok, jnp.int32(TR * toks), jnp.int32(TC * cols)]).astype(jnp.int32)
    slabs = gather_slabs(tokens)
    both = lambda w: (w, lax.ppermute(w, "rep", swap))
    w_qkv, w_out, w_up, w_down = (both(w) for w in (w_qkv, w_out, w_up, w_down))
    blocks_out, blocks_in = routes(dest_device, dest_slot)
    count = dest_device.shape[0]
    each = count // reps
    tile_rows = TR // reps
    cells = tile_cells(tile_rows)

    def attend(slabs, layer_index):
        keep, *sends = attention(place, slabs, attn_gain, w_qkv, w_out, layer_index)
        for k, part in enumerate(sends):
            keep = keep + lax.ppermute(part, "col", shift_by(k + 1, cols))
        return [keep] + [lax.ppermute(keep, "col", shift_by(k, cols)) for k in range(1, cols)]

    pieces = attend(slabs, 0)
    keep, *sends = mlp(place, pieces, mlp_gain, w_up, w_down, 0)
    for k, part in enumerate(sends):
        keep = keep + lax.ppermute(part, "col", shift_by(k + 1, cols))
    feature = keep.shape[1] // reps
    low, high = keep[:, :feature], keep[:, feature:]
    near = jnp.where(rep == 0, low, high)
    far = lax.ppermute(jnp.where(rep == 0, high, low), "rep", swap)
    in_blocks = lambda x: x.reshape(each, -1, feature)
    index = jnp.where(blocks_out // each == rep, blocks_out % each, each + blocks_out % each)
    capacity = index.shape[1]
    outgoing = pick_blocks([in_blocks(near), in_blocks(far)], index.reshape(-1), toks, capacity)
    incoming = [outgoing[0]] + [
        lax.ppermute(outgoing[k], "tok", shift_by(k, toks)) for k in range(1, toks)
    ]
    (moved,) = pick_blocks(incoming, blocks_in, 1, count)
    pieces = attend(gather_slabs(moved.reshape(-1, feature)), 1)

    own, other = pooled_mlp(place, pieces, pillar[None], cells, mlp_gain, w_up, w_down, 1)
    sums = [own[k] + lax.ppermute(other[k], "rep", swap) for k in range(cols)]
    tile = sums[0]
    for k in range(1, cols):
        tile = tile + lax.ppermute(sums[k], "col", shift_by(k, cols))
    edge = BORDER * (TC + 2 * BORDER)
    edge_rows = jnp.where(rep == 0, tile[:edge], tile[-edge:])
    pairs = [(i * reps + reps - 1, (i + 1) * reps) for i in range(toks - 1)]
    halo = lax.ppermute(edge_rows, ("tok", "rep"), pairs + [(b, a) for a, b in pairs])
    return raster_layers(place, tile, halo, depth_weight, point_weight, raster_gain, tile_rows)


def solution(mesh):
    placed = (
        P(("scene", "tok"), ("col", "rep")),
        P(None, None, None, ("col", "rep")),
        P(None, ("col", "rep"), None),
        P(None, None, ("col", "rep")),
        P(None, ("col", "rep"), None),
        P(),
        P(),
        P(("scene", "tok")),
        P(("scene", "tok")),
        P(("scene", "tok")),
        P(),
        P(),
        P(),
    )
    return jax.shard_map(
        on_device,
        mesh=mesh,
        in_specs=placed,
        out_specs=P(("scene", "tok", "rep"), "col", None),
        check_vma=False,
    )
```

time: 516 us -> 217 us (0.42)
  matrix products: 165 us -> 0 us
  waiting for transfers between devices: 258 us -> 95.3 us
  Pallas kernels: 0 us -> 65.1 us
  other arithmetic: 27 us -> 8.3 us
  between operations: 14.3 us -> 0.18 us
  starting transfers between devices: 25.4 us -> 37.8 us
  local copies, waits for them, and re-layouts: 21.6 us -> 9.44 us
    dot_general x22 -> x0, matrix products: 165 us -> none  [the longest x2 56 us: patch_attention(): jnp.einsum('qhd,khd->hqk', query_projection, key_proj, precision=MATMUL_P...]
    psum x2 -> x0, waiting for transfers between devices: 102 us -> none  [block_layer(): stream = stream + lax.psum(partial_out, ('col', 'rep'))]
    ppermute x8 -> x26, waiting for transfers between devices: 13 us -> 95.3 us  [the longest x2 24 us: attend(): keep = keep + lax.ppermute(part, 'col', shift_by(k + 1, cols))]
    all_gather x3 -> x0, waiting for transfers between devices: 69.5 us -> none  [widen(): return lax.all_gather(slice_cols, ('col', 'rep'), axis=1, tiled=True)]
    pallas_call x0 -> x7, Pallas kernels: none -> 65.1 us  [the longest x2 38.5 us: attention(): pl.pallas_call(functools.partial(attention_kernel, cols, heads_per_step),...]
    reduce_scatter x2 -> x0, waiting for transfers between devices: 57.4 us -> none  [block_layer(): lax.psum_scatter(partial_mlp, ('col', 'rep'), scatter_dimension=1, tiled=...]
    ppermute x8 -> x26, starting transfers between devices: 16.6 us -> 37.8 us  [the longest x1 6.95 us: on_device(): lax.ppermute(edge_rows, ('tok', 'rep'), pairs + [(b, a) for a, b in pairs])]
    reduce_sum x13 -> x3, other arithmetic: 21.6 us -> 1.2 us  [the longest x1 0.77 us: routes(): jnp.sum(matches * jnp.arange(peers * capacity, dtype=jnp.int32), axis=1)]
  transfers between devices with their start and end apart: 17 -> 26, of which waited for: 12 -> 14; matrix products, arithmetic and copies ran while one was open for 2% -> 5% of each run, Pallas kernels for 0% -> 9%
where the time goes in v1:
time: 217 us; the launch traced here: 216 us
  waiting for transfers between devices  95.3 us (44%)
  Pallas kernels  65.1 us (30%)
  starting transfers between devices  37.8 us (17%)
  local copies, waits for them, and re-layouts  9.44 us (4%)
  other arithmetic  8.3 us (4%)
    pallas_call x2, Pallas kernels, attention(): pl.pallas_call(functools.partial(attention_kernel, cols, heads_per_step),...  38.5 us
    ppermute x2, waiting for transfers between devices, attend(): keep = keep + lax.ppermute(part, 'col', shift_by(k + 1, cols))  24 us
    ppermute x2, waiting for transfers between devices, gather_slabs(): lax.ppermute(piece, 'col', shift_by(k, cols))  23 us
    ppermute x2, waiting for transfers between devices, attend(): lax.ppermute(keep, 'col', shift_by(k, cols))  20 us
    ppermute x3, waiting for transfers between devices, on_device(): lax.ppermute(outgoing[k], 'tok', shift_by(k, toks))  9.5 us
    ppermute x1, waiting for transfers between devices, on_device(): tile = tile + lax.ppermute(sums[k], 'col', shift_by(k, cols))  9.46 us
    pallas_call x1, Pallas kernels, pooled_mlp(): pl.pallas_call(functools.partial(pooled_mlp_kernel, cols), grid=(1,), in_...  8.94 us
    pallas_call x1, Pallas kernels, mlp(): pl.pallas_call(functools.partial(mlp_kernel, cols), grid=(1,), in_specs=[...  7.81 us
  transfers between devices with their start and end apart: 26, of which 14 were waited for; matrix products, arithmetic and copies ran while one was open for 5% of the time, Pallas kernels for 9%

profile of v1, /device:TPU:1, one launch (start us, length us, event | category | flops | bytes accessed | tf_op | source)
XLA Modules:
  0.0 216.2 jit_solution(11384326371750091869)
XLA Ops:
  0.1 2.7 %collective-permute-start.4 = (f32[1024,128]{1,0:T(8,128)}, f32[1024,128]{1,0:T(8,128)S(1)}, u32[]{:S(2)}, u32[]{:S(2)}) collective-permute-start(f32[1024,128]{1,0:T(8,128)} %refs_0_.1), channel_id=1, source_target_pairs={{0,2},{2,0},{1,3},{3,1},{4,6},{6,4},{5,7},{7,5},{8,10},{10,8},{9,1... | collective-permute-start | bytes 1572872 | tf_op jit(solution)/shard_map/ppermute | solution.py:67
  3.2 12.0 %collective-permute-done.4.refs_2_ = f32[1024,128]{1,0:T(8,128)S(1)} collective-permute-done((f32[1024,128]{1,0:T(8,128)}, f32[1024,128]{1,0:T(8,128)S(1)}, u32[]{:S(2)}, u32[]{:S(2)}) %collective-permute-start.4) | collective-permute-done | bytes 524320 | tf_op jit(solution)/shard_map/ppermute | solution.py:67
  16.9 1.3 fusion.5
  18.3 19.3 %attention.2 = (f32[256,512]{1,0:T(8,128)}, f32[256,512]{1,0:T(8,128)}) custom-call(s32[5]{0:T(128)} %stack.34.place, f32[1024,128]{1,0:T(8,128)} %refs_0_.1, f32[1024,128]{1,0:T(8,128)} %collective-permute-done.3.refs_1_, f32[1024,128]{1,0:T(8,128)} %copy-done.13, f32[1024,128]{1,0:T(8,128)} %collective-permute-done.5.refs_3_, ...), custom_call_target="tpu_custom_call" | custom-call | flops 6000000000 | bytes 6000000 | tf_op jit(solution)/shard_map/attention/pallas_call | solution.py:167
  37.6 1.5 collective-permute-start.8
  39.1 11.9 %collective-permute-done.8 = f32[256,512]{1,0:T(8,128)S(1)} collective-permute-done((f32[256,512]{1,0:T(8,128)}, f32[256,512]{1,0:T(8,128)S(1)}, u32[]{:S(2)}, u32[]{:S(2)}) %collective-permute-start.8) | collective-permute-done | bytes 524320 | tf_op jit(solution)/shard_map/ppermute | solution.py:485
  51.0 1.1 add.257.refs_0_
  52.1 1.5 collective-permute-start.9
  54.5 10.0 %collective-permute-done.9.refs_1_ = f32[256,512]{1,0:T(8,128)S(1)} collective-permute-done((f32[256,512]{1,0:T(8,128)S(1)}, f32[256,512]{1,0:T(8,128)S(1)}, u32[]{:S(2)}, u32[]{:S(2)}) %collective-permute-start.9) | collective-permute-done | bytes 524320 | tf_op jit(solution)/shard_map/ppermute | solution.py:486
  65.3 7.8 %mlp.1 = (f32[512,256]{1,0:T(8,128)}, f32[512,256]{1,0:T(8,128)}) custom-call(s32[5]{0:T(128)} %stack.34.place, f32[256,512]{1,0:T(8,128)} %copy-done.2, f32[256,512]{1,0:T(8,128)} %copy-done.16, f32[1,512]{1,0:T(1,128)} %get-tuple-element.41.refs_2_, f32[2,512,512]{2,1,0:T(8,128)} %refs_5_.7, f32[2,512,512]{2,1,0:T(8,128)} %copy-done.10, ...), custom_call_target="tpu_custom_call" | custom-call | flops 3221225472 | bytes 6000000 | tf_op jit(solution)/shard_map/mlp/pallas_call | solution.py:242
  73.1 1.5 collective-permute-start.12
  75.0 1.3 collective-permute-start
  76.4 2.3 %collective-permute-start.1 = (s32[5]{0:T(128)S(1)}, s32[5]{0:T(128)S(1)}, u32[]{:S(2)}, u32[]{:S(2)}) collective-permute-start(s32[5]{0:T(128)S(1)} %get-tuple-element.35), channel_id=1, source_target_pairs={{0,8},{4,12},{8,0},{12,4},{1,9},{5,13},{9,1},{13,5},{2,10},{6,14},... | collective-permute-start | bytes 68 | tf_op jit(solution)/shard_map/ppermute | solution.py:364
  78.7 1.1 collective-permute-start.2
  79.8 4.9 %collective-permute-done.12 = f32[512,256]{1,0:T(8,128)S(1)} collective-permute-done((f32[512,256]{1,0:T(8,128)}, f32[512,256]{1,0:T(8,128)S(1)}, u32[]{:S(2)}, u32[]{:S(2)}) %collective-permute-start.12) | collective-permute-done | bytes 524320 | tf_op jit(solution)/shard_map/ppermute | solution.py:491
  84.7 1.1 add.258
  86.6 3.0 %collective-permute-start.13 = (f32[512,128]{1,0:T(8,128)S(1)}, f32[512,128]{1,0:T(8,128)S(1)}, u32[]{:S(2)}, u32[]{:S(2)}) collective-permute-start(f32[512,128]{1,0:T(8,128)S(1)} %get-tuple-element.38), channel_id=1, source_target_pairs={{0,1},{1,0},{2,3},{3,2},{4,5},{5,4},{6,7},{7,6},{8,9},{9,8},{10,11... | collective-permute-start | bytes 786440 | tf_op jit(solution)/shard_map/ppermute | solution.py:495
  91.4 1.9 pick_blocks.2
  93.3 1.5 collective-permute-start.14
  94.8 2.3 %collective-permute-start.15 = (f32[5,64,128]{2,1,0:T(8,128)}, f32[5,64,128]{2,1,0:T(8,128)S(1)}, u32[]{:S(2)}, u32[]{:S(2)}) collective-permute-start(f32[5,64,128]{2,1,0:T(8,128)} %get-tuple-element.25), channel_id=1, source_target_pairs={{0,8},{4,12},{8,0},{12,4},{1,9},{5,13},{9,1},{13,5},{2,10},{6,14},... | collective-permute-start | bytes 491528 | tf_op jit(solution)/shard_map/ppermute | solution.py:501
  97.2 1.1 collective-permute-start.16
  99.3 2.1 collective-permute-done.14.refs_1_
  101.4 7.4 %collective-permute-done.15.refs_2_ = f32[5,64,128]{2,1,0:T(8,128)S(1)} collective-permute-done((f32[5,64,128]{2,1,0:T(8,128)}, f32[5,64,128]{2,1,0:T(8,128)S(1)}, u32[]{:S(2)}, u32[]{:S(2)}) %collective-permute-start.15) | collective-permute-done | bytes 163872 | tf_op jit(solution)/shard_map/ppermute | solution.py:501
  109.5 2.0 pick_blocks.3
  111.5 1.2 collective-permute-start.18
  112.7 0.9 collective-permute-start.17
  113.6 11.0 %collective-permute-done.18.refs_2_ = f32[1024,128]{1,0:T(8,128)S(1)} collective-permute-done((f32[1024,128]{1,0:T(8,128)}, f32[1024,128]{1,0:T(8,128)S(1)}, u32[]{:S(2)}, u32[]{:S(2)}) %collective-permute-start.18) | collective-permute-done | bytes 524320 | tf_op jit(solution)/shard_map/ppermute | solution.py:67
  124.6 1.4 collective-permute-start.19
  126.1 1.5 collective-permute-done.19.refs_3_
  127.6 0.8 copy-done.17
  128.5 19.2 %attention.3 = (f32[256,512]{1,0:T(8,128)}, f32[256,512]{1,0:T(8,128)}) custom-call(s32[5]{0:T(128)} %stack.34.place, f32[1024,128]{1,0:T(8,128)} %bitcast.15, f32[1024,128]{1,0:T(8,128)} %copy-done.15, f32[1024,128]{1,0:T(8,128)} %copy-done.14, f32[1024,128]{1,0:T(8,128)} %copy-done.17, f32[1,512]{1,0:T(1,128)} %get-tuple-element.42.refs_4_, ...), custom_call_target="tpu_custom_call" | custom-call | flops 6000000000 | bytes 6000000 | tf_op jit(solution)/shard_map/attention/pallas_call | solution.py:167
  147.7 1.2 collective-permute-start.20
  148.9 12.1 %collective-permute-done.20 = f32[256,512]{1,0:T(8,128)S(1)} collective-permute-done((f32[256,512]{1,0:T(8,128)}, f32[256,512]{1,0:T(8,128)S(1)}, u32[]{:S(2)}, u32[]{:S(2)}) %collective-permute-start.20) | collective-permute-done | bytes 524320 | tf_op jit(solution)/shard_map/ppermute | solution.py:485
  161.0 1.1 add.259.refs_0_
  162.2 1.3 collective-permute-start.21
  163.5 1.0 copy.29.refs_3_
  164.5 10.0 %collective-permute-done.21.refs_1_ = f32[256,512]{1,0:T(8,128)S(1)} collective-permute-done((f32[256,512]{1,0:T(8,128)S(1)}, f32[256,512]{1,0:T(8,128)S(1)}, u32[]{:S(2)}, u32[]{:S(2)}) %collective-permute-start.21) | collective-permute-done | bytes 524320 | tf_op jit(solution)/shard_map/ppermute | solution.py:486
  174.5 0.8 copy-done.12
  175.3 8.9 %mlp_pool.1 = (f32[200,512]{1,0:T(8,128)}, f32[200,512]{1,0:T(8,128)}, f32[200,512]{1,0:T(8,128)}, f32[200,512]{1,0:T(8,128)}) custom-call(s32[5]{0:T(128)} %stack.34.place, f32[256,512]{1,0:T(8,128)} %copy-done.1, f32[256,512]{1,0:T(8,128)} %copy-done.12, s32[1,1024]{1,0:T(1,128)} %bitcast.20, s32[4,200,1]{2,1,0:T(8,128)} %copy.29.refs_3_, ...), custom_call_target="tpu_custom_call" | custom-call | flops 3221225472 | bytes 6000000 | tf_op jit(solution)/shard_map/mlp_pool/pallas_call | solution.py:300
  184.2 2.1 collective-permute-start.23
  186.4 1.5 collective-permute-done.23
  187.9 1.1 add.279
  189.0 1.3 collective-permute-start.24
  190.3 9.5 %collective-permute-done.24 = f32[200,512]{1,0:T(8,128)S(1)} collective-permute-done((f32[200,512]{1,0:T(8,128)S(1)}, f32[200,512]{1,0:T(8,128)S(1)}, u32[]{:S(2)}, u32[]{:S(2)}) %collective-permute-start.24) | collective-permute-done | bytes 409632 | tf_op jit(solution)/shard_map/ppermute | solution.py:510
  199.7 1.1 add_add_fusion.tile
  200.9 6.9 %collective-permute-start.25 = (f32[40,512]{1,0:T(8,128)S(1)}, f32[40,512]{1,0:T(8,128)S(1)}, u32[]{:S(2)}, u32[]{:S(2)}) collective-permute-start(f32[40,512]{1,0:T(8,128)S(1)} %slice_select_fusion.2), channel_id=1, source_target_pairs={{1,4},{5,8},{9,12},{4,1},{8,5},{12,9},{3,6},{7,10},{11,14},{6,3},{... | collective-permute-start | bytes 245768 | tf_op jit(solution)/shard_map/ppermute | solution.py:514
  208.5 1.2 collective-permute-done.25.halo
  210.3 5.9 %raster.1 = f32[8,16,512]{2,1,0:T(8,128)} custom-call(s32[5]{0:T(128)} %stack.34.place, f32[200,512]{1,0:T(8,128)} %copy-done, f32[40,512]{1,0:T(8,128)} %copy-done.7, f32[2,3,3,512]{3,2,1,0:T(4,128)} %copy.30.depth, f32[2,512,1024]{2,1,0:T(8,128)} %point.1, f32[2,512]{1,0:T(2,128)} %gain.1), custom_call_target="tpu_custom_call" | custom-call | tf_op jit(solution)/shard_map/raster/pallas_call | solution.py:424
  (84 shorter events, 10.1 us)
Async XLA Ops:
  0.0 18.2 %collective-permute-start.6 = (f32[2,3,512,128]{3,2,1,0:T(8,128)}, f32[2,3,512,128]{3,2,1,0:T(8,128)}, u32[]{:S(2)}, u32[]{:S(2)}) collective-permute-start(f32[2,3,512,128]{3,2,1,0:T(8,128)} %refs_5_.6), channel_id=1, source_target_pairs={{0,1},{1,0},{2,3},{3,2},{4,5},{5,4},{6,7},{7,6},{8,9},{9,8},{10,11... | collective-permute-start | bytes 4718600 | tf_op jit(solution)/shard_map/ppermute | solution.py:474
  0.1 15.2 %collective-permute-start.4 = (f32[1024,128]{1,0:T(8,128)}, f32[1024,128]{1,0:T(8,128)S(1)}, u32[]{:S(2)}, u32[]{:S(2)}) collective-permute-start(f32[1024,128]{1,0:T(8,128)} %refs_0_.1), channel_id=1, source_target_pairs={{0,2},{2,0},{1,3},{3,1},{4,6},{6,4},{5,7},{7,5},{8,10},{10,8},{9,1... | collective-permute-start | bytes 1572872 | tf_op jit(solution)/shard_map/ppermute | solution.py:67
  2.7 13.1 %collective-permute-start.7 = (f32[2,128,512]{2,1,0:T(8,128)}, f32[2,128,512]{2,1,0:T(8,128)S(1)}, u32[]{:S(2)}, u32[]{:S(2)}) collective-permute-start(f32[2,128,512]{2,1,0:T(8,128)} %refs_7_.4), channel_id=1, source_target_pairs={{0,1},{1,0},{2,3},{3,2},{4,5},{5,4},{6,7},{7,6},{8,9},{9,8},{10,11... | collective-permute-start | bytes 1572872 | tf_op jit(solution)/shard_map/ppermute | solution.py:474
  3.0 15.2 %collective-permute-start.3 = (f32[1024,128]{1,0:T(8,128)}, f32[1024,128]{1,0:T(8,128)}, u32[]{:S(2)}, u32[]{:S(2)}) collective-permute-start(f32[1024,128]{1,0:T(8,128)} %refs_0_.1), channel_id=1, source_target_pairs={{0,1},{1,0},{2,3},{3,2},{4,5},{5,4},{6,7},{7,6},{8,9},{9,8},{10,11... | collective-permute-start | bytes 1572872 | tf_op jit(solution)/shard_map/ppermute | solution.py:68
  15.2 3.0 %copy-start.13 = (f32[1024,128]{1,0:T(8,128)}, f32[1024,128]{1,0:T(8,128)S(1)}, u32[]{:S(2)}) copy-start(f32[1024,128]{1,0:T(8,128)S(1)} %collective-permute-done.4.refs_2_) | copy-start | bytes 1572868
  15.2 3.0 %collective-permute-start.5 = (f32[1024,128]{1,0:T(8,128)S(1)}, f32[1024,128]{1,0:T(8,128)}, u32[]{:S(2)}, u32[]{:S(2)}) collective-permute-start(f32[1024,128]{1,0:T(8,128)S(1)} %collective-permute-done.4.refs_2_), channel_id=1, source_target_pairs={{0,1},{1,0},{2,3},{3,2},{4,5},{5,4},{6,7},{7,6},{8,9},{9,8},{10,11... | collective-permute-start | bytes 1572872 | tf_op jit(solution)/shard_map/ppermute | solution.py:68
  15.8 38.7 %collective-permute-start.10 = (f32[2,512,512]{2,1,0:T(8,128)}, f32[2,512,512]{2,1,0:T(8,128)S(1)}, u32[]{:S(2)}, u32[]{:S(2)}) collective-permute-start(f32[2,512,512]{2,1,0:T(8,128)} %refs_5_.7), channel_id=1, source_target_pairs={{0,1},{1,0},{2,3},{3,2},{4,5},{5,4},{6,7},{7,6},{8,9},{9,8},{10,11... | collective-permute-start | bytes 6291464 | tf_op jit(solution)/shard_map/ppermute | solution.py:474
  15.8 2.5 %copy-start.11 = (f32[2,128,512]{2,1,0:T(8,128)}, f32[2,128,512]{2,1,0:T(8,128)S(1)}, u32[]{:S(2)}) copy-start(f32[2,128,512]{2,1,0:T(8,128)S(1)} %collective-permute-done.7.refs_8_) | copy-start | bytes 1572868
  15.8 38.6 %collective-permute-start.11 = (f32[2,512,512]{2,1,0:T(8,128)}, f32[2,512,512]{2,1,0:T(8,128)}, u32[]{:S(2)}, u32[]{:S(2)}) collective-permute-start(f32[2,512,512]{2,1,0:T(8,128)} %refs_7_.5), channel_id=1, source_target_pairs={{0,1},{1,0},{2,3},{3,2},{4,5},{5,4},{6,7},{7,6},{8,9},{9,8},{10,11... | collective-permute-start | bytes 6291464 | tf_op jit(solution)/shard_map/ppermute | solution.py:474
  18.3 20.8 %copy-start.18 = (s32[16]{0:T(128)S(1)}, s32[16]{0:T(128)}, u32[]{:S(2)}) copy-start(s32[16]{0:T(128)} %param.20) | copy-start | bytes 196
  18.3 35.6 %copy-start.9 = (f32[2,512]{1,0:T(2,128)S(1)}, f32[2,512]{1,0:T(2,128)}, u32[]{:S(2)}) copy-start(f32[2,512]{1,0:T(2,128)} %param.19) | copy-start | bytes 12292
  37.6 13.4 %collective-permute-start.8 = (f32[256,512]{1,0:T(8,128)}, f32[256,512]{1,0:T(8,128)S(1)}, u32[]{:S(2)}, u32[]{:S(2)}) collective-permute-start(f32[256,512]{1,0:T(8,128)} %get-tuple-element.20), channel_id=1, source_target_pairs={{0,2},{2,0},{1,3},{3,1},{4,6},{6,4},{5,7},{7,5},{8,10},{10,8},{9,1... | collective-permute-start | bytes 1572872 | tf_op jit(solution)/shard_map/ppermute | solution.py:485
  52.1 12.4 %copy-start.2 = (f32[256,512]{1,0:T(8,128)}, f32[256,512]{1,0:T(8,128)S(1)}, u32[]{:S(2)}) copy-start(f32[256,512]{1,0:T(8,128)S(1)} %add.257.refs_0_) | copy-start | bytes 1572868
  52.1 12.4 %collective-permute-start.9 = (f32[256,512]{1,0:T(8,128)S(1)}, f32[256,512]{1,0:T(8,128)S(1)}, u32[]{:S(2)}, u32[]{:S(2)}) collective-permute-start(f32[256,512]{1,0:T(8,128)S(1)} %add.257.refs_0_), channel_id=1, source_target_pairs={{0,2},{2,0},{1,3},{3,1},{4,6},{6,4},{5,7},{7,5},{8,10},{10,8},{9,1... | collective-permute-start | bytes 1572872 | tf_op jit(solution)/shard_map/ppermute | solution.py:486
  54.5 10.1 %copy-start.10 = (f32[2,512,512]{2,1,0:T(8,128)}, f32[2,512,512]{2,1,0:T(8,128)S(1)}, u32[]{:S(2)}) copy-start(f32[2,512,512]{2,1,0:T(8,128)S(1)} %collective-permute-done.10.refs_4_.refs_6_) | copy-start | bytes 6291460
  64.5 0.8 copy-start.16
  65.3 9.3 %copy-start.19 = (s32[16]{0:T(128)S(1)}, s32[16]{0:T(128)}, u32[]{:S(2)}) copy-start(s32[16]{0:T(128)} %param.21) | copy-start | bytes 196
  73.1 11.6 %collective-permute-start.12 = (f32[512,256]{1,0:T(8,128)}, f32[512,256]{1,0:T(8,128)S(1)}, u32[]{:S(2)}, u32[]{:S(2)}) collective-permute-start(f32[512,256]{1,0:T(8,128)} %get-tuple-element.22), channel_id=1, source_target_pairs={{0,2},{2,0},{1,3},{3,1},{4,6},{6,4},{5,7},{7,5},{8,10},{10,8},{9,1... | collective-permute-start | bytes 1572872 | tf_op jit(solution)/shard_map/ppermute | solution.py:491
  75.0 15.3 %collective-permute-start = (s32[5]{0:T(128)S(1)}, s32[5]{0:T(128)S(1)}, u32[]{:S(2)}, u32[]{:S(2)}) collective-permute-start(s32[5]{0:T(128)S(1)} %get-tuple-element.33), channel_id=1, source_target_pairs={{0,4},{4,8},{8,12},{12,0},{1,5},{5,9},{9,13},{13,1},{2,6},{6,10},{... | collective-permute-start | bytes 68 | tf_op jit(solution)/shard_map/ppermute | solution.py:364
  76.4 14.0 %collective-permute-start.1 = (s32[5]{0:T(128)S(1)}, s32[5]{0:T(128)S(1)}, u32[]{:S(2)}, u32[]{:S(2)}) collective-permute-start(s32[5]{0:T(128)S(1)} %get-tuple-element.35), channel_id=1, source_target_pairs={{0,8},{4,12},{8,0},{12,4},{1,9},{5,13},{9,1},{13,5},{2,10},{6,14},... | collective-permute-start | bytes 68 | tf_op jit(solution)/shard_map/ppermute | solution.py:364
  78.7 11.8 %collective-permute-start.2 = (s32[5]{0:T(128)S(1)}, s32[5]{0:T(128)S(1)}, u32[]{:S(2)}, u32[]{:S(2)}) collective-permute-start(s32[5]{0:T(128)S(1)} %get-tuple-element.34), channel_id=1, source_target_pairs={{0,12},{4,0},{8,4},{12,8},{1,13},{5,1},{9,5},{13,9},{2,14},{6,2},{... | collective-permute-start | bytes 68 | tf_op jit(solution)/shard_map/ppermute | solution.py:364
  86.6 4.1 %collective-permute-start.13 = (f32[512,128]{1,0:T(8,128)S(1)}, f32[512,128]{1,0:T(8,128)S(1)}, u32[]{:S(2)}, u32[]{:S(2)}) collective-permute-start(f32[512,128]{1,0:T(8,128)S(1)} %get-tuple-element.38), channel_id=1, source_target_pairs={{0,1},{1,0},{2,3},{3,2},{4,5},{5,4},{6,7},{7,6},{8,9},{9,8},{10,11... | collective-permute-start | bytes 786440 | tf_op jit(solution)/shard_map/ppermute | solution.py:495
  90.7 0.7 copy-start.3
  93.3 8.1 %collective-permute-start.14 = (f32[5,64,128]{2,1,0:T(8,128)}, f32[5,64,128]{2,1,0:T(8,128)S(1)}, u32[]{:S(2)}, u32[]{:S(2)}) collective-permute-start(f32[5,64,128]{2,1,0:T(8,128)} %get-tuple-element.24), channel_id=1, source_target_pairs={{0,4},{4,8},{8,12},{12,0},{1,5},{5,9},{9,13},{13,1},{2,6},{6,10},{... | collective-permute-start | bytes 491528 | tf_op jit(solution)/shard_map/ppermute | solution.py:501
  94.8 13.9 %collective-permute-start.15 = (f32[5,64,128]{2,1,0:T(8,128)}, f32[5,64,128]{2,1,0:T(8,128)S(1)}, u32[]{:S(2)}, u32[]{:S(2)}) collective-permute-start(f32[5,64,128]{2,1,0:T(8,128)} %get-tuple-element.25), channel_id=1, source_target_pairs={{0,8},{4,12},{8,0},{12,4},{1,9},{5,13},{9,1},{13,5},{2,10},{6,14},... | collective-permute-start | bytes 491528 | tf_op jit(solution)/shard_map/ppermute | solution.py:501
  97.2 11.6 %collective-permute-start.16 = (f32[5,64,128]{2,1,0:T(8,128)}, f32[5,64,128]{2,1,0:T(8,128)S(1)}, u32[]{:S(2)}, u32[]{:S(2)}) collective-permute-start(f32[5,64,128]{2,1,0:T(8,128)} %get-tuple-element.26), channel_id=1, source_target_pairs={{0,12},{4,0},{8,4},{12,8},{1,13},{5,1},{9,5},{13,9},{2,14},{6,2},{... | collective-permute-start | bytes 491528 | tf_op jit(solution)/shard_map/ppermute | solution.py:501
  101.4 7.4 %copy-start.4 = (f32[5,64,128]{2,1,0:T(8,128)}, f32[5,64,128]{2,1,0:T(8,128)S(1)}, u32[]{:S(2)}) copy-start(f32[5,64,128]{2,1,0:T(8,128)S(1)} %collective-permute-done.14.refs_1_) | copy-start | bytes 491524
  108.8 0.7 copy-start.5
  108.8 0.7 copy-start.6
  111.5 13.1 %collective-permute-start.18 = (f32[1024,128]{1,0:T(8,128)}, f32[1024,128]{1,0:T(8,128)S(1)}, u32[]{:S(2)}, u32[]{:S(2)}) collective-permute-start(f32[1024,128]{1,0:T(8,128)} %bitcast.13), channel_id=1, source_target_pairs={{0,2},{2,0},{1,3},{3,1},{4,6},{6,4},{5,7},{7,5},{8,10},{10,8},{9,1... | collective-permute-start | bytes 1572872 | tf_op jit(solution)/shard_map/ppermute | solution.py:67
  112.7 13.3 %collective-permute-start.17 = (f32[1024,128]{1,0:T(8,128)}, f32[1024,128]{1,0:T(8,128)S(1)}, u32[]{:S(2)}, u32[]{:S(2)}) collective-permute-start(f32[1024,128]{1,0:T(8,128)} %bitcast.14), channel_id=1, source_target_pairs={{0,1},{1,0},{2,3},{3,2},{4,5},{5,4},{6,7},{7,6},{8,9},{9,8},{10,11... | collective-permute-start | bytes 1572872 | tf_op jit(solution)/shard_map/ppermute | solution.py:68
  124.6 3.0 %copy-start.14 = (f32[1024,128]{1,0:T(8,128)}, f32[1024,128]{1,0:T(8,128)S(1)}, u32[]{:S(2)}) copy-start(f32[1024,128]{1,0:T(8,128)S(1)} %collective-permute-done.18.refs_2_) | copy-start | bytes 1572868
  124.6 3.0 %collective-permute-start.19 = (f32[1024,128]{1,0:T(8,128)S(1)}, f32[1024,128]{1,0:T(8,128)S(1)}, u32[]{:S(2)}, u32[]{:S(2)}) collective-permute-start(f32[1024,128]{1,0:T(8,128)S(1)} %collective-permute-done.18.refs_2_), channel_id=1, source_target_pairs={{0,1},{1,0},{2,3},{3,2},{4,5},{5,4},{6,7},{7,6},{8,9},{9,8},{10,11... | collective-permute-start | bytes 1572872 | tf_op jit(solution)/shard_map/ppermute | solution.py:68
  126.1 1.5 copy-start.15
  127.6 0.8 copy-start.17
  147.7 13.3 %collective-permute-start.20 = (f32[256,512]{1,0:T(8,128)}, f32[256,512]{1,0:T(8,128)S(1)}, u32[]{:S(2)}, u32[]{:S(2)}) collective-permute-start(f32[256,512]{1,0:T(8,128)} %get-tuple-element.28), channel_id=1, source_target_pairs={{0,2},{2,0},{1,3},{3,1},{4,6},{6,4},{5,7},{7,5},{8,10},{10,8},{9,1... | collective-permute-start | bytes 1572872 | tf_op jit(solution)/shard_map/ppermute | solution.py:485
  162.2 12.3 %copy-start.1 = (f32[256,512]{1,0:T(8,128)}, f32[256,512]{1,0:T(8,128)S(1)}, u32[]{:S(2)}) copy-start(f32[256,512]{1,0:T(8,128)S(1)} %add.259.refs_0_) | copy-start | bytes 1572868
  162.2 12.3 %collective-permute-start.21 = (f32[256,512]{1,0:T(8,128)S(1)}, f32[256,512]{1,0:T(8,128)S(1)}, u32[]{:S(2)}, u32[]{:S(2)}) collective-permute-start(f32[256,512]{1,0:T(8,128)S(1)} %add.259.refs_0_), channel_id=1, source_target_pairs={{0,2},{2,0},{1,3},{3,1},{4,6},{6,4},{5,7},{7,5},{8,10},{10,8},{9,1... | collective-permute-start | bytes 1572872 | tf_op jit(solution)/shard_map/ppermute | solution.py:486
  174.5 0.8 copy-start.12
  184.2 23.6 %copy-start.8 = (f32[2,3,3,512]{3,0,2,1:T(2,128)S(1)}, f32[2,3,3,512]{3,0,2,1:T(2,128)}, u32[]{:S(2)}) copy-start(f32[2,3,3,512]{3,0,2,1:T(2,128)} %param.23) | copy-start | bytes 110596
  184.2 3.7 %collective-permute-start.23 = (f32[200,512]{1,0:T(8,128)}, f32[200,512]{1,0:T(8,128)S(1)}, u32[]{:S(2)}, u32[]{:S(2)}) collective-permute-start(f32[200,512]{1,0:T(8,128)} %get-tuple-element.32), channel_id=1, source_target_pairs={{0,1},{1,0},{2,3},{3,2},{4,5},{5,4},{6,7},{7,6},{8,9},{9,8},{10,11... | collective-permute-start | bytes 1228808 | tf_op jit(solution)/shard_map/ppermute | solution.py:507
  186.3 3.9 %collective-permute-start.22 = (f32[200,512]{1,0:T(8,128)}, f32[200,512]{1,0:T(8,128)S(1)}, u32[]{:S(2)}, u32[]{:S(2)}) collective-permute-start(f32[200,512]{1,0:T(8,128)} %get-tuple-element.30), channel_id=1, source_target_pairs={{0,1},{1,0},{2,3},{3,2},{4,5},{5,4},{6,7},{7,6},{8,9},{9,8},{10,11... | collective-permute-start | bytes 1228808 | tf_op jit(solution)/shard_map/ppermute | solution.py:507
  189.0 10.7 %collective-permute-start.24 = (f32[200,512]{1,0:T(8,128)S(1)}, f32[200,512]{1,0:T(8,128)S(1)}, u32[]{:S(2)}, u32[]{:S(2)}) collective-permute-start(f32[200,512]{1,0:T(8,128)S(1)} %add.279), channel_id=1, source_target_pairs={{0,2},{2,0},{1,3},{3,1},{4,6},{6,4},{5,7},{7,5},{8,10},{10,8},{9,1... | collective-permute-start | bytes 1228808 | tf_op jit(solution)/shard_map/ppermute | solution.py:510
  200.8 8.9 %copy-start = (f32[200,512]{1,0:T(8,128)}, f32[200,512]{1,0:T(8,128)S(1)}, u32[]{:S(2)}) copy-start(f32[200,512]{1,0:T(8,128)S(1)} %add_add_fusion.tile) | copy-start | bytes 1228804
  200.9 8.8 %collective-permute-start.25 = (f32[40,512]{1,0:T(8,128)S(1)}, f32[40,512]{1,0:T(8,128)S(1)}, u32[]{:S(2)}, u32[]{:S(2)}) collective-permute-start(f32[40,512]{1,0:T(8,128)S(1)} %slice_select_fusion.2), channel_id=1, source_target_pairs={{1,4},{5,8},{9,12},{4,1},{8,5},{12,9},{3,6},{7,10},{11,14},{6,3},{... | collective-permute-start | bytes 245768 | tf_op jit(solution)/shard_map/ppermute | solution.py:514
  209.7 0.6 copy-start.7

commit v2 on v1

--- a/solution.py
+++ b/solution.py
@@ -68,38 +68,70 @@
     return [(p, lax.ppermute(p, "rep", shift_by(1, reps))) for p in [piece] + far]
 
 
-def attention_kernel(cols, heads_per_step, place, *refs):
+def qkv_kernel(cols, units, halves, place, *refs):
     slabs = refs[: 2 * cols]
-    gain, wq0, wq1, wo0, wo1, keep_ref = refs[2 * cols : 2 * cols + 6]
-    send_refs = refs[2 * cols + 6 : 2 * cols + 6 + cols - 1]
-    x_all, q_t, k_t, v_t, attended = refs[2 * cols + 6 + cols - 1 :]
+    gain = refs[2 * cols]
+    pieces = refs[2 * cols + 1 : 2 * cols + 1 + units]
+    q_t, k_t, v_t, x_half, x_all = refs[2 * cols + 1 + units :]
     col, rep = place[0], place[1]
     rows, width = x_all.shape
     slab = width // cols
     half = q_t.shape[1]
+    for k in range(cols):
+        near, other = slabs[2 * k][...], slabs[2 * k + 1][...]
+        low = jnp.where(rep == 0, near, other)
+        high = jnp.where(rep == 0, other, near)
+        at = pl.multiple_of(lax.rem(col + cols - k, cols) * slab, 128)
+        x_all[:, pl.ds(at, slab)] = jnp.concatenate([low, high], axis=1)
+    weights = [split2(jnp.concatenate([u[j] for u in pieces], axis=0)) for j in range(3)]
+    dims = (((1,), (1,)), ((), ()))
+    chunk = 256
+    for start in range(0, rows, chunk):
+        normed = split2(layer_norm(x_all[start : start + chunk, :], gain[...]))
+        k_t[:, start : start + chunk] = dot3(weights[1], normed, dims)
+        v_t[:, start : start + chunk] = dot3(weights[2], normed, dims)
+    first = (rep if halves == "rep" else col) * half
+    chunk = min(chunk, half)
+    for start in range(0, half, chunk):
+        values = x_all[pl.ds(pl.multiple_of(first + start, chunk), chunk), :]
+        x_half[start : start + chunk, :] = values
+        normed = split2(layer_norm(values, gain[...]))
+        q_t[:, start : start + chunk] = dot3(weights[0], normed, dims) * (LOG2E * HD**-0.5)
+
+
+def project(place, slabs, gain, units, halves):
+    cols = len(slabs)
+    rows = slabs[0][0].shape[0]
+    width = units[0].shape[-1]
+    features = sum(u.shape[1] for u in units)
+    half = rows // lax.axis_size(halves)
+    shape = lambda *dims: jax.ShapeDtypeStruct(dims, F32)
+    return pl.pallas_call(
+        functools.partial(qkv_kernel, cols, len(units), halves),
+        in_specs=[smem()] + [vmem()] * (2 * cols + 1 + len(units)),
+        out_specs=[vmem()] * 4,
+        out_shape=[
+            shape(features, half),
+            shape(features, rows),
+            shape(features, rows),
+            shape(half, width),
+        ],
+        scratch_shapes=[pltpu.VMEM((rows, width), F32)],
+        compiler_params=params(),
+        cost_estimate=pl.CostEstimate(
+            flops=6 * rows * width * features * 3, bytes_accessed=8 * 10**6, transcendentals=0
+        ),
+        name="project",
+    )(place, *[p for pair in slabs for p in pair], gain, *units)
+
+
+def attention_kernel(parts, units, heads_per_step, scatter, place, *refs):
+    q_t, k_t, v_t, x_half = refs[:4]
+    pieces = refs[4 : 4 + units]
+    outs = refs[4 + units : -1]
+    attended = refs[-1]
+    half = q_t.shape[1]
     step = pl.program_id(0)
-
-    @pl.when(step == 0)
-    def _():
-        for k in range(cols):
-            near, other = slabs[2 * k][...], slabs[2 * k + 1][...]
-            low = jnp.where(rep == 0, near, other)
-            high = jnp.where(rep == 0, other, near)
-            at = pl.multiple_of(lax.rem(col + cols - k, cols) * slab, 128)
-            x_all[:, pl.ds(at, slab)] = jnp.concatenate([low, high], axis=1)
-        weights = [
-            split2(jnp.concatenate([wq0[0, j], wq1[0, j]], axis=1)) for j in range(3)
-        ]
-        chunk = 256
-        for start in range(0, rows, chunk):
-            normed = split2(layer_norm(x_all[start : start + chunk, :], gain[...]))
-            k_t[:, start : start + chunk] = dot3(normed, weights[1]).T
-            v_t[:, start : start + chunk] = dot3(normed, weights[2]).T
-        for start in range(0, half, chunk):
-            at = pl.multiple_of(rep * half + start, chunk)
-            normed = split2(layer_norm(x_all[pl.ds(at, chunk), :], gain[...]))
-            q_t[:, start : start + chunk] = dot3(normed, weights[0]).T * (LOG2E * HD**-0.5)
-
     chunk = min(256, half)
     base = step * heads_per_step * HD
 
@@ -136,142 +168,113 @@
 
     @pl.when(step == pl.num_programs(0) - 1)
     def _():
-        w_out = split2(jnp.concatenate([wo0[0], wo1[0]], axis=0))
-        part = half // cols
-        for k in range(cols):
-            quarter = lax.rem(col + k, cols)
-            at = pl.multiple_of(quarter * part, 128)
-            mine = split2(attended[:, pl.ds(at, part)].T)
-            result = dot3(mine, w_out)
+        w_out = split2(jnp.concatenate([u[3] for u in pieces], axis=0))
+        part = half // parts
+        mine = place[0] if scatter else place[1]
+        for k in range(parts):
+            at = pl.multiple_of(lax.rem(mine + k, parts) * part, 128)
+            result = dot3(split2(attended[:, pl.ds(at, part)].T), w_out)
             if k == 0:
-                keep_ref[...] = result + x_all[pl.ds(rep * half + at, part), :]
+                result = result + x_half[pl.ds(at, part), :]
+            if scatter:
+                outs[k][...] = result
             else:
-                send_refs[k - 1][...] = result
-
-
-def attention(place, slabs, gain, w_qkv, w_out, layer_index):
-    cols = len(slabs)
-    reps = lax.axis_size("rep")
-    rows = slabs[0][0].shape[0]
-    width = w_out[0].shape[-1]
-    chip_width = 2 * w_qkv[0].shape[-1]
-    half = rows // reps
-    part = half // cols
-    heads = chip_width // HD
+                outs[0][pl.ds(at, part), :] = result
+
+
+def attention(place, projected, units, scatter):
+    parts = lax.axis_size("col" if scatter else "rep")
+    features, half = projected[0].shape
+    rows = projected[1].shape[1]
+    width = units[0].shape[-1]
+    heads = features // HD
     heads_per_step = 4
-    local = w_qkv[0].shape[-1]
-    fixed = lambda *block: pl.BlockSpec(
-        (1,) + block, lambda h: (layer_index,) + (0,) * len(block)
-    )
-    out_block = pl.BlockSpec((part, width), lambda h: (0, 0))
+    shapes = [(half // parts, width)] * parts if scatter else [(half, width)]
     return pl.pallas_call(
-        functools.partial(attention_kernel, cols, heads_per_step),
+        functools.partial(attention_kernel, parts, len(units), heads_per_step, scatter),
         grid=(heads // heads_per_step,),
-        in_specs=[smem()]
-        + [vmem()] * (2 * cols)
-        + [vmem()]
-        + [fixed(3, width, local)] * 2
-        + [fixed(local, width)] * 2,
-        out_specs=[out_block] * cols,
-        out_shape=[jax.ShapeDtypeStruct((part, width), F32)] * cols,
-        scratch_shapes=[
-            pltpu.VMEM((rows, width), F32),
-            pltpu.VMEM((chip_width, half), F32),
-            pltpu.VMEM((chip_width, rows), F32),
-            pltpu.VMEM((chip_width, rows), F32),
-            pltpu.VMEM((chip_width, half), F32),
-        ],
+        in_specs=[smem()] + [vmem()] * (4 + len(units)),
+        out_specs=[pl.BlockSpec(s, lambda h: (0, 0)) for s in shapes],
+        out_shape=[jax.ShapeDtypeStruct(s, F32) for s in shapes],
+        scratch_shapes=[pltpu.VMEM((features, half), F32)],
         compiler_params=params(),
         cost_estimate=pl.CostEstimate(
-            flops=6 * 10**9, bytes_accessed=6 * 10**6, transcendentals=heads * rows * half
+            flops=16 * 10**9, bytes_accessed=6 * 10**6, transcendentals=heads * rows * half
         ),
         name="attention",
-    )(
-        place,
-        *[p for pair in slabs for p in pair],
-        gain[layer_index][None],
-        *w_qkv,
-        *w_out,
-    )
+    )(place, *projected, *units)
 
 
 def mlp_rows(values, gain_row, up, down):
     normed = split2(layer_norm(values, gain_row))
-    result = None
-    for w_up, w_down in zip(up, down):
-        hidden = dot3(normed, w_up)
-        hidden = split2(hidden * (0.5 + 0.5 * lax.erf(hidden * 0.5**0.5)))
-        term = dot3(hidden, w_down)
-        result = term if result is None else result + term
-    return result
-
-
-def mlp_kernel(cols, place, *refs):
-    pieces = refs[:cols]
-    gain, wu0, wu1, wd0, wd1, keep_ref = refs[cols : cols + 6]
-    send_refs = refs[cols + 6 : cols + 6 + cols - 1]
-    partial, residual = refs[cols + 6 + cols - 1 :]
-    col = place[0]
+    hidden = dot3(normed, up, (((1,), (1,)), ((), ())))
+    hidden = split2(hidden * (0.5 + 0.5 * lax.erf(hidden * 0.5**0.5)))
+    return dot3(hidden, down)
+
+
+def mlp_kernel(cols, reps, units, place, *refs):
+    pieces = refs[:reps]
+    gain = refs[reps]
+    unit_refs = refs[reps + 1 : reps + 1 + units]
+    outs = refs[reps + 1 + units : -1]
+    partial = refs[-1]
+    col, rep = place[0], place[1]
     part, width = pieces[0].shape
-    slab = width // cols
-    up = [split2(w[0]) for w in (wu0, wu1)]
-    down = [split2(w[0]) for w in (wd0, wd1)]
+    feature = width // (cols * reps)
+    up, down = (split2(jnp.concatenate([u[j] for u in unit_refs], axis=0)) for j in range(2))
+    for k in range(reps):
+        at = pl.multiple_of(lax.rem(rep + reps - k, reps) * part, 128)
+        values = pieces[k][...]
+        result = mlp_rows(values, gain[...], up, down)
+        partial[pl.ds(at, part), :] = result + values if k == 0 else result
+    aligned = feature % 128 == 0
     for k in range(cols):
-        at = pl.multiple_of(lax.rem(col + cols - k, cols) * part, 128)
-        values = pieces[k][...]
-        partial[pl.ds(at, part), :] = mlp_rows(values, gain[...], up, down)
-        residual[pl.ds(at, part), :] = values
-    for k in range(cols):
-        at = pl.multiple_of(lax.rem(col + k, cols) * slab, 128)
-        if k == 0:
-            keep_ref[...] = partial[:, pl.ds(at, slab)] + residual[:, pl.ds(at, slab)]
-        else:
-            send_refs[k - 1][...] = partial[:, pl.ds(at, slab)]
-
-
-def mlp(place, pieces, gain, w_up, w_down, layer_index):
-    cols = len(pieces)
+        for j in range(reps):
+            place_of = lax.rem(col + k, cols) * reps + lax.rem(rep + j, reps)
+            if aligned:
+                at = pl.multiple_of(place_of * feature, 128)
+                outs[k * reps + j][...] = partial[:, pl.ds(at, feature)]
+            else:
+                at = pl.multiple_of(lax.rem(col + k, cols) * reps * feature, 128)
+                slab = partial[:, pl.ds(at, reps * feature)]
+                low, high = slab[:, :feature], slab[:, feature:]
+                outs[k * reps + j][...] = jnp.where(lax.rem(rep + j, reps) == 0, low, high)
+
+
+def mlp(place, pieces, gain, units):
+    cols, reps = lax.axis_size("col"), len(pieces)
     part, width = pieces[0].shape
-    local = w_up[0].shape[-1]
-    rows = part * cols
-    slab = width // cols
-    fixed = lambda *block: pl.BlockSpec(
-        (1,) + block, lambda i: (layer_index,) + (0,) * len(block)
-    )
-    out_block = pl.BlockSpec((rows, slab), lambda i: (0, 0))
+    rows = part * reps
+    feature = width // (cols * reps)
+    hidden = sum(u.shape[1] for u in units)
     return pl.pallas_call(
-        functools.partial(mlp_kernel, cols),
-        grid=(1,),
-        in_specs=[smem()]
-        + [vmem()] * (cols + 1)
-        + [fixed(width, local)] * 2
-        + [fixed(local, width)] * 2,
-        out_specs=[out_block] * cols,
-        out_shape=[jax.ShapeDtypeStruct((rows, slab), F32)] * cols,
-        scratch_shapes=[pltpu.VMEM((rows, width), F32)] * 2,
+        functools.partial(mlp_kernel, cols, reps, len(units)),
+        in_specs=[smem()] + [vmem()] * (reps + 1 + len(units)),
+        out_specs=[vmem()] * (cols * reps),
+        out_shape=[jax.ShapeDtypeStruct((rows, feature), F32)] * (cols * reps),
+        scratch_shapes=[pltpu.VMEM((rows, width), F32)],
         compiler_params=params(),
         cost_estimate=pl.CostEstimate(
-            flops=4 * rows * width * 2 * local * 3, bytes_accessed=6 * 10**6, transcendentals=0
+            flops=4 * rows * width * hidden * 3, bytes_accessed=6 * 10**6, transcendentals=0
         ),
         name="mlp",
-    )(place, *pieces, gain[layer_index][None], *w_up, *w_down)
-
-
-def pooled_mlp_kernel(cols, place, *refs):
-    pieces = refs[:cols]
-    pillar, cells, gain, wu0, wu1, wd0, wd1 = refs[cols : cols + 7]
-    own_refs = refs[cols + 7 : 2 * cols + 7]
-    other_refs = refs[2 * cols + 7 :]
+    )(place, *pieces, gain, *units)
+
+
+def pooled_mlp_kernel(cols, units, place, *refs):
+    near, other, pillar, cells, gain = refs[:5]
+    unit_refs = refs[5 : 5 + units]
+    outs = refs[5 + units :]
     col, rep = place[0], place[1]
-    part = pieces[0].shape[0]
-    up = [split2(w[0]) for w in (wu0, wu1)]
-    down = [split2(w[0]) for w in (wd0, wd1)]
+    half = near.shape[0]
+    part = half // 2
+    up, down = (split2(jnp.concatenate([u[j] for u in unit_refs], axis=0)) for j in range(2))
     totals = [None] * (2 * cols)
-    for k in range(cols):
-        source = lax.rem(col + cols - k, cols)
-        at = pl.multiple_of(rep * part * cols + source * part, 128)
-        tokens_cells = pillar[:, pl.ds(at, part)]
-        values = pieces[k][...]
+    for k in range(2):
+        source = lax.rem(rep + k, 2) * part
+        tokens_cells = pillar[:, pl.ds(pl.multiple_of(col * half + source, 128), part)]
+        here = pl.ds(pl.multiple_of(source, 128), part)
+        values = near[here, :] + other[here, :]
         result = mlp_rows(values, gain[...], up, down)
         if k == 0:
             result = result + values
@@ -282,37 +285,27 @@
                 chosen, low, preferred_element_type=F32
             )
             totals[i] = term if totals[i] is None else totals[i] + term
-    for k in range(cols):
-        own_refs[k][...] = totals[2 * k]
-        other_refs[k][...] = totals[2 * k + 1]
-
-
-def pooled_mlp(place, pieces, pillar, cells, gain, w_up, w_down, layer_index):
-    cols = len(pieces)
-    part, width = pieces[0].shape
-    local = w_up[0].shape[-1]
-    rows = part * cols
+    for i in range(2 * cols):
+        outs[i][...] = totals[i]
+
+
+def pooled_mlp(place, near, other, pillar, cells, gain, units):
+    cols = lax.axis_size("col")
+    rows, width = near.shape
     count = cells.shape[1]
-    fixed = lambda *block: pl.BlockSpec(
-        (1,) + block, lambda i: (layer_index,) + (0,) * len(block)
-    )
-    out_block = pl.BlockSpec((count, width), lambda i: (0, 0))
+    hidden = sum(u.shape[1] for u in units)
     outs = pl.pallas_call(
-        functools.partial(pooled_mlp_kernel, cols),
-        grid=(1,),
-        in_specs=[smem()]
-        + [vmem()] * (cols + 3)
-        + [fixed(width, local)] * 2
-        + [fixed(local, width)] * 2,
-        out_specs=[out_block] * (2 * cols),
+        functools.partial(pooled_mlp_kernel, cols, len(units)),
+        in_specs=[smem()] + [vmem()] * (5 + len(units)),
+        out_specs=[vmem()] * (2 * cols),
         out_shape=[jax.ShapeDtypeStruct((count, width), F32)] * (2 * cols),
         compiler_params=params(),
         cost_estimate=pl.CostEstimate(
-            flops=4 * rows * width * 2 * local * 3, bytes_accessed=6 * 10**6, transcendentals=0
+            flops=4 * rows * width * hidden * 3, bytes_accessed=6 * 10**6, transcendentals=0
         ),
         name="mlp_pool",
-    )(place, *pieces, pillar, cells, gain[layer_index][None], *w_up, *w_down)
-    return outs[:cols], outs[cols:]
+    )(place, near, other, pillar, cells, gain, *units)
+    return outs[::2], outs[1::2]
 
 
 def pick_blocks_kernel(outs, counts, index, *refs):
@@ -471,39 +464,70 @@
     swap = shift_by(1, reps)
     place = jnp.stack([col, rep, tok, jnp.int32(TR * toks), jnp.int32(TC * cols)]).astype(jnp.int32)
     slabs = gather_slabs(tokens)
-    both = lambda w: (w, lax.ppermute(w, "rep", swap))
-    w_qkv, w_out, w_up, w_down = (both(w) for w in (w_qkv, w_out, w_up, w_down))
+    heads_unit = [
+        jnp.concatenate([jnp.swapaxes(w_qkv[l], 1, 2), w_out[l][None]], axis=0) for l in range(2)
+    ]
+    hidden_unit = [jnp.stack([w_up[l].T, w_down[l]], axis=0) for l in range(2)]
+
+    def far_units(unit, pieces, piece, after=None):
+        scenes = lax.axis_size("scene")
+        size = unit.shape[1] // (scenes * pieces)
+        start = (lax.axis_index("scene") * pieces + piece) * size
+        if after is not None:
+            start = start + jnp.minimum(jnp.abs(after[0, 0]), 0.0).astype(jnp.int32)
+        own = lax.dynamic_slice_in_dim(unit, start, size, 1)
+        found = []
+        for k in range(1, cols):
+            direct = lax.ppermute(own, "col", shift_by(k, cols))
+            found += [direct] + [
+                lax.ppermute(direct, "scene", shift_by(j, scenes)) for j in range(1, scenes)
+            ]
+        return found
+
     blocks_out, blocks_in = routes(dest_device, dest_slot)
     count = dest_device.shape[0]
-    each = count // reps
     tile_rows = TR // reps
     cells = tile_cells(tile_rows)
 
-    def attend(slabs, layer_index):
-        keep, *sends = attention(place, slabs, attn_gain, w_qkv, w_out, layer_index)
-        for k, part in enumerate(sends):
-            keep = keep + lax.ppermute(part, "col", shift_by(k + 1, cols))
-        return [keep] + [lax.ppermute(keep, "col", shift_by(k, cols)) for k in range(1, cols)]
-
-    pieces = attend(slabs, 0)
-    keep, *sends = mlp(place, pieces, mlp_gain, w_up, w_down, 0)
+    units = [heads_unit[0], lax.ppermute(heads_unit[0], "rep", swap)]
+    far_hidden = far_units(hidden_unit[0], 2, 0) + far_units(hidden_unit[0], 2, 1)
+    projected = project(place, slabs, attn_gain[:1], units, "rep")
+    keep, *sends = attention(place, projected, units, True)
     for k, part in enumerate(sends):
         keep = keep + lax.ppermute(part, "col", shift_by(k + 1, cols))
-    feature = keep.shape[1] // reps
-    low, high = keep[:, :feature], keep[:, feature:]
-    near = jnp.where(rep == 0, low, high)
-    far = lax.ppermute(jnp.where(rep == 0, high, low), "rep", swap)
-    in_blocks = lambda x: x.reshape(each, -1, feature)
-    index = jnp.where(blocks_out // each == rep, blocks_out % each, each + blocks_out % each)
+    far_heads = far_units(heads_unit[1], 1, 0, keep)
+    pieces = [keep, lax.ppermute(keep, "rep", swap)]
+    outs = mlp(place, pieces, mlp_gain[:1], [hidden_unit[0]] + far_hidden)
+    parts = [outs[k * reps] + lax.ppermute(outs[k * reps + 1], "rep", swap) for k in range(cols)]
+    gathered = [parts[0]] + [
+        lax.ppermute(parts[k], "col", shift_by(k, cols)) for k in range(1, cols)
+    ]
+    far_hidden = far_units(hidden_unit[1], 1, 0, gathered[-1])
+    feature = parts[0].shape[1]
+    each = count // (reps * cols)
+    of_rep, of_col = blocks_out // (each * cols), blocks_out // each % cols
+    index = ((col - of_col) % cols * reps + of_rep) * each + blocks_out % each
     capacity = index.shape[1]
-    outgoing = pick_blocks([in_blocks(near), in_blocks(far)], index.reshape(-1), toks, capacity)
+    outgoing = pick_blocks(
+        [g.reshape(reps * each, -1, feature) for g in gathered], index.reshape(-1), toks, capacity
+    )
     incoming = [outgoing[0]] + [
         lax.ppermute(outgoing[k], "tok", shift_by(k, toks)) for k in range(1, toks)
     ]
     (moved,) = pick_blocks(incoming, blocks_in, 1, count)
-    pieces = attend(gather_slabs(moved.reshape(-1, feature)), 1)
-
-    own, other = pooled_mlp(place, pieces, pillar[None], cells, mlp_gain, w_up, w_down, 1)
+
+    units = [heads_unit[1]] + far_heads
+    projected = project(place, gather_slabs(moved.reshape(-1, feature)), attn_gain[1:], units, "col")
+    (near,) = attention(place, projected, units, False)
+    own, other = pooled_mlp(
+        place,
+        near,
+        lax.ppermute(near, "rep", swap),
+        pillar[None],
+        cells,
+        mlp_gain[1:],
+        [hidden_unit[1]] + far_hidden,
+    )
     sums = [own[k] + lax.ppermute(other[k], "rep", swap) for k in range(cols)]
     tile = sums[0]
     for k in range(1, cols):

time: 217 us -> 220 us (1.014)
  waiting for transfers between devices: 95.3 us -> 75.4 us
  local copies, waits for them, and re-layouts: 9.44 us -> 19.2 us
  other arithmetic: 8.3 us -> 16.1 us
  Pallas kernels: 65.1 us -> 72 us
  starting transfers between devices: 37.8 us -> 35.2 us
    ppermute x9 -> x14, waiting for transfers between devices: 44.1 us -> 8.89 us  [the longest x4 7.48 us: far_units(): lax.ppermute(direct, 'scene', shift_by(j, scenes))]
    ppermute x2, waiting for transfers between devices: 23 us -> 35.7 us  [gather_slabs(): lax.ppermute(piece, 'col', shift_by(k, cols))]
    pallas_call x4 -> x6, Pallas kernels: 55.3 us -> 62.1 us  [the longest x2 33.5 us: attention(): pl.pallas_call(functools.partial(attention_kernel, parts, len(units), hea...]
    slice x2 -> x8, local copies, waits for them, and re-layouts: 1.93 us -> 7.62 us  [the longest x2 2.39 us: far_units(): start = start + jnp.minimum(jnp.abs(after[0, 0]), 0.0).astype(jnp.int32)]
    ppermute x1, waiting for transfers between devices: 4.93 us -> 10.1 us  [on_device(): keep = keep + lax.ppermute(part, 'col', shift_by(k + 1, cols))]
    another operation x0 -> x4, other arithmetic: none -> 4.31 us  [on_device(): hidden_unit = [jnp.stack([w_up[l].T, w_down[l]], axis=0) for l in range(2)]]
    unnamed x41 -> x51, local copies, waits for them, and re-layouts: 5.12 us -> 9.21 us
    ppermute x1, starting transfers between devices: 6.95 us -> 2.97 us  [on_device(): lax.ppermute(edge_rows, ('tok', 'rep'), pairs + [(b, a) for a, b in pairs])]
  transfers between devices with their start and end apart: 26 -> 31, of which waited for: 14 -> 10; matrix products, arithmetic and copies ran while one was open for 5% -> 13% of each run, Pallas kernels for 9% -> 22%
where the time goes in v2:
time: 220 us
  waiting for transfers between devices  75.4 us (34%)
  Pallas kernels  72 us (33%)
  starting transfers between devices  35.2 us (16%)
  local copies, waits for them, and re-layouts  19.2 us (9%)
  other arithmetic  16.1 us (7%)
    ppermute x2, waiting for transfers between devices, gather_slabs(): lax.ppermute(piece, 'col', shift_by(k, cols))  35.7 us
    pallas_call x2, Pallas kernels, attention(): pl.pallas_call(functools.partial(attention_kernel, parts, len(units), hea...  33.5 us
    pallas_call x2, Pallas kernels, project(): pl.pallas_call(functools.partial(qkv_kernel, cols, len(units), halves), i...  12.3 us
    ppermute x1, waiting for transfers between devices, on_device(): tile = tile + lax.ppermute(sums[k], 'col', shift_by(k, cols))  10.7 us
    ppermute x1, waiting for transfers between devices, on_device(): keep = keep + lax.ppermute(part, 'col', shift_by(k + 1, cols))  10.1 us
    unnamed x51, local copies, waits for them, and re-layouts  9.21 us
    pallas_call x1, Pallas kernels, pooled_mlp(): pl.pallas_call(functools.partial(pooled_mlp_kernel, cols, len(units)), in...  8.93 us
    ppermute x4, waiting for transfers between devices, far_units(): lax.ppermute(direct, 'scene', shift_by(j, scenes))  7.48 us
  transfers between devices with their start and end apart: 31, of which 10 were waited for; matrix products, arithmetic and copies ran while one was open for 13% of the time, Pallas kernels for 22%

profile of v2, /device:TPU:1, one launch (start us, length us, event | category | flops | bytes accessed | tf_op | source)
XLA Modules:
  0.0 219.6 jit_solution(7699890319138707168)
XLA Ops:
  0.1 2.7 %collective-permute-start.4 = (f32[1024,128]{1,0:T(8,128)}, f32[1024,128]{1,0:T(8,128)}, u32[]{:S(2)}, u32[]{:S(2)}) collective-permute-start(f32[1024,128]{1,0:T(8,128)} %refs_0_.1), channel_id=1, source_target_pairs={{0,2},{2,0},{1,3},{3,1},{4,6},{6,4},{5,7},{7,5},{8,10},{10,8},{9,1... | collective-permute-start | bytes 1572872 | tf_op jit(solution)/shard_map/ppermute | solution.py:67
  2.7 2.4 %fusion.16 = (f32[1,3,512,128]{3,2,1,0:T(8,128)}, f32[1,3,512,128]{3,2,1,0:T(8,128)S(1)}) fusion(f32[2,3,512,128]{3,2,1,0:T(8,128)} %param.14), kind=kLoop, calls=%fused_computation.75 | loop fusion | bytes 3145728 | tf_op jit(solution)/shard_map/slice | solution.py:468
  5.4 1.1 pad_maximum_fusion.3.refs_5_.refs_4_
  7.5 7.7 %collective-permute-done.4.refs_2_ = f32[1024,128]{1,0:T(8,128)} collective-permute-done((f32[1024,128]{1,0:T(8,128)}, f32[1024,128]{1,0:T(8,128)}, u32[]{:S(2)}, u32[]{:S(2)}) %collective-permute-start.4) | collective-permute-done | bytes 524320 | tf_op jit(solution)/shard_map/ppermute | solution.py:67
  15.9 1.5 fusion.14
  17.4 1.6 copy.48
  19.0 1.1 fusion.3
  20.1 1.5 collective-permute-start.9
  23.0 6.1 %project.2 = (f32[256,512]{1,0:T(8,128)}, f32[256,1024]{1,0:T(8,128)}, f32[256,1024]{1,0:T(8,128)}, f32[512,512]{1,0:T(8,128)}) custom-call(s32[5]{0:T(128)} %stack.46.place, f32[1024,128]{1,0:T(8,128)} %refs_0_.1, f32[1024,128]{1,0:T(8,128)} %collective-permute-done.3.refs_1_, f32[1024,128]{1,0:T(8,128)} %collective-permute-done.4.refs_2_, ...), custom_call_target="tpu_custom_call" | custom-call | flops 2415919104 | bytes 8000000 | tf_op jit(solution)/shard_map/project/pallas_call | solution.py:109
  29.2 16.8 %attention.2 = (f32[256,512]{1,0:T(8,128)}, f32[256,512]{1,0:T(8,128)}) custom-call(s32[5]{0:T(128)} %stack.46.place, f32[256,512]{1,0:T(8,128)} %get-tuple-element.27.refs_0_, f32[256,1024]{1,0:T(8,128)} %get-tuple-element.28.refs_1_, f32[256,1024]{1,0:T(8,128)} %get-tuple-element.29.refs_2_, f32[512,512]{1,0:T(8,128)} %get-tuple-element.30.refs_3_, ...), custom_call_target="tpu_custom_call" | custom-call | flops 16000000000 | bytes 6000000 | tf_op jit(solution)/shard_map/attention/pallas_call | solution.py:193
  45.9 1.5 collective-permute-start.7
  47.5 1.2 collective-permute-start.10
  49.0 10.1 %collective-permute-done.7 = f32[256,512]{1,0:T(8,128)S(1)} collective-permute-done((f32[256,512]{1,0:T(8,128)}, f32[256,512]{1,0:T(8,128)S(1)}, u32[]{:S(2)}, u32[]{:S(2)}) %collective-permute-start.7) | collective-permute-done | bytes 524320 | tf_op jit(solution)/shard_map/ppermute | solution.py:497
  59.1 1.1 add.295.refs_0_
  60.2 1.5 collective-permute-start.8
  62.0 1.5 pad_maximum_fusion.refs_3_
  64.1 7.5 %collective-permute-done.12.refs_7_ = f32[2,128,512]{2,1,0:T(8,128)S(1)} collective-permute-done((f32[2,128,512]{2,1,0:T(8,128)}, f32[2,128,512]{2,1,0:T(8,128)S(1)}, u32[]{:S(2)}, u32[]{:S(2)}) %collective-permute-start.12) | collective-permute-done | bytes 524320 | tf_op jit(solution)/shard_map/ppermute | solution.py:483
  72.5 7.3 %mlp.1 = (f32[512,128]{1,0:T(8,128)}, f32[512,128]{1,0:T(8,128)}, f32[512,128]{1,0:T(8,128)}, f32[512,128]{1,0:T(8,128)}) custom-call(s32[5]{0:T(128)} %stack.46.place, f32[256,512]{1,0:T(8,128)} %copy-done.4, f32[256,512]{1,0:T(8,128)} %copy-done.19, f32[1,512]{1,0:T(1,128)} %get-tuple-element.65.refs_2_, f32[2,512,512]{2,1,0:T(8,128)} %pad_maximum_fusion.refs_3_, ...), custom_call_target="tpu_custom_call" | custom-call | flops 3221225472 | bytes 6000000 | tf_op jit(solution)/shard_map/mlp/pallas_call | solution.py:250
  79.9 1.7 collective-permute-start.14
  81.8 3.6 %collective-permute-start.2 = (s32[5]{0:T(128)S(1)}, s32[5]{0:T(128)S(1)}, u32[]{:S(2)}, u32[]{:S(2)}) collective-permute-start(s32[5]{0:T(128)S(1)} %get-tuple-element.50), channel_id=1, source_target_pairs={{0,12},{4,0},{8,4},{12,8},{1,13},{5,1},{9,5},{13,9},{2,14},{6,2},{... | collective-permute-start | bytes 68 | tf_op jit(solution)/shard_map/ppermute | solution.py:357
  87.5 1.7 add.300
  89.7 1.6 copy.50
  92.6 1.2 slice.80
  94.5 1.7 add.299
  96.2 1.3 collective-permute-done.15
  97.5 1.9 pick_blocks.2
  99.4 2.2 %collective-permute-start.16 = (f32[5,64,128]{2,1,0:T(8,128)}, f32[5,64,128]{2,1,0:T(8,128)S(1)}, u32[]{:S(2)}, u32[]{:S(2)}) collective-permute-start(f32[5,64,128]{2,1,0:T(8,128)} %get-tuple-element.38), channel_id=1, source_target_pairs={{0,4},{4,8},{8,12},{12,0},{1,5},{5,9},{9,13},{13,1},{2,6},{6,10},{... | collective-permute-start | bytes 491528 | tf_op jit(solution)/shard_map/ppermute | solution.py:515
  102.2 1.5 collective-permute-start.18
  104.8 1.2 slice.81
  106.8 1.3 collective-permute-start.25
  108.1 6.5 %collective-permute-done.17.refs_2_ = f32[5,64,128]{2,1,0:T(8,128)S(1)} collective-permute-done((f32[5,64,128]{2,1,0:T(8,128)}, f32[5,64,128]{2,1,0:T(8,128)S(1)}, u32[]{:S(2)}, u32[]{:S(2)}) %collective-permute-start.17) | collective-permute-done | bytes 163872 | tf_op jit(solution)/shard_map/ppermute | solution.py:515
  115.2 2.0 pick_blocks.3
  117.5 1.2 collective-permute-start.23
  118.8 3.8 %collective-permute-start.19 = (f32[1024,128]{1,0:T(8,128)}, f32[1024,128]{1,0:T(8,128)S(1)}, u32[]{:S(2)}, u32[]{:S(2)}) collective-permute-start(f32[1024,128]{1,0:T(8,128)} %bitcast.39), channel_id=1, source_target_pairs={{0,1},{1,0},{2,3},{3,2},{4,5},{5,4},{6,7},{7,6},{8,9},{9,8},{10,11... | collective-permute-start | bytes 1572872 | tf_op jit(solution)/shard_map/ppermute | solution.py:68
  122.6 28.0 %collective-permute-done.20.refs_2_ = f32[1024,128]{1,0:T(8,128)S(1)} collective-permute-done((f32[1024,128]{1,0:T(8,128)}, f32[1024,128]{1,0:T(8,128)S(1)}, u32[]{:S(2)}, u32[]{:S(2)}) %collective-permute-start.20) | collective-permute-done | bytes 524320 | tf_op jit(solution)/shard_map/ppermute | solution.py:67
  150.6 2.3 %collective-permute-start.21 = (f32[1024,128]{1,0:T(8,128)S(1)}, f32[1024,128]{1,0:T(8,128)S(1)}, u32[]{:S(2)}, u32[]{:S(2)}) collective-permute-start(f32[1024,128]{1,0:T(8,128)S(1)} %collective-permute-done.20.refs_2_), channel_id=1, source_target_pairs={{0,1},{1,0},{2,3},{3,2},{4,5},{5,4},{6,7},{7,6},{8,9},{9,8},{10,11... | collective-permute-start | bytes 1572872 | tf_op jit(solution)/shard_map/ppermute | solution.py:68
  152.8 1.1 pad_maximum_fusion.2.refs_5_.refs_4_
  153.9 1.3 collective-permute-start.26
  156.4 6.2 %project.3 = (f32[256,512]{1,0:T(8,128)}, f32[256,1024]{1,0:T(8,128)}, f32[256,1024]{1,0:T(8,128)}, f32[512,512]{1,0:T(8,128)}) custom-call(s32[5]{0:T(128)} %stack.46.place, f32[1024,128]{1,0:T(8,128)} %bitcast.40, f32[1024,128]{1,0:T(8,128)} %copy-done.18, f32[1024,128]{1,0:T(8,128)} %copy-done.15, f32[1024,128]{1,0:T(8,128)} %copy-done.20, ...), custom_call_target="tpu_custom_call" | custom-call | flops 2415919104 | bytes 8000000 | tf_op jit(solution)/shard_map/project/pallas_call | solution.py:109
  162.6 16.7 %attention.3.refs_0_ = f32[512,512]{1,0:T(8,128)} custom-call(s32[5]{0:T(128)} %stack.46.place, f32[256,512]{1,0:T(8,128)} %get-tuple-element.41.refs_0_, f32[256,1024]{1,0:T(8,128)} %get-tuple-element.42.refs_1_, f32[256,1024]{1,0:T(8,128)} %get-tuple-element.43.refs_2_, f32[512,512]{1,0:T(8,128)} %get-tuple-element.44.refs_3_, ...), custom_call_target="tpu_custom_call" | custom-call | flops 16000000000 | bytes 6000000 | tf_op jit(solution)/shard_map/attention/pallas_call | solution.py:193
  180.7 1.5 pad_maximum_fusion.1.refs_5_
  183.2 8.9 %mlp_pool.1 = (f32[200,512]{1,0:T(8,128)}, f32[200,512]{1,0:T(8,128)}, f32[200,512]{1,0:T(8,128)}, f32[200,512]{1,0:T(8,128)}) custom-call(s32[5]{0:T(128)} %stack.46.place, f32[512,512]{1,0:T(8,128)} %attention.3.refs_0_, f32[512,512]{1,0:T(8,128)} %collective-permute-done.24.refs_1_, s32[1,1024]{1,0:T(1,128)} %bitcast.44, s32[4,200,1]{2,1,0:T(8,128)} %copy.45.refs_3_, ...), custom_call_target="tpu_custom_call" | custom-call | flops 3221225472 | bytes 6000000 | tf_op jit(solution)/shard_map/mlp_pool/pallas_call | solution.py:297
  192.7 1.4 collective-permute-done.28
  195.5 10.7 %collective-permute-done.29 = f32[200,512]{1,0:T(8,128)S(1)} collective-permute-done((f32[200,512]{1,0:T(8,128)S(1)}, f32[200,512]{1,0:T(8,128)S(1)}, u32[]{:S(2)}, u32[]{:S(2)}) %collective-permute-start.29) | collective-permute-done | bytes 409632 | tf_op jit(solution)/shard_map/ppermute | solution.py:534
  206.1 1.1 add_add_fusion.tile
  207.3 3.0 %collective-permute-start.30 = (f32[40,512]{1,0:T(8,128)S(1)}, f32[40,512]{1,0:T(8,128)S(1)}, u32[]{:S(2)}, u32[]{:S(2)}) collective-permute-start(f32[40,512]{1,0:T(8,128)S(1)} %slice_select_fusion), channel_id=1, source_target_pairs={{1,4},{5,8},{9,12},{4,1},{8,5},{12,9},{3,6},{7,10},{11,14},{6,3},{... | collective-permute-start | bytes 245768 | tf_op jit(solution)/shard_map/ppermute | solution.py:538
  210.9 2.2 collective-permute-done.30.halo
  213.7 5.9 %raster.1 = f32[8,16,512]{2,1,0:T(8,128)} custom-call(s32[5]{0:T(128)} %stack.46.place, f32[200,512]{1,0:T(8,128)} %copy-done.1, f32[40,512]{1,0:T(8,128)} %copy-done.9, f32[2,3,3,512]{3,2,1,0:T(4,128)} %copy.46.depth, f32[2,512,1024]{2,1,0:T(8,128)} %point.1, f32[2,512]{1,0:T(2,128)} %gain.1), custom_call_target="tpu_custom_call" | custom-call | tf_op jit(solution)/shard_map/raster/pallas_call | solution.py:417
  (118 shorter events, 19.3 us)
Async XLA Ops:
  0.0 5.1 %copy-start.5 = (f32[2,128,512]{2,1,0:T(8,128)S(1)}, f32[2,128,512]{2,1,0:T(8,128)}, u32[]{:S(2)}) copy-start(f32[2,128,512]{2,1,0:T(8,128)} %param.15) | copy-start | bytes 1572868
  0.0 23.0 %collective-permute-start.3 = (f32[1024,128]{1,0:T(8,128)}, f32[1024,128]{1,0:T(8,128)}, u32[]{:S(2)}, u32[]{:S(2)}) collective-permute-start(f32[1024,128]{1,0:T(8,128)} %refs_0_.1), channel_id=1, source_target_pairs={{0,1},{1,0},{2,3},{3,2},{4,5},{5,4},{6,7},{7,6},{8,9},{9,8},{10,11... | collective-permute-start | bytes 1572872 | tf_op jit(solution)/shard_map/ppermute | solution.py:68
  0.1 15.2 %collective-permute-start.4 = (f32[1024,128]{1,0:T(8,128)}, f32[1024,128]{1,0:T(8,128)}, u32[]{:S(2)}, u32[]{:S(2)}) collective-permute-start(f32[1024,128]{1,0:T(8,128)} %refs_0_.1), channel_id=1, source_target_pairs={{0,2},{2,0},{1,3},{3,1},{4,6},{6,4},{5,7},{7,5},{8,10},{10,8},{9,1... | collective-permute-start | bytes 1572872 | tf_op jit(solution)/shard_map/ppermute | solution.py:67
  5.4 2.0 copy-start.2
  6.5 9.4 %copy-start.3 = (f32[2,512,512]{2,1,0:T(8,128)S(1)}, f32[2,512,512]{2,1,0:T(8,128)}, u32[]{:S(2)}) copy-start(f32[2,512,512]{2,1,0:T(8,128)} %param.16) | copy-start | bytes 6291460
  6.5 16.5 %collective-permute-start.6 = (f32[4,128,512]{2,1,0:T(8,128)}, f32[4,128,512]{2,1,0:T(8,128)}, u32[]{:S(2)}, u32[]{:S(2)}) collective-permute-start(f32[4,128,512]{2,1,0:T(8,128)} %pad_maximum_fusion.3.refs_5_.refs_4_), channel_id=1, source_target_pairs={{0,1},{1,0},{2,3},{3,2},{4,5},{5,4},{6,7},{7,6},{8,9},{9,8},{10,11... | collective-permute-start | bytes 3145736 | tf_op jit(solution)/shard_map/ppermute | solution.py:492
  15.3 7.8 %collective-permute-start.5 = (f32[1024,128]{1,0:T(8,128)}, f32[1024,128]{1,0:T(8,128)}, u32[]{:S(2)}, u32[]{:S(2)}) collective-permute-start(f32[1024,128]{1,0:T(8,128)} %collective-permute-done.4.refs_2_), channel_id=1, source_target_pairs={{0,1},{1,0},{2,3},{3,2},{4,5},{5,4},{6,7},{7,6},{8,9},{9,8},{10,11... | collective-permute-start | bytes 1572872 | tf_op jit(solution)/shard_map/ppermute | solution.py:68
  19.0 3.3 %copy-start.21 = (s32[16]{0:T(128)S(1)}, s32[16]{0:T(128)}, u32[]{:S(2)}) copy-start(s32[16]{0:T(128)} %param.20) | copy-start | bytes 196
  19.0 3.4 %copy-start.11 = (f32[2,512]{1,0:T(2,128)S(1)}, f32[2,512]{1,0:T(2,128)}, u32[]{:S(2)}) copy-start(f32[2,512]{1,0:T(2,128)} %param.18) | copy-start | bytes 12292
  20.1 27.4 %collective-permute-start.9 = (f32[2,128,512]{2,1,0:T(8,128)}, f32[2,128,512]{2,1,0:T(8,128)}, u32[]{:S(2)}, u32[]{:S(2)}) collective-permute-start(f32[2,128,512]{2,1,0:T(8,128)} %get-tuple-element.59), channel_id=1, source_target_pairs={{0,2},{2,0},{1,3},{3,1},{4,6},{6,4},{5,7},{7,5},{8,10},{10,8},{9,1... | collective-permute-start | bytes 1572872 | tf_op jit(solution)/shard_map/ppermute | solution.py:481
  21.6 27.1 %collective-permute-start.11 = (f32[2,128,512]{2,1,0:T(8,128)}, f32[2,128,512]{2,1,0:T(8,128)}, u32[]{:S(2)}, u32[]{:S(2)}) collective-permute-start(f32[2,128,512]{2,1,0:T(8,128)} %get-tuple-element.58), channel_id=1, source_target_pairs={{0,2},{2,0},{1,3},{3,1},{4,6},{6,4},{5,7},{7,5},{8,10},{10,8},{9,1... | collective-permute-start | bytes 1572872 | tf_op jit(solution)/shard_map/ppermute | solution.py:481
  29.2 32.5 %copy-start.22 = (s32[16]{0:T(128)S(1)}, s32[16]{0:T(128)}, u32[]{:S(2)}) copy-start(s32[16]{0:T(128)} %param.21) | copy-start | bytes 196
  45.9 13.1 %collective-permute-start.7 = (f32[256,512]{1,0:T(8,128)}, f32[256,512]{1,0:T(8,128)S(1)}, u32[]{:S(2)}, u32[]{:S(2)}) collective-permute-start(f32[256,512]{1,0:T(8,128)} %get-tuple-element.32), channel_id=1, source_target_pairs={{0,2},{2,0},{1,3},{3,1},{4,6},{6,4},{5,7},{7,5},{8,10},{10,8},{9,1... | collective-permute-start | bytes 1572872 | tf_op jit(solution)/shard_map/ppermute | solution.py:497
  47.5 16.6 %collective-permute-start.10 = (f32[2,128,512]{2,1,0:T(8,128)}, f32[2,128,512]{2,1,0:T(8,128)S(1)}, u32[]{:S(2)}, u32[]{:S(2)}) collective-permute-start(f32[2,128,512]{2,1,0:T(8,128)} %collective-permute-done.9.refs_4_), channel_id=1, source_target_pairs={{0,16},{16,0},{1,17},{17,1},{2,18},{18,2},{3,19},{19,3},{4,20},{20... | collective-permute-start | bytes 1572872 | tf_op jit(solution)/shard_map/ppermute | solution.py:483
  48.7 22.8 %collective-permute-start.12 = (f32[2,128,512]{2,1,0:T(8,128)}, f32[2,128,512]{2,1,0:T(8,128)S(1)}, u32[]{:S(2)}, u32[]{:S(2)}) collective-permute-start(f32[2,128,512]{2,1,0:T(8,128)} %collective-permute-done.11.refs_6_), channel_id=1, source_target_pairs={{0,16},{16,0},{1,17},{17,1},{2,18},{18,2},{3,19},{19,3},{4,20},{20... | collective-permute-start | bytes 1572872 | tf_op jit(solution)/shard_map/ppermute | solution.py:483
  60.2 3.3 %copy-start.4 = (f32[256,512]{1,0:T(8,128)}, f32[256,512]{1,0:T(8,128)S(1)}, u32[]{:S(2)}) copy-start(f32[256,512]{1,0:T(8,128)S(1)} %add.295.refs_0_) | copy-start | bytes 1572868
  60.2 11.3 %collective-permute-start.8 = (f32[256,512]{1,0:T(8,128)S(1)}, f32[256,512]{1,0:T(8,128)S(1)}, u32[]{:S(2)}, u32[]{:S(2)}) collective-permute-start(f32[256,512]{1,0:T(8,128)S(1)} %add.295.refs_0_), channel_id=1, source_target_pairs={{0,1},{1,0},{2,3},{3,2},{4,5},{5,4},{6,7},{7,6},{8,9},{9,8},{10,11... | collective-permute-start | bytes 1572872 | tf_op jit(solution)/shard_map/ppermute | solution.py:499
  62.0 1.5 copy-start.12
  64.1 7.5 %copy-start.14 = (f32[2,128,512]{2,1,0:T(8,128)}, f32[2,128,512]{2,1,0:T(8,128)S(1)}, u32[]{:S(2)}) copy-start(f32[2,128,512]{2,1,0:T(8,128)S(1)} %collective-permute-done.10.refs_5_) | copy-start | bytes 1572868
  72.5 16.9 %copy-start = (f32[1,3,512,128]{3,2,1,0:T(8,128)S(1)}, f32[1,3,512,128]{3,2,1,0:T(8,128)}, u32[]{:S(2)}) copy-start(f32[1,3,512,128]{3,2,1,0:T(8,128)} %get-tuple-element.60) | copy-start | bytes 2359300
  79.9 7.6 %collective-permute-start.14 = (f32[512,128]{1,0:T(8,128)}, f32[512,128]{1,0:T(8,128)S(1)}, u32[]{:S(2)}, u32[]{:S(2)}) collective-permute-start(f32[512,128]{1,0:T(8,128)} %get-tuple-element.36), channel_id=1, source_target_pairs={{0,1},{1,0},{2,3},{3,2},{4,5},{5,4},{6,7},{7,6},{8,9},{9,8},{10,11... | collective-permute-start | bytes 786440 | tf_op jit(solution)/shard_map/ppermute | solution.py:501
  81.8 9.5 %collective-permute-start.2 = (s32[5]{0:T(128)S(1)}, s32[5]{0:T(128)S(1)}, u32[]{:S(2)}, u32[]{:S(2)}) collective-permute-start(s32[5]{0:T(128)S(1)} %get-tuple-element.50), channel_id=1, source_target_pairs={{0,12},{4,0},{8,4},{12,8},{1,13},{5,1},{9,5},{13,9},{2,14},{6,2},{... | collective-permute-start | bytes 68 | tf_op jit(solution)/shard_map/ppermute | solution.py:357
  85.4 6.0 %collective-permute-start.1 = (s32[5]{0:T(128)S(1)}, s32[5]{0:T(128)S(1)}, u32[]{:S(2)}, u32[]{:S(2)}) collective-permute-start(s32[5]{0:T(128)S(1)} %get-tuple-element.51), channel_id=1, source_target_pairs={{0,8},{4,12},{8,0},{12,4},{1,9},{5,13},{9,1},{13,5},{2,10},{6,14},... | collective-permute-start | bytes 68 | tf_op jit(solution)/shard_map/ppermute | solution.py:357
  85.4 6.1 %collective-permute-start = (s32[5]{0:T(128)S(1)}, s32[5]{0:T(128)S(1)}, u32[]{:S(2)}, u32[]{:S(2)}) collective-permute-start(s32[5]{0:T(128)S(1)} %get-tuple-element.49), channel_id=1, source_target_pairs={{0,4},{4,8},{8,12},{12,0},{1,5},{5,9},{9,13},{13,1},{2,6},{6,10},{... | collective-permute-start | bytes 68 | tf_op jit(solution)/shard_map/ppermute | solution.py:357
  86.6 7.8 %collective-permute-start.13 = (f32[512,128]{1,0:T(8,128)}, f32[512,128]{1,0:T(8,128)}, u32[]{:S(2)}, u32[]{:S(2)}) collective-permute-start(f32[512,128]{1,0:T(8,128)} %get-tuple-element.34), channel_id=1, source_target_pairs={{0,1},{1,0},{2,3},{3,2},{4,5},{5,4},{6,7},{7,6},{8,9},{9,8},{10,11... | collective-permute-start | bytes 786440 | tf_op jit(solution)/shard_map/ppermute | solution.py:501
  87.5 7.0 %copy-start.6 = (f32[512,128]{1,0:T(8,128)S(1)}, f32[512,128]{1,0:T(8,128)}, u32[]{:S(2)}) copy-start(f32[512,128]{1,0:T(8,128)} %get-tuple-element.33) | copy-start | bytes 786436
  89.2 8.3 %collective-permute-start.15 = (f32[512,128]{1,0:T(8,128)}, f32[512,128]{1,0:T(8,128)}, u32[]{:S(2)}, u32[]{:S(2)}) collective-permute-start(f32[512,128]{1,0:T(8,128)} %add.300), channel_id=1, source_target_pairs={{0,2},{2,0},{1,3},{3,1},{4,6},{6,4},{5,7},{7,5},{8,10},{10,8},{9,1... | collective-permute-start | bytes 786440 | tf_op jit(solution)/shard_map/ppermute | solution.py:503
  99.4 8.7 %collective-permute-start.16 = (f32[5,64,128]{2,1,0:T(8,128)}, f32[5,64,128]{2,1,0:T(8,128)S(1)}, u32[]{:S(2)}, u32[]{:S(2)}) collective-permute-start(f32[5,64,128]{2,1,0:T(8,128)} %get-tuple-element.38), channel_id=1, source_target_pairs={{0,4},{4,8},{8,12},{12,0},{1,5},{5,9},{9,13},{13,1},{2,6},{6,10},{... | collective-permute-start | bytes 491528 | tf_op jit(solution)/shard_map/ppermute | solution.py:515
  101.6 13.0 %collective-permute-start.17 = (f32[5,64,128]{2,1,0:T(8,128)}, f32[5,64,128]{2,1,0:T(8,128)S(1)}, u32[]{:S(2)}, u32[]{:S(2)}) collective-permute-start(f32[5,64,128]{2,1,0:T(8,128)} %get-tuple-element.39), channel_id=1, source_target_pairs={{0,8},{4,12},{8,0},{12,4},{1,9},{5,13},{9,1},{13,5},{2,10},{6,14},... | collective-permute-start | bytes 491528 | tf_op jit(solution)/shard_map/ppermute | solution.py:515
  102.2 12.3 %collective-permute-start.18 = (f32[5,64,128]{2,1,0:T(8,128)}, f32[5,64,128]{2,1,0:T(8,128)}, u32[]{:S(2)}, u32[]{:S(2)}) collective-permute-start(f32[5,64,128]{2,1,0:T(8,128)} %get-tuple-element.40), channel_id=1, source_target_pairs={{0,12},{4,0},{8,4},{12,8},{1,13},{5,1},{9,5},{13,9},{2,14},{6,2},{... | collective-permute-start | bytes 491528 | tf_op jit(solution)/shard_map/ppermute | solution.py:515
  104.6 13.0 %collective-permute-start.22 = (f32[4,64,512]{2,1,0:T(8,128)}, f32[4,64,512]{2,1,0:T(8,128)}, u32[]{:S(2)}, u32[]{:S(2)}) collective-permute-start(f32[4,64,512]{2,1,0:T(8,128)} %fusion.1), channel_id=1, source_target_pairs={{0,2},{2,0},{1,3},{3,1},{4,6},{6,4},{5,7},{7,5},{8,10},{10,8},{9,1... | collective-permute-start | bytes 1572872 | tf_op jit(solution)/shard_map/ppermute | solution.py:481
  106.8 47.1 %collective-permute-start.25 = (f32[2,256,512]{2,1,0:T(8,128)S(1)}, f32[2,256,512]{2,1,0:T(8,128)}, u32[]{:S(2)}, u32[]{:S(2)}) collective-permute-start(f32[2,256,512]{2,1,0:T(8,128)S(1)} %fusion), channel_id=1, source_target_pairs={{0,2},{2,0},{1,3},{3,1},{4,6},{6,4},{5,7},{7,5},{8,10},{10,8},{9,1... | collective-permute-start | bytes 3145736 | tf_op jit(solution)/shard_map/ppermute | solution.py:481
  108.1 6.5 %copy-start.7 = (f32[5,64,128]{2,1,0:T(8,128)}, f32[5,64,128]{2,1,0:T(8,128)S(1)}, u32[]{:S(2)}) copy-start(f32[5,64,128]{2,1,0:T(8,128)S(1)} %collective-permute-done.16.refs_1_) | copy-start | bytes 491524
  117.3 33.3 %collective-permute-start.20 = (f32[1024,128]{1,0:T(8,128)}, f32[1024,128]{1,0:T(8,128)S(1)}, u32[]{:S(2)}, u32[]{:S(2)}) collective-permute-start(f32[1024,128]{1,0:T(8,128)} %bitcast.38), channel_id=1, source_target_pairs={{0,2},{2,0},{1,3},{3,1},{4,6},{6,4},{5,7},{7,5},{8,10},{10,8},{9,1... | collective-permute-start | bytes 1572872 | tf_op jit(solution)/shard_map/ppermute | solution.py:67
  117.5 37.7 %collective-permute-start.23 = (f32[4,64,512]{2,1,0:T(8,128)}, f32[4,64,512]{2,1,0:T(8,128)S(1)}, u32[]{:S(2)}, u32[]{:S(2)}) collective-permute-start(f32[4,64,512]{2,1,0:T(8,128)} %collective-permute-done.22.refs_6_.refs_5_), channel_id=1, source_target_pairs={{0,16},{16,0},{1,17},{17,1},{2,18},{18,2},{3,19},{19,3},{4,20},{20... | collective-permute-start | bytes 1572872 | tf_op jit(solution)/shard_map/ppermute | solution.py:483
  118.8 36.4 %collective-permute-start.19 = (f32[1024,128]{1,0:T(8,128)}, f32[1024,128]{1,0:T(8,128)S(1)}, u32[]{:S(2)}, u32[]{:S(2)}) collective-permute-start(f32[1024,128]{1,0:T(8,128)} %bitcast.39), channel_id=1, source_target_pairs={{0,1},{1,0},{2,3},{3,2},{4,5},{5,4},{6,7},{7,6},{8,9},{9,8},{10,11... | collective-permute-start | bytes 1572872 | tf_op jit(solution)/shard_map/ppermute | solution.py:68
  150.6 4.7 %copy-start.15 = (f32[1024,128]{1,0:T(8,128)}, f32[1024,128]{1,0:T(8,128)S(1)}, u32[]{:S(2)}) copy-start(f32[1024,128]{1,0:T(8,128)S(1)} %collective-permute-done.20.refs_2_) | copy-start | bytes 1572868
  150.6 4.6 %collective-permute-start.21 = (f32[1024,128]{1,0:T(8,128)S(1)}, f32[1024,128]{1,0:T(8,128)S(1)}, u32[]{:S(2)}, u32[]{:S(2)}) collective-permute-start(f32[1024,128]{1,0:T(8,128)S(1)} %collective-permute-done.20.refs_2_), channel_id=1, source_target_pairs={{0,1},{1,0},{2,3},{3,2},{4,5},{5,4},{6,7},{7,6},{8,9},{9,8},{10,11... | collective-permute-start | bytes 1572872 | tf_op jit(solution)/shard_map/ppermute | solution.py:68
  153.9 28.3 %collective-permute-start.26 = (f32[2,256,512]{2,1,0:T(8,128)}, f32[2,256,512]{2,1,0:T(8,128)S(1)}, u32[]{:S(2)}, u32[]{:S(2)}) collective-permute-start(f32[2,256,512]{2,1,0:T(8,128)} %collective-permute-done.25.refs_6_), channel_id=1, source_target_pairs={{0,16},{16,0},{1,17},{17,1},{2,18},{18,2},{3,19},{19,3},{4,20},{20... | collective-permute-start | bytes 3145736 | tf_op jit(solution)/shard_map/ppermute | solution.py:483
  155.2 1.0 copy-start.18
  155.2 1.2 copy-start.20
  179.3 3.0 %collective-permute-start.24 = (f32[512,512]{1,0:T(8,128)}, f32[512,512]{1,0:T(8,128)}, u32[]{:S(2)}, u32[]{:S(2)}) collective-permute-start(f32[512,512]{1,0:T(8,128)} %attention.3.refs_0_), channel_id=1, source_target_pairs={{0,1},{1,0},{2,3},{3,2},{4,5},{5,4},{6,7},{7,6},{8,9},{9,8},{10,11... | collective-permute-start | bytes 3145736 | tf_op jit(solution)/shard_map/ppermute | solution.py:525
  192.1 18.1 %copy-start.10 = (f32[2,3,3,512]{3,0,2,1:T(2,128)S(1)}, f32[2,3,3,512]{3,0,2,1:T(2,128)}, u32[]{:S(2)}) copy-start(f32[2,3,3,512]{3,0,2,1:T(2,128)} %param.23) | copy-start | bytes 110596
  192.1 2.0 collective-permute-start.28
  192.3 3.2 %collective-permute-start.27 = (f32[200,512]{1,0:T(8,128)}, f32[200,512]{1,0:T(8,128)S(1)}, u32[]{:S(2)}, u32[]{:S(2)}) collective-permute-start(f32[200,512]{1,0:T(8,128)} %get-tuple-element.46), channel_id=1, source_target_pairs={{0,1},{1,0},{2,3},{3,2},{4,5},{5,4},{6,7},{7,6},{8,9},{9,8},{10,11... | collective-permute-start | bytes 1228808 | tf_op jit(solution)/shard_map/ppermute | solution.py:531
  195.2 11.0 %collective-permute-start.29 = (f32[200,512]{1,0:T(8,128)S(1)}, f32[200,512]{1,0:T(8,128)S(1)}, u32[]{:S(2)}, u32[]{:S(2)}) collective-permute-start(f32[200,512]{1,0:T(8,128)S(1)} %add.324), channel_id=1, source_target_pairs={{0,2},{2,0},{1,3},{3,1},{4,6},{6,4},{5,7},{7,5},{8,10},{10,8},{9,1... | collective-permute-start | bytes 1228808 | tf_op jit(solution)/shard_map/ppermute | solution.py:534
  207.3 5.8 %copy-start.1 = (f32[200,512]{1,0:T(8,128)}, f32[200,512]{1,0:T(8,128)S(1)}, u32[]{:S(2)}) copy-start(f32[200,512]{1,0:T(8,128)S(1)} %add_add_fusion.tile) | copy-start | bytes 1228804
  207.3 5.8 %collective-permute-start.30 = (f32[40,512]{1,0:T(8,128)S(1)}, f32[40,512]{1,0:T(8,128)S(1)}, u32[]{:S(2)}, u32[]{:S(2)}) collective-permute-start(f32[40,512]{1,0:T(8,128)S(1)} %slice_select_fusion), channel_id=1, source_target_pairs={{1,4},{5,8},{9,12},{4,1},{8,5},{12,9},{3,6},{7,10},{11,14},{6,3},{... | collective-permute-start | bytes 245768 | tf_op jit(solution)/shard_map/ppermute | solution.py:538
  (6 other events, 4.9 us)

commit v3 on v2

v3 whole, which is shorter than its diff:
```python
import functools

import jax
import jax.numpy as jnp
from jax import lax
from jax.experimental import pallas as pl
from jax.experimental.pallas import tpu as pltpu
from jax.sharding import PartitionSpec as P

PATCH = 1024
TR = 16
TC = 16
HD = 16
EPSILON = 1e-05
LOG2E = 1.4426950408889634
BF = jnp.bfloat16
F32 = jnp.float32
VMEM_LIMIT = 32 * 2**20
BORDER = 2


def launch(body, name, scalars, arrays, outs, scratch=(), after=(), hbm=(), flops=0, exps=0):
    counts = [len(scalars), len(arrays) + len(hbm), len(after), len(outs)]
    starts = [sum(counts[:i]) for i in range(5)]

    def kernel(*refs):
        body(
            refs[: starts[1]],
            refs[starts[1] : starts[2]],
            refs[starts[3] : starts[4]],
            *refs[starts[4] :],
        )

    return pl.pallas_call(
        kernel,
        in_specs=[pl.BlockSpec(memory_space=pltpu.SMEM)] * counts[0]
        + [pl.BlockSpec(memory_space=pltpu.VMEM)] * counts[1]
        + [pl.BlockSpec(memory_space=pl.ANY)] * counts[2],
        out_specs=[pl.BlockSpec(memory_space=pltpu.VMEM)] * counts[3],
        out_shape=[pltpu.VMEM(shape, F32) for shape in outs],
        scratch_shapes=[pltpu.VMEM(shape, F32) for shape in scratch],
        compiler_params=pltpu.CompilerParams(vmem_limit_bytes=VMEM_LIMIT),
        cost_estimate=pl.CostEstimate(flops=flops, bytes_accessed=0, transcendentals=exps),
        name=name,
    )(
        *scalars,
        *[pltpu.with_memory_space_constraint(x, pltpu.VMEM) for x in arrays],
        *hbm,
        *after,
    )


def split2(x):
    high = x.astype(BF)
    return high, (x - high.astype(F32)).astype(BF)


def split3(x):
    first = x.astype(BF)
    rest = x - first.astype(F32)
    second = rest.astype(BF)
    return first, second, (rest - second.astype(F32)).astype(BF)


def dot3(left, right, dims=(((1,), (0,)), ((), ()))):
    lh, ll = left
    rh, rl = right
    dot = functools.partial(lax.dot_general, dimension_numbers=dims, preferred_element_type=F32)
    return dot(lh, rh) + dot(lh, rl) + dot(ll, rh)


def layer_norm(values, gain_row):
    average = jnp.mean(values, axis=-1, keepdims=True)
    centered = values - average
    variance = jnp.mean(centered * centered, axis=-1, keepdims=True)
    return centered * lax.rsqrt(variance + EPSILON) * gain_row


def shift_by(k, count):
    return [(i, (i + k) % count) for i in range(count)]


def gather_slabs(piece):
    cols = lax.axis_size("col")
    reps = lax.axis_size("rep")
    far = [lax.ppermute(piece, "col", shift_by(k, cols)) for k in range(1, cols)]
    return [(p, lax.ppermute(p, "rep", shift_by(1, reps))) for p in [piece] + far]


def sliced(ref, scene, parts, part):
    size = ref.shape[1] // parts
    at = (scene * (parts // 2) + part) * size
    return ref[:, pl.ds(pl.multiple_of(at, size), size), :]


def prepare(place, w_qkv, w_out, w_up, w_down):
    width = w_out.shape[-1]
    features, hidden = w_out.shape[1], w_down.shape[1]

    def body(scalars, ins, outs):
        (place,) = scalars
        qkv, out, up, down = ins
        for layer in range(2):
            heads, units = outs[2 * layer], outs[2 * layer + 1]
            for j in range(3):
                heads[j] = qkv[layer, j].T
            heads[3] = out[layer]
            units[0] = up[layer].T
            units[1] = down[layer]
        for i in range(2):
            outs[4 + i][...] = sliced(outs[1], place[5], 4, i)

    per_layer = [(4, features, width), (2, hidden, width)]
    return launch(
        body,
        "prepare",
        [place],
        [],
        per_layer * 2 + [(2, hidden // 4, width)] * 2,
        hbm=[w_qkv, w_out, w_up, w_down],
    )


def project(place, slabs, gain, units, halves, after=()):
    cols = len(slabs)
    rows = slabs[0][0].shape[0]
    width = units[0].shape[-1]
    features = sum(u.shape[1] for u in units)
    half = rows // lax.axis_size(halves)

    def body(scalars, ins, outs, x_all):
        (place,) = scalars
        pieces, gain, units = ins[: 2 * cols], ins[2 * cols], ins[2 * cols + 1 :]
        q_t, k_t, v_t, x_half = outs
        col, rep = place[0], place[1]
        slab = width // cols
        for k in range(cols):
            near, other = pieces[2 * k][...], pieces[2 * k + 1][...]
            low = jnp.where(rep == 0, near, other)
            high = jnp.where(rep == 0, other, near)
            at = pl.multiple_of(lax.rem(col + cols - k, cols) * slab, 128)
            x_all[:, pl.ds(at, slab)] = jnp.concatenate([low, high], axis=1)
        weights = [split2(jnp.concatenate([u[j] for u in units], axis=0)) for j in range(3)]
        dims = (((1,), (1,)), ((), ()))
        chunk = 256
        for start in range(0, rows, chunk):
            normed = split2(layer_norm(x_all[start : start + chunk, :], gain[...]))
            k_t[:, start : start + chunk] = dot3(weights[1], normed, dims)
            v_t[:, start : start + chunk] = dot3(weights[2], normed, dims)
        first = (rep if halves == "rep" else col) * half
        chunk = min(chunk, half)
        for start in range(0, half, chunk):
            values = x_all[pl.ds(pl.multiple_of(first + start, chunk), chunk), :]
            x_half[start : start + chunk, :] = values
            normed = split2(layer_norm(values, gain[...]))
            q_t[:, start : start + chunk] = dot3(weights[0], normed, dims) * (LOG2E * HD**-0.5)

    return launch(
        body,
        "project",
        [place],
        [p for pair in slabs for p in pair] + [gain] + units,
        [(features, half), (features, rows), (features, rows), (half, width)],
        [(rows, width)],
        after,
    )


def attention(projected, heads_per_step=4):
    q_t, k_t, v_t = projected
    features, half = q_t.shape
    rows = k_t.shape[1]
    chunk = min(256, half)

    def body(scalars, ins, outs):
        q_t, k_t, v_t = ins
        (attended,) = outs

        def group(step, carry):
            def head_rows(h):
                return pl.ds(pl.multiple_of((step * heads_per_step + h) * HD, HD), HD)

            keys, values = [], []
            for h in range(heads_per_step):
                k1, k2, k3 = split3(k_t[head_rows(h), :])
                keys.append(jnp.concatenate([k1, k2, k1, k3, k2, k1], axis=0))
                v1, v2 = split2(v_t[head_rows(h), :])
                ones = jnp.ones_like(v1)
                values.append(
                    (jnp.concatenate([v1, v2, ones], axis=0), jnp.concatenate([v1, ones], axis=0))
                )

            def scores(h, at):
                q1, q2, q3 = split3(q_t[head_rows(h), at : at + chunk])
                queries = jnp.concatenate([q1, q1, q2, q1, q2, q3], axis=0)
                return lax.dot_general(
                    keys[h], queries, (((0,), (0,)), ((), ())), preferred_element_type=F32
                )

            items = [(h, at) for h in range(heads_per_step) for at in range(0, half, chunk)]
            current = scores(*items[0])
            for i, (h, at) in enumerate(items):
                following = scores(*items[i + 1]) if i + 1 < len(items) else None
                weights = jnp.exp2(current - jnp.max(current, axis=0, keepdims=True))
                high, low = split2(weights)
                first = jnp.dot(values[h][0], high, preferred_element_type=F32)
                second = jnp.dot(values[h][1], low, preferred_element_type=F32)
                total = first[:HD] + first[HD : 2 * HD] + second[:HD]
                norm = first[2 * HD : 2 * HD + 1] + second[HD : HD + 1]
                attended[head_rows(h), at : at + chunk] = total / norm
                current = following
            return carry

        lax.fori_loop(0, features // HD // heads_per_step, group, 0)

    (attended,) = launch(
        body,
        "attention",
        [],
        projected,
        [(features, half)],
        flops=16 * 10**9,
        exps=features // HD * rows * half,
    )
    return attended


def output_rows(place, attended, x_half, units, scatter, after=()):
    parts = lax.axis_size("col" if scatter else "rep")
    half, width = x_half.shape
    part = half // parts

    def body(scalars, ins, outs):
        (place,) = scalars
        attended, x_half, *units = ins
        w_out = split2(jnp.concatenate([u[3] for u in units], axis=0))
        mine = place[0] if scatter else place[1]
        for k in range(parts):
            at = pl.multiple_of(lax.rem(mine + k, parts) * part, 128)
            result = dot3(split2(attended[:, pl.ds(at, part)].T), w_out)
            if k == 0:
                result = result + x_half[pl.ds(at, part), :]
            if scatter:
                outs[k][...] = result
            else:
                outs[0][pl.ds(at, part), :] = result

    return launch(
        body,
        "output_rows",
        [place],
        [attended, x_half] + units,
        [(part, width)] * parts if scatter else [(half, width)],
        after=after,
    )


def sum_rows(place, keep, received, unit, after=()):
    def body(scalars, ins, outs):
        (place,) = scalars
        total = ins[0][...]
        for ref in ins[1:-1]:
            total = total + ref[...]
        outs[0][...] = total
        outs[1][...] = sliced(ins[-1], place[5], 2, 0)

    kinds, count, width = unit.shape
    return launch(
        body,
        "sum_rows",
        [place],
        [keep] + received + [unit],
        [keep.shape, (kinds, count // 2, width)],
        after=after,
    )


def sum_pairs(own, received, after=()):
    def body(scalars, ins, outs):
        for k, out in enumerate(outs):
            out[...] = ins[k][...] + ins[len(own) + k][...]

    return launch(body, "sum_pairs", [], own + received, [x.shape for x in own], after=after)


def slice_unit(place, unit, part, after=()):
    def body(scalars, ins, outs):
        outs[0][...] = sliced(ins[0], scalars[0][5], 4, part)

    kinds, count, width = unit.shape
    (out,) = launch(
        body, "slice_unit", [place], [unit], [(kinds, count // 4, width)], after=after
    )
    return out


def mlp_rows(values, gain_row, up, down):
    normed = split2(layer_norm(values, gain_row))
    hidden = dot3(normed, up, (((1,), (1,)), ((), ())))
    hidden = split2(hidden * (0.5 + 0.5 * lax.erf(hidden * 0.5**0.5)))
    return dot3(hidden, down)


def mlp(place, pieces, gain, units):
    cols, reps = lax.axis_size("col"), len(pieces)
    part, width = pieces[0].shape
    rows = part * reps
    feature = width // (cols * reps)
    hidden = sum(u.shape[1] for u in units)

    def body(scalars, ins, outs, partial):
        (place,) = scalars
        pieces, gain, units = ins[:reps], ins[reps], ins[reps + 1 :]
        col, rep = place[0], place[1]
        up, down = (split2(jnp.concatenate([u[j] for u in units], axis=0)) for j in range(2))
        for k in range(reps):
            at = pl.multiple_of(lax.rem(rep + reps - k, reps) * part, 128)
            values = pieces[k][...]
            result = mlp_rows(values, gain[...], up, down)
            partial[pl.ds(at, part), :] = result + values if k == 0 else result
        for k in range(cols):
            for j in range(reps):
                to_rep = lax.rem(rep + j, reps)
                to_col = lax.rem(col + k, cols)
                out = outs[k * reps + j]
                if feature % 128 == 0:
                    at = pl.multiple_of((to_col * reps + to_rep) * feature, 128)
                    out[...] = partial[:, pl.ds(at, feature)]
                else:
                    at = pl.multiple_of(to_col * reps * feature, 128)
                    slab = partial[:, pl.ds(at, reps * feature)]
                    out[...] = jnp.where(to_rep == 0, slab[:, :feature], slab[:, feature:])

    return launch(
        body,
        "mlp",
        [place],
        pieces + [gain] + units,
        [(rows, feature)] * (cols * reps),
        [(rows, width)],
        flops=4 * rows * width * hidden * 3,
    )


def pooled_mlp(place, near, other, pillar, cells, gain, units):
    cols = lax.axis_size("col")
    half, width = near.shape
    count = cells.shape[1]
    hidden = sum(u.shape[1] for u in units)

    def body(scalars, ins, outs):
        (place,) = scalars
        near, other, pillar, cells, gain, *units = ins
        col, rep = place[0], place[1]
        part = half // 2
        up, down = (split2(jnp.concatenate([u[j] for u in units], axis=0)) for j in range(2))
        totals = [None] * (2 * cols)
        for k in range(2):
            source = lax.rem(rep + k, 2) * part
            tokens_cells = pillar[:, pl.ds(pl.multiple_of(col * half + source, 128), part)]
            here = pl.ds(pl.multiple_of(source, 128), part)
            values = near[here, :] + other[here, :]
            result = mlp_rows(values, gain[...], up, down)
            if k == 0:
                result = result + values
            high, low = split2(result)
            for i in range(2 * cols):
                chosen = jnp.where(cells[i] == tokens_cells, 1.0, 0.0).astype(BF)
                term = jnp.dot(chosen, high, preferred_element_type=F32) + jnp.dot(
                    chosen, low, preferred_element_type=F32
                )
                totals[i] = term if totals[i] is None else totals[i] + term
        for i in range(2 * cols):
            outs[i][...] = totals[i]

    outs = launch(
        body,
        "mlp_pool",
        [place],
        [near, other, pillar, cells, gain] + units,
        [(count, width)] * (2 * cols),
        flops=4 * half * width * hidden * 3,
    )
    return outs[::2], outs[1::2]


def pick_blocks(place, sources, index, outs, each, unit=None, after=()):
    counts = [s.shape[0] for s in sources]
    shape = sources[0].shape[1:]

    def body(scalars, ins, targets, blocks):
        place, index = scalars
        start = 0
        for ref, count in zip(ins, counts):
            blocks[start : start + count] = ref[...]
            start += count
        for o in range(outs):
            for j in range(each):
                targets[o][j] = blocks[index[o * each + j]]
        if unit is not None:
            targets[-1][...] = sliced(ins[-1], place[5], 4, 0)

    more = [] if unit is None else [unit]
    return launch(
        body,
        "pick_blocks",
        [place, index],
        list(sources) + more,
        [(each,) + shape] * outs + [(2, u.shape[1] // 4, u.shape[2]) for u in more],
        [(sum(counts),) + shape],
        after,
    )


def routes(dest_device, dest_slot):
    count = dest_device.shape[0]
    peers = lax.axis_size("tok")
    capacity = max(2, (count + peers - 4) // (peers - 1))
    order = jnp.arange(count, dtype=jnp.int32)
    earlier = (dest_device[:, None] == dest_device[None, :]) & (order[None, :] < order[:, None])
    rank = jnp.sum(earlier.astype(jnp.int32), axis=1)
    shifts = jnp.arange(peers, dtype=jnp.int32)
    targets = (lax.axis_index("tok") + shifts) % peers
    places = jnp.arange(capacity, dtype=jnp.int32)
    chosen = (
        (targets[:, None, None] == dest_device[None, None, :])
        & (places[None, :, None] == rank[None, None, :])
    ).astype(jnp.int32)
    blocks = jnp.sum(chosen * order, axis=-1)
    slots = jnp.sum(chosen * (dest_slot + 1), axis=-1)
    arrived = jnp.stack(
        [slots[0]]
        + [lax.ppermute(slots[k], "tok", shift_by(k, peers)) for k in range(1, peers)]
    ).reshape(-1)
    matches = (arrived[None, :] == order[:, None] + 1).astype(jnp.int32)
    sources = jnp.sum(matches * jnp.arange(peers * capacity, dtype=jnp.int32), axis=1)
    return blocks, sources


def raster_kernel(reps, scalars, ins, outs, cells, normed):
    (place,) = scalars
    tile, halo, depth, gain, point = ins
    (out_ref,) = outs
    tok, col, rep, height, full_width = (place[i] for i in (2, 0, 1, 3, 4))
    tile_rows = out_ref.shape[0]
    tile_cols = out_ref.shape[1]
    width = out_ref.shape[2]
    wide = tile_cols + 2 * BORDER
    kept = tile_rows + BORDER
    padded = cells.shape[1]
    cells[...] = jnp.zeros_like(cells)
    normed[...] = jnp.zeros_like(normed)
    first = BORDER * (1 - rep)
    for i in range(kept):
        cells[first + i, 0:wide, :] = tile[i * wide : (i + 1) * wide, :]
    other = (tile_rows + BORDER) * rep
    for i in range(BORDER):
        cells[other + i, 0:wide, :] = halo[i * wide : (i + 1) * wide, :]
    lead = 8
    row_zero = tok * (tile_rows * reps) + rep * tile_rows - BORDER
    col_zero = col * tile_cols - BORDER
    for layer in range(2):
        rim = layer + 1
        grid_rows = tile_rows + 2 * BORDER - 2 * rim
        low_col, span = (0, padded) if layer == 0 else (BORDER, tile_cols)
        values = cells[...]
        mean = jnp.mean(values * values, axis=-1, keepdims=True)
        normed[:, lead : lead + padded, :] = values * lax.rsqrt(mean + EPSILON) * gain[layer : layer + 1]
        mixed = None
        for a in range(3):
            for b in range(3):
                start = lead + low_col + b - 1
                term = (
                    normed[rim - 1 + a : rim - 1 + a + grid_rows, start : start + span, :]
                    * depth[layer, a, b][None, None, :]
                )
                mixed = term if mixed is None else mixed + term
        left = split2(mixed.reshape(grid_rows * span, width))
        value = dot3(left, split2(point[layer, :, :width]))
        gate = dot3(left, split2(point[layer, :, width:]))
        change = (value * jax.nn.sigmoid(gate)).reshape(grid_rows, span, width)
        centre = cells[rim : rim + grid_rows, low_col : low_col + span, :]
        if layer == 0:
            row = row_zero + rim + lax.broadcasted_iota(jnp.int32, (grid_rows, span, 1), 0)
            column = col_zero + lax.broadcasted_iota(jnp.int32, (grid_rows, span, 1), 1)
            inside = (row >= 0) & (row < height) & (column >= 0) & (column < full_width)
            cells[rim : rim + grid_rows, :, :] = jnp.where(inside, centre + change, 0.0)
        else:
            out_ref[...] = centre + change


def raster_layers(place, tile, halo, depth_weight, point_weight, raster_gain, tile_rows):
    reps = lax.axis_size("rep")
    width = tile.shape[-1]
    padded = -(-(TC + 2 * BORDER) // 8) * 8
    kernel = functools.partial(raster_kernel, reps)
    arrays = [place, tile, halo, depth_weight, raster_gain, point_weight]
    return pl.pallas_call(
        lambda *refs: kernel(refs[:1], refs[1:6], refs[6:7], *refs[7:]),
        in_specs=[pl.BlockSpec(memory_space=pltpu.SMEM)]
        + [pl.BlockSpec(memory_space=pltpu.VMEM)] * 5,
        out_specs=pl.BlockSpec(memory_space=pltpu.VMEM),
        out_shape=jax.ShapeDtypeStruct((tile_rows, TC, width), F32),
        scratch_shapes=[
            pltpu.VMEM((tile_rows + 2 * BORDER, padded, width), F32),
            pltpu.VMEM((tile_rows + 2 * BORDER, padded + 16, width), F32),
        ],
        compiler_params=pltpu.CompilerParams(vmem_limit_bytes=VMEM_LIMIT),
        name="raster",
    )(*arrays[:1], *[pltpu.with_memory_space_constraint(x, pltpu.VMEM) for x in arrays[1:]])


def tile_cells(tile_rows):
    cols = lax.axis_size("col")
    tok, col, rep = (lax.axis_index(a) for a in ("tok", "col", "rep"))
    full_width = TC * cols
    wide = TC + 2 * BORDER
    flat = jnp.arange((tile_rows + BORDER) * wide, dtype=jnp.int32)
    row, column = flat // wide, flat % wide
    tables = []
    for k in range(cols):
        for r in (rep, 1 - rep):
            x = ((col + k) % cols) * TC - BORDER + column
            y = tok * TR + r * (tile_rows - BORDER) + row
            tables.append(jnp.where((x >= 0) & (x < full_width), y * full_width + x, -2))
    return jnp.stack(tables)[:, :, None]


def on_device(
    tokens,
    w_qkv,
    w_out,
    w_up,
    w_down,
    attn_gain,
    mlp_gain,
    dest_device,
    dest_slot,
    pillar,
    depth_weight,
    point_weight,
    raster_gain,
):
    cols, reps, toks = (lax.axis_size(a) for a in ("col", "rep", "tok"))
    tok, col, rep = (lax.axis_index(a) for a in ("tok", "col", "rep"))
    swap = shift_by(1, reps)
    scene_swap = shift_by(1, lax.axis_size("scene"))
    numbers = [col, rep, tok, TR * toks, TC * cols, lax.axis_index("scene")]
    place = jnp.stack([jnp.int32(n) for n in numbers])
    to_cols = lambda x: [lax.ppermute(x, "col", shift_by(k, cols)) for k in range(1, cols)]
    to_scene = lambda xs: [lax.ppermute(x, "scene", scene_swap) for x in xs]

    slabs = gather_slabs(tokens)
    heads0, hidden0, heads1, hidden1, *own_hidden0 = prepare(place, w_qkv, w_out, w_up, w_down)
    blocks_out, blocks_in = routes(dest_device, dest_slot)
    count = dest_device.shape[0]
    each = count // (reps * cols)
    of_rep, of_col = blocks_out // (each * cols), blocks_out // each % cols
    picks = ((col - of_col) % cols * reps + of_rep) * each + blocks_out % each
    capacity = picks.shape[1]
    picks = picks.reshape(-1)
    tile_rows = TR // reps
    cells = tile_cells(tile_rows)

    units = [heads0, lax.ppermute(heads0, "rep", swap)]
    direct = [to_cols(x) for x in own_hidden0]
    *projected, x_half = project(
        place, slabs, attn_gain[:1], units, "rep", (picks, blocks_in, cells)
    )
    passed = [to_scene(x) for x in direct]
    attended = attention(projected)
    keep, *sends = output_rows(place, attended, x_half, units, True, passed[0])
    received = [
        lax.ppermute(part, "col", shift_by(k + 1, cols)) for k, part in enumerate(sends)
    ]
    keep, own_heads1 = sum_rows(place, keep, received, heads1)
    far_heads1 = to_cols(own_heads1)
    outs = mlp(
        place,
        [keep, lax.ppermute(keep, "rep", swap)],
        mlp_gain[:1],
        [hidden0] + [u for x in direct + passed for u in x],
    )
    others = [lax.ppermute(x, "rep", swap) for x in outs[1::2]]
    parts = sum_pairs(list(outs[::2]), others, far_heads1)
    gathered = [parts[0]] + [
        lax.ppermute(parts[k], "col", shift_by(k, cols)) for k in range(1, cols)
    ]
    feature = parts[0].shape[1]
    *outgoing, own_hidden1 = pick_blocks(
        place,
        [g.reshape(reps * each, -1, feature) for g in gathered],
        picks,
        toks,
        capacity,
        hidden1,
    )
    incoming = [outgoing[0]] + [
        lax.ppermute(outgoing[k], "tok", shift_by(k, toks)) for k in range(1, toks)
    ]
    direct = to_cols(own_hidden1)
    (moved,) = pick_blocks(place, incoming, blocks_in, 1, count, None, direct)
    moved = moved.reshape(-1, feature)
    slabs = gather_slabs(moved)
    more = to_cols(slice_unit(place, hidden1, 1, (slabs[0][1],)))

    units = [heads1] + far_heads1 + to_scene(far_heads1)
    *projected, x_half = project(place, slabs, attn_gain[1:], units, "col")
    attended = attention(projected)
    more_passed = to_scene(more)
    (near,) = output_rows(place, attended, x_half, units, False, more_passed)
    own, other = pooled_mlp(
        place,
        near,
        lax.ppermute(near, "rep", swap),
        pillar[None],
        cells,
        mlp_gain[1:],
        [hidden1] + direct + to_scene(direct) + more + more_passed,
    )
    sums = [own[k] + lax.ppermute(other[k], "rep", swap) for k in range(cols)]
    tile = sums[0]
    for k in range(1, cols):
        tile = tile + lax.ppermute(sums[k], "col", shift_by(k, cols))
    edge = BORDER * (TC + 2 * BORDER)
    edge_rows = jnp.where(rep == 0, tile[:edge], tile[-edge:])
    pairs = [(i * reps + reps - 1, (i + 1) * reps) for i in range(toks - 1)]
    halo = lax.ppermute(edge_rows, ("tok", "rep"), pairs + [(b, a) for a, b in pairs])
    return raster_layers(place, tile, halo, depth_weight, point_weight, raster_gain, tile_rows)


def solution(mesh):
    placed = (
        P(("scene", "tok"), ("col", "rep")),
        P(None, None, None, ("col", "rep")),
        P(None, ("col", "rep"), None),
        P(None, None, ("col", "rep")),
        P(None, ("col", "rep"), None),
        P(),
        P(),
        P(("scene", "tok")),
        P(("scene", "tok")),
        P(("scene", "tok")),
        P(),
        P(),
        P(),
    )
    return jax.shard_map(
        on_device,
        mesh=mesh,
        in_specs=placed,
        out_specs=P(("scene", "tok", "rep"), "col", None),
        check_vma=False,
    )
```

time: 220 us -> 209 us (0.950)
  Pallas kernels: 72 us -> 56.8 us
  other arithmetic: 16.1 us -> 5.96 us
  local copies, waits for them, and re-layouts: 19.2 us -> 25.7 us
  waiting for transfers between devices: 75.4 us -> 80.9 us
  starting transfers between devices: 35.2 us -> 38.1 us
    ppermute x2, waiting for transfers between devices: 35.7 us -> 9.88 us  [gather_slabs(): lax.ppermute(piece, 'col', shift_by(k, cols))]
    ppermute x13 -> x15, waiting for transfers between devices: 17.6 us -> 40.6 us  [the longest x5 16.4 us: on_device(): lax.ppermute(x, 'col', shift_by(k, cols))]
    pallas_call x9 -> x15, Pallas kernels: 72 us -> 56.8 us  [the longest x14 52.7 us: launch(): pl.pallas_call(kernel, in_specs=[pl.BlockSpec(memory_space=pltpu.SMEM)] *...]
    slice x7 -> x1, local copies, waits for them, and re-layouts: 7.04 us -> 1.36 us  [on_device(): *projected, x_half = project(place, slabs, attn_gain[1:], units, 'col')]
    ppermute x1, waiting for transfers between devices: 1.29 us -> 6.75 us  [on_device(): lax.ppermute(parts[k], 'col', shift_by(k, cols))]
    another operation x4, local copies, waits for them, and re-layouts: 0.37 us -> 5.18 us  [routes(): jnp.stack([slots[0]] + [lax.ppermute(slots[k], 'tok', shift_by(k, peers))...]
    ppermute x3, waiting for transfers between devices: 6.46 us -> 10.9 us  [on_device(): lax.ppermute(outgoing[k], 'tok', shift_by(k, toks))]
    another operation x4 -> x0, other arithmetic: 4.31 us -> none  [on_device(): hidden_unit = [jnp.stack([w_up[l].T, w_down[l]], axis=0) for l in range(2)]]
  transfers between devices with their start and end apart: 31 -> 33, of which waited for: 10 -> 13; matrix products, arithmetic and copies ran while one was open for 13% -> 9% of each run, Pallas kernels for 22% -> 21%
where the time goes in v3:
time: 209 us; the launch traced here: 208 us
  waiting for transfers between devices  80.9 us (39%)
  Pallas kernels  56.8 us (27%)
  starting transfers between devices  38.1 us (18%)
  local copies, waits for them, and re-layouts  25.7 us (12%)
  other arithmetic  5.96 us (3%)
    pallas_call x14, Pallas kernels, launch(): pl.pallas_call(kernel, in_specs=[pl.BlockSpec(memory_space=pltpu.SMEM)] *...  52.7 us
    ppermute x5, waiting for transfers between devices, on_device(): lax.ppermute(x, 'col', shift_by(k, cols))  16.4 us
    unnamed x47, local copies, waits for them, and re-layouts  13.1 us
    ppermute x5, waiting for transfers between devices, on_device(): to_scene = lambda xs: [lax.ppermute(x, 'scene', scene_swap) for x in xs]  12.1 us
    ppermute x3, waiting for transfers between devices, on_device(): lax.ppermute(outgoing[k], 'tok', shift_by(k, toks))  10.9 us
    ppermute x1, waiting for transfers between devices, on_device(): lax.ppermute(part, 'col', shift_by(k + 1, cols))  10.9 us
    ppermute x2, waiting for transfers between devices, gather_slabs(): lax.ppermute(piece, 'col', shift_by(k, cols))  9.88 us
    ppermute x1, waiting for transfers between devices, on_device(): tile = tile + lax.ppermute(sums[k], 'col', shift_by(k, cols))  9.28 us
  transfers between devices with their start and end apart: 33, of which 13 were waited for; matrix products, arithmetic and copies ran while one was open for 9% of the time, Pallas kernels for 21%

profile of v3, /device:TPU:1, one launch (start us, length us, event | category | flops | bytes accessed | tf_op | source)
XLA Modules:
  0.0 207.9 jit_solution(9127001513030023844)
XLA Ops:
  0.0 2.0 collective-permute-start.4
  3.1 1.6 copy-done.1
  4.7 1.6 copy-done.2
  6.3 1.4 copy-done.3
  8.7 2.7 %prepare.1 = (f32[4,128,512]{2,1,0:T(8,128)}, f32[2,512,512]{2,1,0:T(8,128)S(1)}, f32[4,128,512]{2,1,0:T(8,128)S(1)}, f32[2,512,512]{2,1,0:T(8,128)S(1)}, f32[2,...) custom-call(s32[6]{0:T(128)S(1)} %stack.38.refs_0_, f32[2,3,512,128]{3,2,1,0:T(8,128)S(1)} %copy-done.3, ...), custom_call_target="tpu_custom_call" | custom-call | tf_op jit(solution)/shard_map/prepare/pallas_call | solution.py:34
  11.5 1.3 copy-done.15
  14.7 1.3 slice_reduce_fusion.2
  16.0 1.3 collective-permute-start
  19.1 1.3 copy.30
  20.4 1.3 reduce_sum.42
  21.7 1.3 fusion.3.refs_8_.refs_1_
  24.6 1.4 fusion.11
  26.0 2.3 %collective-permute-start.1 = (s32[5]{0:T(128)}, s32[5]{0:T(128)}, u32[]{:S(2)}, u32[]{:S(2)}) collective-permute-start(s32[5]{0:T(128)} %get-tuple-element.73), channel_id=1, source_target_pairs={{0,8},{4,12},{8,0},{12,4},{1,9},{5,13},{9,1},{13,5},{2,10},{6,14},... | collective-permute-start | bytes 68 | tf_op jit(solution)/shard_map/ppermute | solution.py:433
  28.3 1.3 copy.26
  29.6 1.6 collective-permute-start.2
  31.2 1.3 copy.27
  32.4 1.4 collective-permute-start.11
  33.9 1.3 copy.28
  35.2 1.4 pad_add_fusion
  36.6 1.3 copy.29
  40.0 1.3 collective-permute-start.8
  44.4 4.9 %project.2 = (f32[256,512]{1,0:T(8,128)S(1)}, f32[256,1024]{1,0:T(8,128)S(1)}, f32[256,1024]{1,0:T(8,128)S(1)}, f32[512,512]{1,0:T(8,128)S(1)}) custom-call(s32[6]{0:T(128)S(1)} %copy-done.7, f32[1024,128]{1,0:T(8,128)S(1)} %copy-done.5, f32[1024,128]{1,0:T(8,128)} %collective-permute-done.3.refs_2_, f32[1024,128]{1,0:T(8,128)} %collective-permute-done.4.refs_3_, ...), custom_call_target="tpu_custom_call" | custom-call | tf_op jit(solution)/shard_map/project/pallas_call | solution.py:34
  49.3 12.5 %attention.2.refs_1_ = f32[256,512]{1,0:T(8,128)S(1)} custom-call(f32[256,512]{1,0:T(8,128)S(1)} %get-tuple-element.39.refs_0_, f32[256,1024]{1,0:T(8,128)S(1)} %get-tuple-element.40.refs_1_, f32[256,1024]{1,0:T(8,128)S(1)} %get-tuple-element.41.refs_2_), custom_call_target="tpu_custom_call" | custom-call | flops 16000000000 | tf_op jit(solution)/shard_map/attention/pallas_call | solution.py:34
  61.9 2.2 %output_rows.2 = (f32[256,512]{1,0:T(8,128)S(1)}, f32[256,512]{1,0:T(8,128)S(1)}) custom-call(s32[6]{0:T(128)S(1)} %copy-done.8, f32[256,512]{1,0:T(8,128)S(1)} %attention.2.refs_1_, f32[512,512]{1,0:T(8,128)S(1)} %get-tuple-element.42.refs_2_, f32[4,128,512]{2,1,0:T(8,128)} %get-tuple-element.38.refs_6_.refs_3_, ...), custom_call_target="tpu_custom_call" | custom-call | tf_op jit(solution)/shard_map/output_rows/pallas_call | solution.py:34
  64.5 10.9 %collective-permute-done.9.refs_2_ = f32[256,512]{1,0:T(8,128)S(1)} collective-permute-done((f32[256,512]{1,0:T(8,128)S(1)}, f32[256,512]{1,0:T(8,128)S(1)}, u32[]{:S(2)}, u32[]{:S(2)}) %collective-permute-start.9) | collective-permute-done | bytes 524320 | tf_op jit(solution)/shard_map/ppermute | solution.py:574
  76.1 3.2 %collective-permute-start.10 = (f32[256,512]{1,0:T(8,128)S(1)}, f32[256,512]{1,0:T(8,128)S(1)}, u32[]{:S(2)}, u32[]{:S(2)}) collective-permute-start(f32[256,512]{1,0:T(8,128)S(1)} %get-tuple-element.47.refs_1_), channel_id=1, source_target_pairs={{0,1},{1,0},{2,3},{3,2},{4,5},{5,4},{6,7},{7,6},{8,9},{9,8},{10,11... | collective-permute-start | bytes 1572872 | tf_op jit(solution)/shard_map/ppermute | solution.py:580
  80.8 5.1 %mlp.1 = (f32[512,128]{1,0:T(8,128)S(1)}, f32[512,128]{1,0:T(8,128)S(1)}, f32[512,128]{1,0:T(8,128)S(1)}, f32[512,128]{1,0:T(8,128)S(1)}) custom-call(s32[6]{0:T(128)S(1)} %copy-done.8, f32[256,512]{1,0:T(8,128)S(1)} %get-tuple-element.47.refs_1_, f32[256,512]{1,0:T(8,128)S(1)} %collective-permute-done.10.refs_2_, f32[1,512]{1,0:T(1,128)S(1)} %get-tuple-element.77.refs_3_, ...), custom_call_target="tpu_custom_call" | custom-call | flops 3221225472 | tf_op jit(solution)/shard_map/mlp/pallas_call | solution.py:34
  86.4 6.4 %collective-permute-done.15.refs_4_.refs_7_ = f32[4,64,512]{2,1,0:T(8,128)S(1)} collective-permute-done((f32[4,64,512]{2,1,0:T(8,128)S(1)}, f32[4,64,512]{2,1,0:T(8,128)S(1)}, u32[]{:S(2)}, u32[]{:S(2)}) %collective-permute-start.15) | collective-permute-done | bytes 524320 | tf_op jit(solution)/shard_map/ppermute | solution.py:550
  93.2 6.7 %collective-permute-done.16 = f32[512,128]{1,0:T(8,128)S(1)} collective-permute-done((f32[512,128]{1,0:T(8,128)S(1)}, f32[512,128]{1,0:T(8,128)S(1)}, u32[]{:S(2)}, u32[]{:S(2)}) %collective-permute-start.16) | collective-permute-done | bytes 262176 | tf_op jit(solution)/shard_map/ppermute | solution.py:587
  101.6 2.7 %collective-permute-start.18 = (f32[5,64,128]{2,1,0:T(8,128)S(1)}, f32[5,64,128]{2,1,0:T(8,128)S(1)}, u32[]{:S(2)}, u32[]{:S(2)}) collective-permute-start(f32[5,64,128]{2,1,0:T(8,128)S(1)} %get-tuple-element.60), channel_id=1, source_target_pairs={{0,8},{4,12},{8,0},{12,4},{1,9},{5,13},{9,1},{13,5},{2,10},{6,14},... | collective-permute-start | bytes 491528 | tf_op jit(solution)/shard_map/ppermute | solution.py:599
  104.9 2.1 %collective-permute-done.17.refs_3_ = f32[5,64,128]{2,1,0:T(8,128)S(1)} collective-permute-done((f32[5,64,128]{2,1,0:T(8,128)S(1)}, f32[5,64,128]{2,1,0:T(8,128)S(1)}, u32[]{:S(2)}, u32[]{:S(2)}) %collective-permute-start.17) | collective-permute-done | bytes 163872 | tf_op jit(solution)/shard_map/ppermute | solution.py:599
  107.0 8.8 %collective-permute-done.18.refs_4_ = f32[5,64,128]{2,1,0:T(8,128)S(1)} collective-permute-done((f32[5,64,128]{2,1,0:T(8,128)S(1)}, f32[5,64,128]{2,1,0:T(8,128)S(1)}, u32[]{:S(2)}, u32[]{:S(2)}) %collective-permute-start.18) | collective-permute-done | bytes 163872 | tf_op jit(solution)/shard_map/ppermute | solution.py:599
  119.3 1.3 collective-permute-start.25
  120.8 9.9 %collective-permute-done.22.refs_3_ = f32[1024,128]{1,0:T(8,128)S(1)} collective-permute-done((f32[1024,128]{1,0:T(8,128)S(1)}, f32[1024,128]{1,0:T(8,128)S(1)}, u32[]{:S(2)}, u32[]{:S(2)}) %collective-permute-start.22) | collective-permute-done | bytes 524320 | tf_op jit(solution)/shard_map/ppermute | solution.py:86
  130.7 1.3 collective-permute-start.23
  132.0 9.9 %collective-permute-done.25.refs_9_ = f32[2,128,512]{2,1,0:T(8,128)S(1)} collective-permute-done((f32[2,128,512]{2,1,0:T(8,128)S(1)}, f32[2,128,512]{2,1,0:T(8,128)S(1)}, u32[]{:S(2)}, u32[]{:S(2)}) %collective-permute-start.25) | collective-permute-done | bytes 524320 | tf_op jit(solution)/shard_map/ppermute | solution.py:550
  142.0 3.5 %project.3 = (f32[256,512]{1,0:T(8,128)S(1)}, f32[256,1024]{1,0:T(8,128)S(1)}, f32[256,1024]{1,0:T(8,128)S(1)}, f32[512,512]{1,0:T(8,128)S(1)}) custom-call(s32[6]{0:T(128)S(1)} %copy-done.8, f32[1024,128]{1,0:T(8,128)S(1)} %bitcast.15, f32[1024,128]{1,0:T(8,128)S(1)} %collective-permute-done.21.refs_2_, f32[1024,128]{1,0:T(8,128)S(1)} %collective-permute-done.22.refs_3_, ...), custom_call_target="tpu_custom_call" | custom-call | tf_op jit(solution)/shard_map/project/pallas_call | solution.py:34
  145.4 12.4 %attention.3.refs_1_ = f32[256,512]{1,0:T(8,128)S(1)} custom-call(f32[256,512]{1,0:T(8,128)S(1)} %get-tuple-element.63.refs_0_, f32[256,1024]{1,0:T(8,128)S(1)} %get-tuple-element.64.refs_1_, f32[256,1024]{1,0:T(8,128)S(1)} %get-tuple-element.65.refs_2_), custom_call_target="tpu_custom_call" | custom-call | flops 16000000000 | tf_op jit(solution)/shard_map/attention/pallas_call | solution.py:34
  160.3 1.4 collective-permute-start.28
  161.7 12.1 %collective-permute-done.28.refs_8_ = f32[2,128,512]{2,1,0:T(8,128)S(1)} collective-permute-done((f32[2,128,512]{2,1,0:T(8,128)S(1)}, f32[2,128,512]{2,1,0:T(8,128)S(1)}, u32[]{:S(2)}, u32[]{:S(2)}) %collective-permute-start.28) | collective-permute-done | bytes 524320 | tf_op jit(solution)/shard_map/ppermute | solution.py:551
  173.8 5.7 %mlp_pool.1 = (f32[200,512]{1,0:T(8,128)S(1)}, f32[200,512]{1,0:T(8,128)S(1)}, f32[200,512]{1,0:T(8,128)S(1)}, f32[200,512]{1,0:T(8,128)S(1)}) custom-call(s32[6]{0:T(128)S(1)} %copy-done.8, f32[512,512]{1,0:T(8,128)S(1)} %output_rows.3.refs_1_, f32[512,512]{1,0:T(8,128)S(1)} %collective-permute-done.27.refs_2_, s32[1,1024]{1,0:T(1,128)S(1)} %bitcast.18, ...), custom_call_target="tpu_custom_call" | custom-call | flops 3221225472 | tf_op jit(solution)/shard_map/mlp_pool/pallas_call | solution.py:34
  180.5 1.3 collective-permute-done.30
  181.9 1.5 collective-permute-start.31
  183.3 9.3 %collective-permute-done.31 = f32[200,512]{1,0:T(8,128)S(1)} collective-permute-done((f32[200,512]{1,0:T(8,128)S(1)}, f32[200,512]{1,0:T(8,128)S(1)}, u32[]{:S(2)}, u32[]{:S(2)}) %collective-permute-start.31) | collective-permute-done | bytes 409632 | tf_op jit(solution)/shard_map/ppermute | solution.py:624
  192.8 7.0 %collective-permute-start.32 = (f32[40,512]{1,0:T(8,128)S(1)}, f32[40,512]{1,0:T(8,128)S(1)}, u32[]{:S(2)}, u32[]{:S(2)}) collective-permute-start(f32[40,512]{1,0:T(8,128)S(1)} %slice_select_fusion), channel_id=1, source_target_pairs={{1,4},{5,8},{9,12},{4,1},{8,5},{12,9},{3,6},{7,10},{11,14},{6,3},{... | collective-permute-start | bytes 245768 | tf_op jit(solution)/shard_map/ppermute | solution.py:628
  199.7 1.8 collective-permute-done.32.refs_2_
  201.6 2.2 %copy-done = f32[2,512,1024]{2,1,0:T(8,128)S(1)} copy-done((f32[2,512,1024]{2,1,0:T(8,128)S(1)}, f32[2,512,1024]{2,1,0:T(8,128)}, u32[]{:S(2)}) %copy-start) | copy-done | bytes 4194328
  203.8 4.1 %raster.1 = f32[8,16,512]{2,1,0:T(8,128)} custom-call(s32[6]{0:T(128)S(1)} %copy-done.9, f32[200,512]{1,0:T(8,128)S(1)} %add_add_fusion.refs_1_, f32[40,512]{1,0:T(8,128)S(1)} %collective-permute-done.32.refs_2_, f32[2,3,3,512]{3,2,1,0:T(4,128)S(1)} %copy.33.refs_3_, f32[2,512]{1,0:T(2,128)S(1)} %copy-done.12, f32[2,512,1024]{2,1,0:T(8,128)S(1)} %copy-done), custom_call_target="tpu_custom_call" | custom-call | tf_op jit(solution)/shard_map/raster/pallas_call | solution.py:498
  (108 shorter events, 25.6 us)
Async XLA Ops:
  0.0 23.0 %collective-permute-start.4 = (f32[1024,128]{1,0:T(8,128)}, f32[1024,128]{1,0:T(8,128)}, u32[]{:S(2)}, u32[]{:S(2)}) collective-permute-start(f32[1024,128]{1,0:T(8,128)} %refs_1_.3), channel_id=1, source_target_pairs={{0,2},{2,0},{1,3},{3,1},{4,6},{6,4},{5,7},{7,5},{8,10},{10,8},{9,1... | collective-permute-start | bytes 1572872 | tf_op jit(solution)/shard_map/ppermute | solution.py:86
  2.0 39.3 %collective-permute-start.3 = (f32[1024,128]{1,0:T(8,128)}, f32[1024,128]{1,0:T(8,128)}, u32[]{:S(2)}, u32[]{:S(2)}) collective-permute-start(f32[1024,128]{1,0:T(8,128)} %refs_1_.3), channel_id=1, source_target_pairs={{0,1},{1,0},{2,3},{3,2},{4,5},{5,4},{6,7},{7,6},{8,9},{9,8},{10,11... | collective-permute-start | bytes 1572872 | tf_op jit(solution)/shard_map/ppermute | solution.py:87
  3.1 1.6 copy-start.1
  4.7 1.6 copy-start.2
  8.7 2.8 %copy-start.6 = (s32[6]{0:T(128)}, s32[6]{0:T(128)S(1)}, u32[]{:S(2)}) copy-start(s32[6]{0:T(128)S(1)} %stack.38.refs_0_) | copy-start | bytes 76
  8.7 4.9 %copy-start.21 = (s32[16]{0:T(128)S(1)}, s32[16]{0:T(128)}, u32[]{:S(2)}) copy-start(s32[16]{0:T(128)} %param.20) | copy-start | bytes 196
  8.7 5.2 %copy-start.22 = (s32[16]{0:T(128)S(1)}, s32[16]{0:T(128)}, u32[]{:S(2)}) copy-start(s32[16]{0:T(128)} %param.21) | copy-start | bytes 196
  13.6 27.7 %collective-permute-start.6 = (f32[4,128,512]{2,1,0:T(8,128)}, f32[4,128,512]{2,1,0:T(8,128)}, u32[]{:S(2)}, u32[]{:S(2)}) collective-permute-start(f32[4,128,512]{2,1,0:T(8,128)} %get-tuple-element.38.refs_6_.refs_3_), channel_id=1, source_target_pairs={{0,1},{1,0},{2,3},{3,2},{4,5},{5,4},{6,7},{7,6},{8,9},{9,8},{10,11... | collective-permute-start | bytes 3145736 | tf_op jit(solution)/shard_map/ppermute | solution.py:565
  16.0 9.9 %collective-permute-start = (s32[5]{0:T(128)}, s32[5]{0:T(128)}, u32[]{:S(2)}, u32[]{:S(2)}) collective-permute-start(s32[5]{0:T(128)} %get-tuple-element.71), channel_id=1, source_target_pairs={{0,4},{4,8},{8,12},{12,0},{1,5},{5,9},{9,13},{13,1},{2,6},{6,10},{... | collective-permute-start | bytes 68 | tf_op jit(solution)/shard_map/ppermute | solution.py:433
  17.3 22.7 %collective-permute-start.7 = (f32[2,128,512]{2,1,0:T(8,128)}, f32[2,128,512]{2,1,0:T(8,128)}, u32[]{:S(2)}, u32[]{:S(2)}) collective-permute-start(f32[2,128,512]{2,1,0:T(8,128)} %get-tuple-element.43), channel_id=1, source_target_pairs={{0,2},{2,0},{1,3},{3,1},{4,6},{6,4},{5,7},{7,5},{8,10},{10,8},{9,1... | collective-permute-start | bytes 1572872 | tf_op jit(solution)/shard_map/ppermute | solution.py:550
  23.0 18.4 %collective-permute-start.5 = (f32[1024,128]{1,0:T(8,128)}, f32[1024,128]{1,0:T(8,128)}, u32[]{:S(2)}, u32[]{:S(2)}) collective-permute-start(f32[1024,128]{1,0:T(8,128)} %collective-permute-done.4.refs_3_), channel_id=1, source_target_pairs={{0,1},{1,0},{2,3},{3,2},{4,5},{5,4},{6,7},{7,6},{8,9},{9,8},{10,11... | collective-permute-start | bytes 1572872 | tf_op jit(solution)/shard_map/ppermute | solution.py:87
  26.0 3.6 %collective-permute-start.1 = (s32[5]{0:T(128)}, s32[5]{0:T(128)}, u32[]{:S(2)}, u32[]{:S(2)}) collective-permute-start(s32[5]{0:T(128)} %get-tuple-element.73), channel_id=1, source_target_pairs={{0,8},{4,12},{8,0},{12,4},{1,9},{5,13},{9,1},{13,5},{2,10},{6,14},... | collective-permute-start | bytes 68 | tf_op jit(solution)/shard_map/ppermute | solution.py:433
  29.6 2.9 %collective-permute-start.2 = (s32[5]{0:T(128)}, s32[5]{0:T(128)}, u32[]{:S(2)}, u32[]{:S(2)}) collective-permute-start(s32[5]{0:T(128)} %get-tuple-element.72), channel_id=1, source_target_pairs={{0,12},{4,0},{8,4},{12,8},{1,13},{5,1},{9,5},{13,9},{2,14},{6,2},{... | collective-permute-start | bytes 68 | tf_op jit(solution)/shard_map/ppermute | solution.py:433
  32.4 32.0 %collective-permute-start.11 = (f32[2,128,512]{2,1,0:T(8,128)}, f32[2,128,512]{2,1,0:T(8,128)}, u32[]{:S(2)}, u32[]{:S(2)}) collective-permute-start(f32[2,128,512]{2,1,0:T(8,128)} %copy-done.17), channel_id=1, source_target_pairs={{0,2},{2,0},{1,3},{3,1},{4,6},{6,4},{5,7},{7,5},{8,10},{10,8},{9,1... | collective-permute-start | bytes 1572872 | tf_op jit(solution)/shard_map/ppermute | solution.py:550
  40.0 21.8 %collective-permute-start.8 = (f32[2,128,512]{2,1,0:T(8,128)}, f32[2,128,512]{2,1,0:T(8,128)S(1)}, u32[]{:S(2)}, u32[]{:S(2)}) collective-permute-start(f32[2,128,512]{2,1,0:T(8,128)} %collective-permute-done.7.refs_5_), channel_id=1, source_target_pairs={{0,16},{16,0},{1,17},{17,1},{2,18},{18,2},{3,19},{19,3},{4,20},{20... | collective-permute-start | bytes 1572872 | tf_op jit(solution)/shard_map/ppermute | solution.py:551
  49.3 12.5 %copy-start.8 = (s32[6]{0:T(128)S(1)}, s32[6]{0:T(128)}, u32[]{:S(2)}) copy-start(s32[6]{0:T(128)} %copy-done.6) | copy-start | bytes 76
  64.1 15.1 %copy-start.20 = (f32[2,512]{1,0:T(2,128)S(1)}, f32[2,512]{1,0:T(2,128)}, u32[]{:S(2)}) copy-start(f32[2,512]{1,0:T(2,128)} %param.19) | copy-start | bytes 12292
  64.1 16.7 %copy-start.16 = (f32[2,512,512]{2,1,0:T(8,128)S(1)}, f32[2,512,512]{2,1,0:T(8,128)}, u32[]{:S(2)}) copy-start(f32[2,512,512]{2,1,0:T(8,128)} %copy-done.15) | copy-start | bytes 6291460
  64.1 11.3 %collective-permute-start.9 = (f32[256,512]{1,0:T(8,128)S(1)}, f32[256,512]{1,0:T(8,128)S(1)}, u32[]{:S(2)}, u32[]{:S(2)}) collective-permute-start(f32[256,512]{1,0:T(8,128)S(1)} %get-tuple-element.45), channel_id=1, source_target_pairs={{0,2},{2,0},{1,3},{3,1},{4,6},{6,4},{5,7},{7,5},{8,10},{10,8},{9,1... | collective-permute-start | bytes 1572872 | tf_op jit(solution)/shard_map/ppermute | solution.py:574
  64.4 15.1 %collective-permute-start.12 = (f32[2,128,512]{2,1,0:T(8,128)}, f32[2,128,512]{2,1,0:T(8,128)S(1)}, u32[]{:S(2)}, u32[]{:S(2)}) collective-permute-start(f32[2,128,512]{2,1,0:T(8,128)} %collective-permute-done.11.refs_6_), channel_id=1, source_target_pairs={{0,16},{16,0},{1,17},{17,1},{2,18},{18,2},{3,19},{19,3},{4,20},{20... | collective-permute-start | bytes 1572872 | tf_op jit(solution)/shard_map/ppermute | solution.py:551
  76.1 4.7 %collective-permute-start.10 = (f32[256,512]{1,0:T(8,128)S(1)}, f32[256,512]{1,0:T(8,128)S(1)}, u32[]{:S(2)}, u32[]{:S(2)}) collective-permute-start(f32[256,512]{1,0:T(8,128)S(1)} %get-tuple-element.47.refs_1_), channel_id=1, source_target_pairs={{0,1},{1,0},{2,3},{3,2},{4,5},{5,4},{6,7},{7,6},{8,9},{9,8},{10,11... | collective-permute-start | bytes 1572872 | tf_op jit(solution)/shard_map/ppermute | solution.py:580
  79.2 13.6 %collective-permute-start.15 = (f32[4,64,512]{2,1,0:T(8,128)S(1)}, f32[4,64,512]{2,1,0:T(8,128)S(1)}, u32[]{:S(2)}, u32[]{:S(2)}) collective-permute-start(f32[4,64,512]{2,1,0:T(8,128)S(1)} %get-tuple-element.54), channel_id=1, source_target_pairs={{0,2},{2,0},{1,3},{3,1},{4,6},{6,4},{5,7},{7,5},{8,10},{10,8},{9,1... | collective-permute-start | bytes 1572872 | tf_op jit(solution)/shard_map/ppermute | solution.py:550
  80.8 19.2 %copy-start.14 = (s32[20]{0:T(128)S(1)}, s32[20]{0:T(128)}, u32[]{:S(2)}) copy-start(s32[20]{0:T(128)} %fusion.3.refs_8_.refs_1_) | copy-start | bytes 244
  85.8 7.0 %collective-permute-start.13 = (f32[512,128]{1,0:T(8,128)S(1)}, f32[512,128]{1,0:T(8,128)S(1)}, u32[]{:S(2)}, u32[]{:S(2)}) collective-permute-start(f32[512,128]{1,0:T(8,128)S(1)} %get-tuple-element.52), channel_id=1, source_target_pairs={{0,1},{1,0},{2,3},{3,2},{4,5},{5,4},{6,7},{7,6},{8,9},{9,8},{10,11... | collective-permute-start | bytes 786440 | tf_op jit(solution)/shard_map/ppermute | solution.py:584
  86.3 6.6 %collective-permute-start.14 = (f32[512,128]{1,0:T(8,128)S(1)}, f32[512,128]{1,0:T(8,128)S(1)}, u32[]{:S(2)}, u32[]{:S(2)}) collective-permute-start(f32[512,128]{1,0:T(8,128)S(1)} %get-tuple-element.53), channel_id=1, source_target_pairs={{0,1},{1,0},{2,3},{3,2},{4,5},{5,4},{6,7},{7,6},{8,9},{9,8},{10,11... | collective-permute-start | bytes 786440 | tf_op jit(solution)/shard_map/ppermute | solution.py:584
  92.9 7.1 %collective-permute-start.16 = (f32[512,128]{1,0:T(8,128)S(1)}, f32[512,128]{1,0:T(8,128)S(1)}, u32[]{:S(2)}, u32[]{:S(2)}) collective-permute-start(f32[512,128]{1,0:T(8,128)S(1)} %get-tuple-element.56), channel_id=1, source_target_pairs={{0,2},{2,0},{1,3},{3,1},{4,6},{6,4},{5,7},{7,5},{8,10},{10,8},{9,1... | collective-permute-start | bytes 786440 | tf_op jit(solution)/shard_map/ppermute | solution.py:587
  100.6 15.3 %collective-permute-start.20 = (f32[2,128,512]{2,1,0:T(8,128)S(1)}, f32[2,128,512]{2,1,0:T(8,128)S(1)}, u32[]{:S(2)}, u32[]{:S(2)}) collective-permute-start(f32[2,128,512]{2,1,0:T(8,128)S(1)} %get-tuple-element.62), channel_id=1, source_target_pairs={{0,2},{2,0},{1,3},{3,1},{4,6},{6,4},{5,7},{7,5},{8,10},{10,8},{9,1... | collective-permute-start | bytes 1572872 | tf_op jit(solution)/shard_map/ppermute | solution.py:550
  100.9 6.1 %collective-permute-start.17 = (f32[5,64,128]{2,1,0:T(8,128)S(1)}, f32[5,64,128]{2,1,0:T(8,128)S(1)}, u32[]{:S(2)}, u32[]{:S(2)}) collective-permute-start(f32[5,64,128]{2,1,0:T(8,128)S(1)} %get-tuple-element.59), channel_id=1, source_target_pairs={{0,4},{4,8},{8,12},{12,0},{1,5},{5,9},{9,13},{13,1},{2,6},{6,10},{... | collective-permute-start | bytes 491528 | tf_op jit(solution)/shard_map/ppermute | solution.py:599
  101.6 14.3 %collective-permute-start.18 = (f32[5,64,128]{2,1,0:T(8,128)S(1)}, f32[5,64,128]{2,1,0:T(8,128)S(1)}, u32[]{:S(2)}, u32[]{:S(2)}) collective-permute-start(f32[5,64,128]{2,1,0:T(8,128)S(1)} %get-tuple-element.60), channel_id=1, source_target_pairs={{0,8},{4,12},{8,0},{12,4},{1,9},{5,13},{9,1},{13,5},{2,10},{6,14},... | collective-permute-start | bytes 491528 | tf_op jit(solution)/shard_map/ppermute | solution.py:599
  104.3 11.6 %collective-permute-start.19 = (f32[5,64,128]{2,1,0:T(8,128)S(1)}, f32[5,64,128]{2,1,0:T(8,128)S(1)}, u32[]{:S(2)}, u32[]{:S(2)}) collective-permute-start(f32[5,64,128]{2,1,0:T(8,128)S(1)} %get-tuple-element.61), channel_id=1, source_target_pairs={{0,12},{4,0},{8,4},{12,8},{1,13},{5,1},{9,5},{13,9},{2,14},{6,2},{... | collective-permute-start | bytes 491528 | tf_op jit(solution)/shard_map/ppermute | solution.py:599
  115.9 26.1 %copy-start.11 = (f32[1,512]{1,0:T(1,128)S(1)}, f32[1,512]{1,0:T(1,128)}, u32[]{:S(2)}) copy-start(f32[1,512]{1,0:T(1,128)} %get-tuple-element.78.refs_5_) | copy-start | bytes 6148
  116.5 2.2 %collective-permute-start.21 = (f32[1024,128]{1,0:T(8,128)S(1)}, f32[1024,128]{1,0:T(8,128)S(1)}, u32[]{:S(2)}, u32[]{:S(2)}) collective-permute-start(f32[1024,128]{1,0:T(8,128)S(1)} %bitcast.13), channel_id=1, source_target_pairs={{0,1},{1,0},{2,3},{3,2},{4,5},{5,4},{6,7},{7,6},{8,9},{9,8},{10,11... | collective-permute-start | bytes 1572872 | tf_op jit(solution)/shard_map/ppermute | solution.py:87
  117.2 13.5 %collective-permute-start.22 = (f32[1024,128]{1,0:T(8,128)S(1)}, f32[1024,128]{1,0:T(8,128)S(1)}, u32[]{:S(2)}, u32[]{:S(2)}) collective-permute-start(f32[1024,128]{1,0:T(8,128)S(1)} %bitcast.14), channel_id=1, source_target_pairs={{0,2},{2,0},{1,3},{3,1},{4,6},{6,4},{5,7},{7,5},{8,10},{10,8},{9,1... | collective-permute-start | bytes 1572872 | tf_op jit(solution)/shard_map/ppermute | solution.py:86
  119.3 22.6 %collective-permute-start.25 = (f32[2,128,512]{2,1,0:T(8,128)S(1)}, f32[2,128,512]{2,1,0:T(8,128)S(1)}, u32[]{:S(2)}, u32[]{:S(2)}) collective-permute-start(f32[2,128,512]{2,1,0:T(8,128)S(1)} %slice_unit.1), channel_id=1, source_target_pairs={{0,2},{2,0},{1,3},{3,1},{4,6},{6,4},{5,7},{7,5},{8,10},{10,8},{9,1... | collective-permute-start | bytes 1572872 | tf_op jit(solution)/shard_map/ppermute | solution.py:550
  120.6 21.4 %collective-permute-start.24 = (f32[4,64,512]{2,1,0:T(8,128)S(1)}, f32[4,64,512]{2,1,0:T(8,128)S(1)}, u32[]{:S(2)}, u32[]{:S(2)}) collective-permute-start(f32[4,64,512]{2,1,0:T(8,128)S(1)} %collective-permute-done.15.refs_4_.refs_7_), channel_id=1, source_target_pairs={{0,16},{16,0},{1,17},{17,1},{2,18},{18,2},{3,19},{19,3},{4,20},{20... | collective-permute-start | bytes 1572872 | tf_op jit(solution)/shard_map/ppermute | solution.py:551
  130.7 11.3 %collective-permute-start.23 = (f32[1024,128]{1,0:T(8,128)S(1)}, f32[1024,128]{1,0:T(8,128)S(1)}, u32[]{:S(2)}, u32[]{:S(2)}) collective-permute-start(f32[1024,128]{1,0:T(8,128)S(1)} %collective-permute-done.22.refs_3_), channel_id=1, source_target_pairs={{0,1},{1,0},{2,3},{3,2},{4,5},{5,4},{6,7},{7,6},{8,9},{9,8},{10,11... | collective-permute-start | bytes 1572872 | tf_op jit(solution)/shard_map/ppermute | solution.py:87
  141.9 16.0 %collective-permute-start.26 = (f32[2,128,512]{2,1,0:T(8,128)S(1)}, f32[2,128,512]{2,1,0:T(8,128)S(1)}, u32[]{:S(2)}, u32[]{:S(2)}) collective-permute-start(f32[2,128,512]{2,1,0:T(8,128)S(1)} %collective-permute-done.25.refs_9_), channel_id=1, source_target_pairs={{0,16},{16,0},{1,17},{17,1},{2,18},{18,2},{3,19},{19,3},{4,20},{20... | collective-permute-start | bytes 1572872 | tf_op jit(solution)/shard_map/ppermute | solution.py:551
  157.9 15.9 %copy-start.18 = (s32[1024]{0:T(1024)S(1)}, s32[1024]{0:T(1024)}, u32[]{:S(2)}) copy-start(s32[1024]{0:T(1024)} %param.22) | copy-start | bytes 12292
  159.1 14.7 %collective-permute-start.27 = (f32[512,512]{1,0:T(8,128)S(1)}, f32[512,512]{1,0:T(8,128)S(1)}, u32[]{:S(2)}, u32[]{:S(2)}) collective-permute-start(f32[512,512]{1,0:T(8,128)S(1)} %output_rows.3.refs_1_), channel_id=1, source_target_pairs={{0,1},{1,0},{2,3},{3,2},{4,5},{5,4},{6,7},{7,6},{8,9},{9,8},{10,11... | collective-permute-start | bytes 3145736 | tf_op jit(solution)/shard_map/ppermute | solution.py:615
  160.3 13.5 %collective-permute-start.28 = (f32[2,128,512]{2,1,0:T(8,128)S(1)}, f32[2,128,512]{2,1,0:T(8,128)S(1)}, u32[]{:S(2)}, u32[]{:S(2)}) collective-permute-start(f32[2,128,512]{2,1,0:T(8,128)S(1)} %collective-permute-done.20.refs_6_.refs_7_), channel_id=1, source_target_pairs={{0,16},{16,0},{1,17},{17,1},{2,18},{18,2},{3,19},{19,3},{4,20},{20... | collective-permute-start | bytes 1572872 | tf_op jit(solution)/shard_map/ppermute | solution.py:551
  179.5 20.2 %copy-start.19 = (f32[2,3,3,512]{3,0,2,1:T(2,128)S(1)}, f32[2,3,3,512]{3,0,2,1:T(2,128)}, u32[]{:S(2)}) copy-start(f32[2,3,3,512]{3,0,2,1:T(2,128)} %param.23) | copy-start | bytes 110596
  179.5 22.1 %copy-start.9 = (s32[6]{0:T(128)S(1)}, s32[6]{0:T(128)}, u32[]{:S(2)}) copy-start(s32[6]{0:T(128)} %copy-done.6) | copy-start | bytes 76
  179.5 22.1 %copy-start.12 = (f32[2,512]{1,0:T(2,128)S(1)}, f32[2,512]{1,0:T(2,128)}, u32[]{:S(2)}) copy-start(f32[2,512]{1,0:T(2,128)} %refs_4_.3) | copy-start | bytes 12292
  179.5 2.3 %collective-permute-start.30 = (f32[200,512]{1,0:T(8,128)S(1)}, f32[200,512]{1,0:T(8,128)S(1)}, u32[]{:S(2)}, u32[]{:S(2)}) collective-permute-start(f32[200,512]{1,0:T(8,128)S(1)} %get-tuple-element.70), channel_id=1, source_target_pairs={{0,1},{1,0},{2,3},{3,2},{4,5},{5,4},{6,7},{7,6},{8,9},{9,8},{10,11... | collective-permute-start | bytes 1228808 | tf_op jit(solution)/shard_map/ppermute | solution.py:621
  180.4 2.9 %collective-permute-start.29 = (f32[200,512]{1,0:T(8,128)S(1)}, f32[200,512]{1,0:T(8,128)S(1)}, u32[]{:S(2)}, u32[]{:S(2)}) collective-permute-start(f32[200,512]{1,0:T(8,128)S(1)} %get-tuple-element.68), channel_id=1, source_target_pairs={{0,1},{1,0},{2,3},{3,2},{4,5},{5,4},{6,7},{7,6},{8,9},{9,8},{10,11... | collective-permute-start | bytes 1228808 | tf_op jit(solution)/shard_map/ppermute | solution.py:621
  181.9 10.7 %collective-permute-start.31 = (f32[200,512]{1,0:T(8,128)S(1)}, f32[200,512]{1,0:T(8,128)S(1)}, u32[]{:S(2)}, u32[]{:S(2)}) collective-permute-start(f32[200,512]{1,0:T(8,128)S(1)} %add.284), channel_id=1, source_target_pairs={{0,2},{2,0},{1,3},{3,1},{4,6},{6,4},{5,7},{7,5},{8,10},{10,8},{9,1... | collective-permute-start | bytes 1228808 | tf_op jit(solution)/shard_map/ppermute | solution.py:624
  192.8 8.8 %collective-permute-start.32 = (f32[40,512]{1,0:T(8,128)S(1)}, f32[40,512]{1,0:T(8,128)S(1)}, u32[]{:S(2)}, u32[]{:S(2)}) collective-permute-start(f32[40,512]{1,0:T(8,128)S(1)} %slice_select_fusion), channel_id=1, source_target_pairs={{1,4},{5,8},{9,12},{4,1},{8,5},{12,9},{3,6},{7,10},{11,14},{6,3},{... | collective-permute-start | bytes 245768 | tf_op jit(solution)/shard_map/ppermute | solution.py:628
  201.6 2.2 %copy-start = (f32[2,512,1024]{2,1,0:T(8,128)S(1)}, f32[2,512,1024]{2,1,0:T(8,128)}, u32[]{:S(2)}) copy-start(f32[2,512,1024]{2,1,0:T(8,128)} %refs_5_.1) | copy-start | bytes 12582916
  (8 other events, 7.7 us)
